TPU v7x, 512 devices: a whole 4x8x8 slice. The times are simulated.
512 devices in a mesh: layer: 8 (over z), row: 8 (over x, core), col: 8 (over y).
Axes of the slice: x: 4, y: 8, z: 8, core: 2. Of those that a mesh axis runs over, the one named last changes fastest.
Arguments:
- rhs_low: bfloat16 [8, 2, 8, 384, 512], P('layer', None, 'col'), may hold values from -6 to 6
- inv_low: bfloat16 [8, 2, 8, 384, 384], P('layer', None, 'col'), as said below
- blocks: bfloat16 [8, 8, 8, 2, 4, 384, 384], P('layer', 'row', 'col'), may hold values from -0.02734375 to 0.02734375
- targets: int32 [8, 8, 8, 2, 4], P('layer', 'row', 'col'), may hold values from 1 to 5, as said below
- rhs_anc: bfloat16 [32, 384, 512], P('row', None, ('layer', 'col')), may hold values from -6 to 6
- inv_anc: bfloat16 [32, 384, 384], P('row'), as said below
Outputs:
- solution_low: bfloat16 [8, 2, 8, 384, 512], P('layer', None, 'col', None, 'row')
- solution_anc: float32 [32, 384, 512], P('row', None, ('layer', 'col'))
Inputs may be any that keep to these rules, and one draw needn't show every extreme that they name: For each g, r, c, l the 4 values targets[g, r, c, l, :] are distinct. A value t < 2 is greater than l; a value t >= 2 names ancestor r * 4 + t - 2. `inv_low`: each block is lower triangular. `inv_anc`: each block is lower triangular.
All inputs are finite; a program needn't handle non-finite values.
Results may differ from a plain program's by a relative error of at most 0.011.
Values may be sent and summed in bfloat16 or wider, within the bound.
No kernel may reach another device: no remote copies, remote signals or barrier semaphores. Data moves between devices by JAX's collectives and lax.ppermute only.
A program may use at most 64 MiB of HBM per device.

v0:
```python
import jax
import jax.numpy as jnp
from jax import lax
from jax.sharding import PartitionSpec as P


def in_blocks(shard, dim, size):
    dims = shard.shape
    tiles = shard.reshape(*dims[:dim], size, dims[dim] // size, *dims[dim + 1 :])
    return jnp.moveaxis(tiles, dim, 0)


def summed_on_arrival(shard, axis, dim):
    tiles = in_blocks(shard, dim, lax.axis_size(axis))
    arrived = lax.all_to_all(tiles, axis, split_axis=0, concat_axis=0, tiled=True)
    return arrived.astype(jnp.float32).sum(axis=0)


def joined_along(tiles, dim):
    tiles = jnp.moveaxis(tiles, 0, dim)
    dims = tiles.shape
    return tiles.reshape(*dims[:dim], dims[dim] * dims[dim + 1], *dims[dim + 2 :])


def from_everyone(shard, axis):
    copies = jnp.broadcast_to(shard, (lax.axis_size(axis), *shard.shape))
    return lax.all_to_all(copies, axis, split_axis=0, concat_axis=0, tiled=True)


def gathered_copies(shard, axis, dim):
    return joined_along(from_everyone(shard, axis), dim)


def broadcast(shard, axis, root):
    return lax.dynamic_index_in_dim(lax.all_gather(shard, axis), root, 0, keepdims=False)


def solve_block(inverse, right_side, partial_value):
    residual = (right_side.astype(jnp.float32) - partial_value).astype(jnp.bfloat16)
    return jnp.dot(inverse, residual, preferred_element_type=jnp.float32).astype(jnp.bfloat16)


def on_device(rhs_low, inv_low, blocks, targets, rhs_anc, inv_anc):
    row_index = lax.axis_index("row")
    column_index = lax.axis_index("col")
    grid_rows = lax.axis_size("row")
    levels = rhs_low.shape[1]
    block_width = inv_low.shape[-1]
    load_cases = rhs_low.shape[-1]
    per_row = blocks.shape[4]
    share = load_cases // grid_rows
    collected = jnp.zeros((levels + inv_anc.shape[0], block_width, load_cases), jnp.float32)
    pieces = []
    for current in range(levels):
        owner = (current + column_index) % grid_rows
        right_side = rhs_low[0, current, 0]
        inverse = inv_low[0, current, 0]
        if current == 0:
            nothing = jnp.zeros((block_width, load_cases), jnp.float32)
            answer = solve_block(inverse, right_side, nothing)
        else:
            shares = summed_on_arrival(collected[current].astype(jnp.bfloat16), "col", 1)
            summed = gathered_copies(shares.astype(jnp.bfloat16), "col", 1).astype(shares.dtype)
            answer = broadcast(solve_block(inverse, right_side, summed), "row", owner)
        pieces.append(lax.dynamic_slice_in_dim(answer, row_index * share, share, 1))
        stacked = blocks[0, 0, 0, current].reshape(per_row * block_width, block_width)
        product = jnp.dot(stacked, answer, preferred_element_type=jnp.float32).reshape(
            per_row, block_width, load_cases
        )
        for member in range(per_row):
            target = targets[0, 0, 0, current, member]
            before = lax.dynamic_index_in_dim(collected, target, 0, keepdims=False)
            collected = lax.dynamic_update_index_in_dim(
                collected, before + product[member], target, 0
            )
    solution_low = jnp.stack(pieces, 0)[None, :, None]
    ancestor_part = collected[levels:]
    merged = summed_on_arrival(ancestor_part.astype(jnp.bfloat16), "layer", 2)
    merged = summed_on_arrival(merged.astype(jnp.bfloat16), "col", 2)
    residual = (rhs_anc.astype(jnp.float32) - merged).astype(jnp.bfloat16)
    solution_anc = jnp.einsum("awv,avk->awk", inv_anc, residual, preferred_element_type=jnp.float32)
    return (solution_low, solution_anc)


def solution(mesh):
    in_specs = (
        P("layer", None, "col", None, None),
        P("layer", None, "col", None, None),
        P("layer", "row", "col", None, None, None, None),
        P("layer", "row", "col", None, None),
        P("row", None, ("layer", "col")),
        P("row", None, None),
    )
    out_specs = (P("layer", None, "col", None, "row"), P("row", None, ("layer", "col")))
    return jax.shard_map(
        on_device, mesh=mesh, in_specs=in_specs, out_specs=out_specs, check_vma=False
    )
```

profile of v0, /device:TPU:2, one launch (start us, length us, event | category | flops | bytes accessed | tf_op | source)
XLA Modules:
  0.0 201.2 jit_solution(9465125905723739728)
XLA Ops:
  7.2 0.0 copy-start
  7.2 1.7 fusion.26
  13.7 1.9 fusion.25
  16.3 1.5 convolution_convert_fusion.1
  17.7 0.0 copy-start.3
  17.7 0.8 copy-done.3
  18.5 2.7 %convolution_bitcast_fusion.1 = f32[1536,512]{0,1:T(8,128)} fusion(bf16[384,512]{1,0:T(8,128)(2,1)S(1)} %convolution_convert_fusion.1, bf16[1536,384]{1,0:T(8,128)(2,1)S(1)} %bitcast.110), kind=kOutput, calls=%fused_computation.1 | convolution fusion | flops 603979776 | bytes 4718592 | tf_op jit(solution)/shard_map/dot_general | solution.py:67
  21.7 0.0 copy-start.1
  21.7 2.6 %broadcast_in_dim.20 = f32[6,384,512]{1,2,0:T(8,128)} broadcast(f32[]{:T(128)} %constant.84.clone.1), dimensions={} | broadcast | bytes 4718596 | tf_op jit(solution)/shard_map/broadcast_in_dim | solution.py:52
  24.4 0.8 copy-done.1
  25.1 1.0 fusion.15
  26.1 2.2 %fusion.14 = f32[6,384,512]{1,2,0:T(8,128)} fusion(f32[6,384,512]{1,2,0:T(8,128)} %fusion.15, s32[]{:T(128)S(6)} %select_n.55, f32[1536,512]{0,1:T(8,128)S(1)} %copy-done.1), kind=kLoop, calls=%fused_computation.29 | loop fusion | flops 196608 | bytes 2359300 | tf_op jit(solution)/shard_map/jit(dynamic_update_index_in_dim)/dynamic_update_slice | solution.py:73
  28.9 2.3 %fusion.12 = f32[6,384,512]{1,2,0:T(8,128)} fusion(f32[6,384,512]{1,2,0:T(8,128)} %fusion.14, s32[]{:T(128)S(6)} %select_n.56, f32[1536,512]{0,1:T(8,128)} %convolution_bitcast_fusion.1), kind=kLoop, calls=%fused_computation.26 | loop fusion | flops 196608 | bytes 2359300 | tf_op jit(solution)/shard_map/jit(dynamic_update_index_in_dim)/dynamic_update_slice | solution.py:73
  31.8 0.0 slice-start
  31.8 2.4 %fusion.10 = f32[6,384,512]{1,2,0:T(8,128)} fusion(f32[6,384,512]{1,2,0:T(8,128)} %fusion.12, s32[]{:T(128)S(6)} %select_n.57, f32[1536,512]{0,1:T(8,128)} %convolution_bitcast_fusion.1), kind=kLoop, calls=%fused_computation.23 | loop fusion | flops 196608 | bytes 2359300 | tf_op jit(solution)/shard_map/jit(dynamic_update_index_in_dim)/dynamic_update_slice | solution.py:73
  34.2 1.2 slice.169
  35.4 21.6 %all_to_all.20 = bf16[8,384,64]{1,2,0:T(8,128)(2,1)S(1)} all-to-all(bf16[8,384,64]{1,2,0:T(8,128)(2,1)S(1)} %bitcast.113), channel_id=1, replica_groups=mesh['layer'=8,'row'=8,'col'=8] {'col'}, dimensions={0} | all-to-all | bytes 786432 | tf_op jit(solution)/shard_map/all_to_all | solution.py:15
  57.0 0.1 reduce_sum.33
  57.0 0.8 broadcast_in_dim.22
  57.8 3.5 %all-to-all-start.1 = ((bf16[8,384,64]{1,2,0:T(8,128)(2,1)}), bf16[8,384,64]{1,2,0:T(8,128)(2,1)S(1)}, u32[]{:S(2)}, u32[]{:S(2)}) async-start(bf16[8,384,64]{1,2,0:T(8,128)(2,1)} %broadcast_in_dim.22), calls=%async_computation.1 | async-start | bytes 786432 | tf_op jit(solution)/shard_map/all_to_all | solution.py:27
  61.3 0.0 all-gather.3.cloned.1.call-start
  61.3 0.0 slice-done
  61.3 0.2 copy.21
  61.6 13.2 %all-to-all-done.1 = bf16[8,384,64]{1,2,0:T(8,128)(2,1)S(1)} async-done(((bf16[8,384,64]{1,2,0:T(8,128)(2,1)}), bf16[8,384,64]{1,2,0:T(8,128)(2,1)S(1)}, u32[]{:S(2)}, u32[]{:S(2)}) %all-to-all-start.1) | async-done | bytes 393248 | tf_op jit(solution)/shard_map/all_to_all | solution.py:27
  74.7 0.1 convert_element_type.70
  74.8 2.2 %fusion = bf16[384,512]{0,1:T(8,128)(2,1)} fusion(f32[1,1,1,384,512]{3,4,2,1,0:T(8,128)S(1)} %bitcast.111, bf16[1,1,1,384,512]{3,4,2,1,0:T(8,128)(2,1)S(1)} %copy.21, bf16[1,2,1,384,384]{4,3,2,1,0:T(8,128)(2,1)} %param.7), kind=kOutput, calls=%fused_computation.6 | convolution fusion | flops 151781376 | bytes 1867776 | tf_op jit(solution)/shard_map/dot_general | solution.py:40
  77.0 0.0 all-gather.3.cloned.1.call-update
  84.8 23.9 %all-gather.3.cloned.1.call-done = bf16[3072,512]{0,1:T(8,128)(2,1)} async-done(((bf16[384,512]{0,1:T(8,128)(2,1)}), bf16[3072,512]{0,1:T(8,128)(2,1)}) %all-gather.3.cloned.1.call-update) | async-done | bytes 3145744 | tf_op jit(solution)/shard_map/all_gather | solution.py:35
  108.7 2.6 %copy.24 = bf16[64,8,8,384]{3,2,1,0:T(8,128)(2,1)S(1)} copy(bf16[64,8,8,384]{3,1,2,0:T(8,128)(2,1)} %bitcast.112) | data formatting | bytes 6291456
  111.3 0.0 copy-start.2
  111.3 1.6 copy-done.2
  113.0 0.8 constant_dynamic-slice_fusion
  113.8 1.0 copy.23
  114.8 1.0 convolution_bitcast_fusion
  115.8 2.2 %fusion.8 = f32[6,384,512]{1,2,0:T(8,128)} fusion(f32[6,384,512]{1,2,0:T(8,128)} %fusion.10, s32[]{:T(128)S(6)} %select_n.62, f32[1536,512]{0,1:T(8,128)S(1)} %convolution_bitcast_fusion), kind=kLoop, calls=%fused_computation.19 | loop fusion | flops 196608 | bytes 2359300 | tf_op jit(solution)/shard_map/jit(dynamic_update_index_in_dim)/dynamic_update_slice | solution.py:73
  118.0 2.1 %fusion.6 = f32[6,384,512]{1,2,0:T(8,128)} fusion(f32[6,384,512]{1,2,0:T(8,128)} %fusion.8, s32[]{:T(128)S(6)} %select_n.63, f32[1536,512]{0,1:T(8,128)S(1)} %convolution_bitcast_fusion), kind=kLoop, calls=%fused_computation.16 | loop fusion | flops 196608 | bytes 2359300 | tf_op jit(solution)/shard_map/jit(dynamic_update_index_in_dim)/dynamic_update_slice | solution.py:73
  120.1 2.2 %fusion.4 = f32[6,384,512]{1,2,0:T(8,128)} fusion(f32[6,384,512]{1,2,0:T(8,128)} %fusion.6, s32[]{:T(128)S(6)} %select_n.64, f32[1536,512]{0,1:T(8,128)S(1)} %convolution_bitcast_fusion), kind=kLoop, calls=%fused_computation.13 | loop fusion | flops 196608 | bytes 2359300 | tf_op jit(solution)/shard_map/jit(dynamic_update_index_in_dim)/dynamic_update_slice | solution.py:73
  122.3 2.1 %fusion.2 = f32[6,384,512]{1,2,0:T(8,128)} fusion(f32[6,384,512]{1,2,0:T(8,128)} %fusion.4, s32[]{:T(128)S(6)} %select_n.65, f32[1536,512]{0,1:T(8,128)S(1)} %convolution_bitcast_fusion), kind=kLoop, calls=%fused_computation.10 | loop fusion | flops 196608 | bytes 2359300 | tf_op jit(solution)/shard_map/jit(dynamic_update_index_in_dim)/dynamic_update_slice | solution.py:73
  124.4 2.1 %slice.168 = bf16[4,384,512]{1,2,0:T(8,128)(2,1)S(1)} slice(f32[6,384,512]{1,2,0:T(8,128)} %fusion.2), slice={[2:6], [0:384], [0:512]} | slice | bytes 3145728 | tf_op jit(solution)/shard_map/slice | solution.py:77
  126.5 1.3 copy.26
  127.8 0.0 copy-start.4
  127.8 7.5 %all-to-all-start.2 = ((bf16[8,4,384,64]{2,3,1,0:T(8,128)(2,1)}), bf16[8,4,384,64]{2,3,1,0:T(8,128)(2,1)S(1)}, u32[]{:S(2)}, u32[]{:S(2)}) async-start(bf16[8,4,384,64]{2,3,1,0:T(8,128)(2,1)} %bitcast.105), calls=%async_computation.2 | async-start | bytes 3145728 | tf_op jit(solution)/shard_map/all_to_all | solution.py:15
  135.3 40.4 %all-to-all-done.2 = bf16[8,4,384,64]{2,3,1,0:T(8,128)(2,1)S(1)} async-done(((bf16[8,4,384,64]{2,3,1,0:T(8,128)(2,1)}), bf16[8,4,384,64]{2,3,1,0:T(8,128)(2,1)S(1)}, u32[]{:S(2)}, u32[]{:S(2)}) %all-to-all-start.2) | async-done | bytes 1572896 | tf_op jit(solution)/shard_map/all_to_all | solution.py:15
  175.7 0.3 reduce_sum.34
  176.0 0.7 copy.19
  176.7 6.7 %all-to-all-start.3 = ((bf16[8,4,384,8]{2,3,1,0:T(8,128)(2,1)}), bf16[8,4,384,8]{2,3,1,0:T(8,128)(2,1)S(1)}, u32[]{:S(2)}, u32[]{:S(2)}) async-start(bf16[8,4,384,8]{2,3,1,0:T(8,128)(2,1)} %copy.19), calls=%async_computation.3 | async-start | bytes 393216 | tf_op jit(solution)/shard_map/all_to_all | solution.py:15
  183.4 1.0 constant_dynamic-slice_fusion.2
  184.4 0.1 copy.14
  184.5 1.1 constant_dynamic-slice_fusion.1
  185.6 0.7 maximum_bitcast_fusion
  186.3 6.9 %all-to-all-done.3 = bf16[8,4,384,8]{2,3,1,0:T(8,128)(2,1)S(1)} async-done(((bf16[8,4,384,8]{2,3,1,0:T(8,128)(2,1)}), bf16[8,4,384,8]{2,3,1,0:T(8,128)(2,1)S(1)}, u32[]{:S(2)}, u32[]{:S(2)}) %all-to-all-start.3) | async-done | bytes 196640 | tf_op jit(solution)/shard_map/all_to_all | solution.py:15
  193.2 0.0 copy-done
  193.2 0.0 copy-done.4
  193.2 1.1 convolution_bitcast_fusion.2
  (2 shorter events, 0.0 us)
Async XLA Ops:
  7.2 186.1 %copy-start = (bf16[4,384,384]{2,1,0:T(8,128)(2,1)S(1)}, bf16[4,384,384]{2,1,0:T(8,128)(2,1)}, u32[]{:S(2)}) copy-start(bf16[4,384,384]{2,1,0:T(8,128)(2,1)} %param.11) | copy-start | bytes 3538948
  17.7 0.8 copy-start.3
  21.7 3.4 %copy-start.1 = (f32[1536,512]{0,1:T(8,128)S(1)}, f32[1536,512]{0,1:T(8,128)}, u32[]{:S(2)}) copy-start(f32[1536,512]{0,1:T(8,128)} %convolution_bitcast_fusion.1) | copy-start | bytes 9437188
  31.8 29.5 %slice-start = ((bf16[1,2,1,384,512]{4,3,2,1,0:T(8,128)(2,1)}), bf16[1,1,1,384,512]{4,3,2,1,0:T(8,128)(2,1)S(1)}, s32[]{:S(2)}) async-start(bf16[1,2,1,384,512]{4,3,2,1,0:T(8,128)(2,1)} %param.6), calls=%async_computation.5 | async-start | bytes 786432 | tf_op jit(solution)/shard_map/slice | solution.py:56
  57.8 16.9 %all-to-all-start.1 = ((bf16[8,384,64]{1,2,0:T(8,128)(2,1)}), bf16[8,384,64]{1,2,0:T(8,128)(2,1)S(1)}, u32[]{:S(2)}, u32[]{:S(2)}) async-start(bf16[8,384,64]{1,2,0:T(8,128)(2,1)} %broadcast_in_dim.22), calls=%async_computation.1 | async-start | bytes 786432 | tf_op jit(solution)/shard_map/all_to_all | solution.py:27
  61.3 47.4 %all-gather.3.cloned.1.call-start = ((), (), s32[]{:S(2)}) async-start(), calls=%async_computation.4 | async-start | bytes 3538944 | tf_op jit(solution)/shard_map/all_gather | solution.py:35
  111.3 1.6 copy-start.2
  127.8 65.4 %copy-start.4 = (bf16[4,384,8]{1,2,0:T(8,128)(2,1)S(1)}, bf16[4,384,8]{1,2,0:T(8,128)(2,1)}, u32[]{:S(2)}) copy-start(bf16[4,384,8]{1,2,0:T(8,128)(2,1)} %param.10) | copy-start | bytes 73732
  127.8 47.9 %all-to-all-start.2 = ((bf16[8,4,384,64]{2,3,1,0:T(8,128)(2,1)}), bf16[8,4,384,64]{2,3,1,0:T(8,128)(2,1)S(1)}, u32[]{:S(2)}, u32[]{:S(2)}) async-start(bf16[8,4,384,64]{2,3,1,0:T(8,128)(2,1)} %bitcast.105), calls=%async_computation.2 | async-start | bytes 3145728 | tf_op jit(solution)/shard_map/all_to_all | solution.py:15
  176.7 16.5 %all-to-all-start.3 = ((bf16[8,4,384,8]{2,3,1,0:T(8,128)(2,1)}), bf16[8,4,384,8]{2,3,1,0:T(8,128)(2,1)S(1)}, u32[]{:S(2)}, u32[]{:S(2)}) async-start(bf16[8,4,384,8]{2,3,1,0:T(8,128)(2,1)} %copy.19), calls=%async_computation.3 | async-start | bytes 393216 | tf_op jit(solution)/shard_map/all_to_all | solution.py:15
Sparse Core Ops, SparseCore 0:
  77.1 31.5 all-gather.2
where the time goes:
time: 202 us; the launch traced here: 201 us
  waiting for transfers between devices  84.3 us (42%)
  between operations  29.3 us (15%)
  local copies, waits for them, and re-layouts  23.2 us (11%)
  blocking collectives  21.6 us (11%)
  starting transfers between devices  17.7 us (9%)
  other arithmetic  16.5 us (8%)
  matrix products  8.41 us (4%)
    all_to_all x2, waiting for transfers between devices, summed_on_arrival(): lax.all_to_all(tiles, axis, split_axis=0, concat_axis=0, tiled=True)  47.3 us
    all_gather x1, waiting for transfers between devices, broadcast(): lax.all_gather(shard, axis)  23.9 us
    all_to_all x1, blocking collectives, summed_on_arrival(): lax.all_to_all(tiles, axis, split_axis=0, concat_axis=0, tiled=True)  21.6 us
    dynamic_update_slice x7, other arithmetic, on_device(): lax.dynamic_update_index_in_dim(collected, before + product[member], targ...  15.5 us
    all_to_all x2, starting transfers between devices, summed_on_arrival(): lax.all_to_all(tiles, axis, split_axis=0, concat_axis=0, tiled=True)  14.2 us
    all_to_all x1, waiting for transfers between devices, from_everyone(): return lax.all_to_all(copies, axis, split_axis=0, concat_axis=0, tiled=True)  13.2 us
    unnamed x14, local copies, waits for them, and re-layouts  7.02 us
  transfers between devices with their start and end apart: 4, of which 4 were waited for; matrix products, arithmetic and copies ran while one was open for 2% of the time, Pallas kernels for 0%

commit v1 on v0

v1 whole, which is shorter than its diff:
```python
import jax
import jax.numpy as jnp
from jax import lax
from jax.experimental import pallas as pl
from jax.experimental.pallas import tpu as pltpu
from jax.sharding import PartitionSpec as P

F32 = jnp.float32
BF16 = jnp.bfloat16
NT = (((1,), (1,)), ((), ()))


def dot_nt(left, right):
    return lax.dot_general(left, right, NT, preferred_element_type=F32)


def slot_of(targets_ref, level, target, per_row):
    slot, found = jnp.int32(0), jnp.int32(0)
    for member in range(per_row):
        hit = targets_ref[level, member] == target
        slot = jnp.where(hit, jnp.int32(member), slot)
        found = jnp.where(hit, jnp.int32(1), found)
    return slot, found


def first_level(targets, place, rhs_low, inv_low, blocks, share):
    _, width, loads = rhs_low.shape
    per_row = blocks.shape[1]

    def body(targets_ref, place_ref, rhs_ref, inv_ref, block_ref, answer_ref, part_ref):
        answer = jnp.dot(inv_ref[0], rhs_ref[0], preferred_element_type=F32).T.astype(BF16)
        answer_ref[...] = answer
        _, found = slot_of(targets_ref, 0, 1, per_row)

        @pl.when(found == 1)
        def _():
            part_ref[...] = dot_nt(answer, block_ref[0, 0]).astype(BF16)

        @pl.when(found == 0)
        def _():
            part_ref[...] = jnp.zeros_like(part_ref)

    whole = lambda i, *_: (0, 0)
    return pl.pallas_call(
        body,
        out_shape=(
            jax.ShapeDtypeStruct((loads, width), BF16),
            jax.ShapeDtypeStruct((loads, width), BF16),
        ),
        grid_spec=pltpu.PrefetchScalarGridSpec(
            num_scalar_prefetch=2,
            grid=(1,),
            in_specs=[
                pl.BlockSpec((1, width, loads), lambda i, *_: (0, 0, 0)),
                pl.BlockSpec((1, width, width), lambda i, *_: (0, 0, 0)),
                pl.BlockSpec(
                    (1, 1, width, width), lambda i, t, p: (0, slot_of(t, 0, 1, per_row)[0], 0, 0)
                ),
            ],
            out_specs=(pl.BlockSpec((loads, width), whole), pl.BlockSpec((loads, width), whole)),
        ),
        compiler_params=pltpu.CompilerParams(vmem_limit_bytes=40 << 20),
        cost_estimate=pl.CostEstimate(
            flops=4 * width * width * loads, bytes_accessed=2_200_000, transcendentals=0
        ),
    )(targets, place, rhs_low, inv_low, blocks)


def second_level(place, part, rhs_low, inv_low, answer0):
    share, width = part.shape
    loads = rhs_low.shape[2]
    lanes = max(share, 128)
    per_lanes = lanes // share

    def body(place_ref, part_ref, rhs_ref, inv_ref, answer0_ref, answer_ref, both_ref):
        turned = rhs_ref[0].astype(F32).T
        right_side = turned[:share]
        for other in range(1, per_lanes):
            right_side = jnp.where(
                place_ref[0] % per_lanes == other,
                turned[other * share : (other + 1) * share],
                right_side,
            )
        residual = (right_side - part_ref[...].astype(F32)).astype(BF16)
        answer = dot_nt(residual, inv_ref[0]).astype(BF16)
        answer_ref[...] = answer
        both_ref[0] = answer0_ref[...]
        both_ref[1] = answer

    return pl.pallas_call(
        body,
        out_shape=(
            jax.ShapeDtypeStruct((share, width), BF16),
            jax.ShapeDtypeStruct((2, share, width), BF16),
        ),
        grid_spec=pltpu.PrefetchScalarGridSpec(
            num_scalar_prefetch=1,
            grid=(1,),
            in_specs=[
                pl.BlockSpec((share, width), lambda i, p: (0, 0)),
                pl.BlockSpec((1, width, lanes), lambda i, p: (1, 0, p[0] // per_lanes)),
                pl.BlockSpec((1, width, width), lambda i, p: (1, 0, 0)),
                pl.BlockSpec((share, width), lambda i, p: (p[0], 0)),
            ],
            out_specs=(
                pl.BlockSpec((share, width), lambda i, p: (0, 0)),
                pl.BlockSpec((2, share, width), lambda i, p: (0, 0, 0)),
            ),
        ),
        cost_estimate=pl.CostEstimate(
            flops=2 * width * width * share, bytes_accessed=600_000, transcendentals=0
        ),
    )(place, part, rhs_low, inv_low, answer0)


def ancestor_parts(targets, answer0, answer1, blocks):
    loads, width = answer0.shape
    per_row = blocks.shape[1]
    count = per_row

    def body(targets_ref, answer0_ref, answer1_ref, block0_ref, block1_ref, out_ref):
        target = pl.program_id(0) + 2
        _, found0 = slot_of(targets_ref, 0, target, per_row)
        _, found1 = slot_of(targets_ref, 1, target, per_row)
        keep0 = jnp.where(found0 == 1, 1.0, 0.0).astype(F32)
        keep1 = jnp.where(found1 == 1, 1.0, 0.0).astype(F32)
        total = dot_nt(answer0_ref[...], block0_ref[0, 0]) * keep0
        total += dot_nt(answer1_ref[...], block1_ref[0, 0]) * keep1
        out_ref[...] = total.astype(BF16)

    def block_spec(level):
        return pl.BlockSpec(
            (1, 1, width, width),
            lambda a, t: (level, slot_of(t, level, a + 2, per_row)[0], 0, 0),
        )

    return pl.pallas_call(
        body,
        out_shape=jax.ShapeDtypeStruct((loads, count * width), BF16),
        grid_spec=pltpu.PrefetchScalarGridSpec(
            num_scalar_prefetch=1,
            grid=(count,),
            in_specs=[
                pl.BlockSpec((loads, width), lambda a, t: (0, 0)),
                pl.BlockSpec((loads, width), lambda a, t: (0, 0)),
                block_spec(0),
                block_spec(1),
            ],
            out_specs=pl.BlockSpec((loads, width), lambda a, t: (0, a)),
        ),
        compiler_params=pltpu.CompilerParams(vmem_limit_bytes=40 << 20),
        cost_estimate=pl.CostEstimate(
            flops=4 * count * width * width * loads, bytes_accessed=5_000_000, transcendentals=0
        ),
    )(targets, answer0, answer1, blocks, blocks)


def ancestor_solve(arrived, rhs_anc, inv_anc):
    sources, loads, _ = arrived.shape
    count, _, width = rhs_anc.shape

    def body(arrived_ref, rhs_ref, inv_ref, out_ref):
        total = jnp.sum(arrived_ref[...].astype(F32), axis=0)
        residual = (rhs_ref[0].astype(F32) - total).astype(BF16)
        out_ref[0] = dot_nt(residual, inv_ref[0])

    return pl.pallas_call(
        body,
        out_shape=jax.ShapeDtypeStruct((count, loads, width), F32),
        grid=(count,),
        in_specs=[
            pl.BlockSpec((sources, loads, width), lambda a: (0, 0, a)),
            pl.BlockSpec((1, loads, width), lambda a: (a, 0, 0)),
            pl.BlockSpec((1, width, width), lambda a: (a, 0, 0)),
        ],
        out_specs=pl.BlockSpec((1, loads, width), lambda a: (a, 0, 0)),
        compiler_params=pltpu.CompilerParams(vmem_limit_bytes=40 << 20),
        cost_estimate=pl.CostEstimate(
            flops=2 * count * width * width * loads, bytes_accessed=3_000_000, transcendentals=0
        ),
    )(arrived, rhs_anc, inv_anc)


def on_device(rhs_low, inv_low, blocks, targets, rhs_anc, inv_anc):
    rows, cols = lax.axis_size("row"), lax.axis_size("col")
    rhs_low, inv_low = rhs_low[0, :, 0], inv_low[0, :, 0]
    blocks, targets = blocks[0, 0, 0], targets[0, 0, 0]
    width, loads = rhs_low.shape[1:]
    share = loads // rows
    place = lax.axis_index("row").astype(jnp.int32).reshape(1)

    answer0, part = first_level(targets, place, rhs_low, inv_low, blocks, share)
    shares = lax.all_to_all(part.reshape(cols, share, width), "col", 0, 0, tiled=True)
    summed = shares.astype(F32).sum(axis=0).astype(BF16)
    turn = [
        (row * cols + col, col * cols + (row - 1) % rows)
        for row in range(rows)
        for col in range(cols)
    ]
    summed = lax.ppermute(summed, ("row", "col"), turn)
    piece, both = second_level(place, summed, rhs_low, inv_low, answer0)
    answer1 = lax.all_gather(piece, "row", axis=0, tiled=True)

    parts = ancestor_parts(targets, answer0, answer1, blocks)
    pieces = lax.axis_size("layer") * cols
    arrived = lax.all_to_all(
        parts.reshape(pieces, loads // pieces, -1), ("layer", "col"), 0, 0, tiled=True
    )
    solved = ancestor_solve(arrived, jnp.swapaxes(rhs_anc, 1, 2), inv_anc)
    return (jnp.swapaxes(both, 1, 2)[None, :, None], jnp.swapaxes(solved, 1, 2))


def solution(mesh):
    in_specs = (
        P("layer", None, "col", None, None),
        P("layer", None, "col", None, None),
        P("layer", "row", "col", None, None, None, None),
        P("layer", "row", "col", None, None),
        P("row", None, ("layer", "col")),
        P("row", None, None),
    )
    out_specs = (P("layer", None, "col", None, "row"), P("row", None, ("layer", "col")))
    return jax.shard_map(
        on_device, mesh=mesh, in_specs=in_specs, out_specs=out_specs, check_vma=False
    )
```

time: 202 us -> 116 us (0.57)
  the two profiles are of different devices: /device:TPU:2 before, /device:TPU:8 now
where the time goes in v1:
time: 116 us; the launch traced here: 115 us
  blocking collectives  91.9 us (79%)
  Pallas kernels  8.82 us (8%)
  waiting for transfers between devices  6.01 us (5%)
  local copies, waits for them, and re-layouts  5.91 us (5%)
  starting transfers between devices  1.92 us (2%)
    all_to_all x1, blocking collectives, on_device(): lax.all_to_all(parts.reshape(pieces, loads // pieces, -1), ('layer', 'col...  54.9 us
    all_to_all x1, blocking collectives, on_device(): lax.all_to_all(part.reshape(cols, share, width), 'col', 0, 0, tiled=True)  20.8 us
    all_gather x1, blocking collectives, on_device(): answer1 = lax.all_gather(piece, 'row', axis=0, tiled=True)  16.2 us
    ppermute x1, waiting for transfers between devices, on_device(): summed = lax.ppermute(summed, ('row', 'col'), turn)  6.01 us
    unnamed x22, local copies, waits for them, and re-layouts  5.91 us
    pallas_call x1, Pallas kernels, ancestor_parts(): pl.pallas_call(body, out_shape=jax.ShapeDtypeStruct((loads, count * width...  3.36 us
  transfers between devices with their start and end apart: 1, of which 1 were waited for; matrix products, arithmetic and copies ran while one was open for 0% of the time, Pallas kernels for 0%

profile of v1, /device:TPU:8, one launch (start us, length us, event | category | flops | bytes accessed | tf_op | source)
XLA Modules:
  0.0 115.3 jit_solution(8735701158621918582)
XLA Ops:
  0.6 0.0 copy-start
  0.6 1.7 %copy-done = bf16[1,1,1,2,4,384,384]{6,5,4,3,2,1,0:T(8,128)(2,1)S(1)} copy-done((bf16[1,1,1,2,4,384,384]{6,5,4,3,2,1,0:T(8,128)(2,1)S(1)}, bf16[1,1,1,2,4,384,384]{6,5,4,3,2,1,0:T(8,128)(2,1)}, u32[]{:S(2)}) %copy-start) | copy-done | bytes 2359320
  2.3 0.0 copy-start.2
  2.3 1.1 copy-done.2
  3.4 0.0 copy-start.3
  3.4 1.1 copy-done.3
  4.5 0.0 copy-start.8
  4.5 0.7 copy-done.8
  5.2 1.4 %shard_map.77 = (bf16[512,384]{1,0:T(8,128)(2,1)S(1)}, bf16[512,384]{1,0:T(8,128)(2,1)S(1)}) custom-call(s32[2,4]{1,0:T(2,128)S(1)} %bitcast.24, s32[1]{0:T(128)} %bitcast.place_ref, bf16[2,384,512]{2,1,0:T(8,128)(2,1)S(1)} %bitcast.19, bf16[2,384,384]{2,1,0:T(8,128)(2,1)S(1)} %bitcast.21, bf16[2,4,384,384]{3,2,1,0:T(8,128)(2,1)S(1)} %bitcast.14), custom_call_target="tpu_custom_call" | custom-call | flops 301989888 | bytes 2200000 | tf_op jit(solution)/shard_map/pallas_call | solution.py:44
  6.6 0.0 copy-start.4
  6.6 0.7 copy-done.4
  7.3 0.0 copy-start.1
  7.3 0.0 copy-start.5
  7.3 0.0 copy-start.9
  7.3 20.8 %all_to_all.10 = bf16[8,64,384]{2,1,0:T(8,128)(2,1)S(1)} all-to-all(bf16[8,64,384]{2,1,0:T(8,128)(2,1)S(1)} %bitcast.22), channel_id=1, replica_groups=mesh['layer'=8,'row'=8,'col'=8] {'col'}, dimensions={0} | all-to-all | bytes 786432 | tf_op jit(solution)/shard_map/all_to_all | solution.py:193
  28.2 0.1 reduce_sum.12
  28.2 1.9 %collective-permute-start = (bf16[64,384]{1,0:T(8,128)(2,1)S(1)}, bf16[64,384]{1,0:T(8,128)(2,1)S(1)}, u32[]{:S(2)}, u32[]{:S(2)}) collective-permute-start(bf16[64,384]{1,0:T(8,128)(2,1)S(1)} %reduce_sum.12), channel_id=1, source_target_pairs={{0,7},{1,15},{2,23},{3,31},{4,39},{5,47},{6,55},{7,63},{8,0},{9,8}... | collective-permute-start | bytes 147464 | tf_op jit(solution)/shard_map/ppermute | solution.py:200
  30.1 6.0 %collective-permute-done.part_ref = bf16[64,384]{1,0:T(8,128)(2,1)S(1)} collective-permute-done((bf16[64,384]{1,0:T(8,128)(2,1)S(1)}, bf16[64,384]{1,0:T(8,128)(2,1)S(1)}, u32[]{:S(2)}, u32[]{:S(2)}) %collective-permute-start) | collective-permute-done | bytes 49184 | tf_op jit(solution)/shard_map/ppermute | solution.py:200
  36.2 0.0 copy-start.10
  36.2 0.6 copy-done.10
  36.8 2.0 %shard_map.78 = (bf16[64,384]{1,0:T(8,128)(2,1)}, bf16[2,64,384]{2,1,0:T(8,128)(2,1)}) custom-call(s32[1]{0:T(128)} %bitcast.place_ref, bf16[64,384]{1,0:T(8,128)(2,1)} %copy-done.10, bf16[2,384,512]{2,1,0:T(8,128)(2,1)} %bitcast.18, bf16[2,384,384]{2,1,0:T(8,128)(2,1)} %bitcast.20, bf16[512,384]{1,0:T(8,128)(2,1)} %copy-done.4), custom_call_target="tpu_custom_call" | custom-call | flops 18874368 | bytes 600000 | tf_op jit(solution)/shard_map/pallas_call | solution.py:90
  38.8 16.2 %all_gather.3.answer1_ref = bf16[512,384]{1,0:T(8,128)(2,1)S(1)} all-gather(bf16[64,384]{1,0:T(8,128)(2,1)} %get-tuple-element.9), channel_id=1, replica_groups=mesh['layer'=8,'row'=8,'col'=8] {'row'}, dimensions={0}, use_global_device_ids=true | all-gather | bytes 442368 | tf_op jit(solution)/shard_map/all_gather | solution.py:202
  55.0 0.0 copy-done.1
  55.0 0.0 copy-done.5
  55.0 0.0 copy-done.9
  55.0 3.4 %shard_map.79 = bf16[512,1536]{1,0:T(8,128)(2,1)S(1)} custom-call(s32[2,4]{1,0:T(2,128)S(1)} %bitcast.25, bf16[512,384]{1,0:T(8,128)(2,1)S(1)} %copy-done.5, bf16[512,384]{1,0:T(8,128)(2,1)S(1)} %all_gather.3.answer1_ref, bf16[2,4,384,384]{3,2,1,0:T(8,128)(2,1)S(1)} %bitcast.15, bf16[2,4,384,384]{3,2,1,0:T(8,128)(2,1)S(1)} %bitcast.16), custom_call_target="tpu_custom_call" | custom-call | flops 1207959552 | bytes 5000000 | tf_op jit(solution)/shard_map/pallas_call | solution.py:137
  58.4 0.0 copy-start.6
  58.4 0.0 copy-start.7
  58.4 54.9 %all_to_all.11.arrived_ref = bf16[64,8,1536]{2,1,0:T(8,128)(2,1)S(1)} all-to-all(bf16[64,8,1536]{2,1,0:T(8,128)(2,1)S(1)} %bitcast.17), channel_id=1, replica_groups=mesh['layer'=8,'row'=8,'col'=8] {'layer','col'}, dimensions={0} | all-to-all | bytes 3145728 | tf_op jit(solution)/shard_map/all_to_all | solution.py:206
  113.3 0.0 copy-done.6
  113.3 0.0 copy-done.7
  113.3 2.1 %shard_map.80 = f32[4,8,384]{2,1,0:T(8,128)} custom-call(bf16[64,8,1536]{2,1,0:T(8,128)(2,1)S(1)} %all_to_all.11.arrived_ref, bf16[4,8,384]{2,1,0:T(8,128)(2,1)S(1)} %bitcast.23, bf16[4,384,384]{2,1,0:T(8,128)(2,1)S(1)} %copy-done.6), custom_call_target="tpu_custom_call" | custom-call | flops 9437184 | bytes 3000000 | tf_op jit(solution)/shard_map/pallas_call | solution.py:167
Async XLA Ops:
  0.6 1.7 %copy-start = (bf16[1,1,1,2,4,384,384]{6,5,4,3,2,1,0:T(8,128)(2,1)S(1)}, bf16[1,1,1,2,4,384,384]{6,5,4,3,2,1,0:T(8,128)(2,1)}, u32[]{:S(2)}) copy-start(bf16[1,1,1,2,4,384,384]{6,5,4,3,2,1,0:T(8,128)(2,1)} %param.8) | copy-start | bytes 7077892
  2.3 1.1 copy-start.2
  3.4 1.1 copy-start.3
  4.5 0.7 copy-start.8
  6.6 0.7 copy-start.4
  7.3 47.7 %copy-start.1 = (bf16[1,1,1,2,4,384,384]{6,5,4,3,2,1,0:T(8,128)(2,1)S(1)}, bf16[1,1,1,2,4,384,384]{6,5,4,3,2,1,0:T(8,128)(2,1)}, u32[]{:S(2)}) copy-start(bf16[1,1,1,2,4,384,384]{6,5,4,3,2,1,0:T(8,128)(2,1)} %param.8) | copy-start | bytes 7077892
  7.3 47.7 %copy-start.5 = (bf16[512,384]{1,0:T(8,128)(2,1)S(1)}, bf16[512,384]{1,0:T(8,128)(2,1)}, u32[]{:S(2)}) copy-start(bf16[512,384]{1,0:T(8,128)(2,1)} %copy-done.4) | copy-start | bytes 1179652
  7.3 47.7 %copy-start.9 = (s32[1,1,1,2,4]{4,3,2,1,0:T(2,128)S(1)}, s32[1,1,1,2,4]{4,3,2,1,0:T(2,128)}, u32[]{:S(2)}) copy-start(s32[1,1,1,2,4]{4,3,2,1,0:T(2,128)} %param.9) | copy-start | bytes 100
  28.2 7.9 %collective-permute-start = (bf16[64,384]{1,0:T(8,128)(2,1)S(1)}, bf16[64,384]{1,0:T(8,128)(2,1)S(1)}, u32[]{:S(2)}, u32[]{:S(2)}) collective-permute-start(bf16[64,384]{1,0:T(8,128)(2,1)S(1)} %reduce_sum.12), channel_id=1, source_target_pairs={{0,7},{1,15},{2,23},{3,31},{4,39},{5,47},{6,55},{7,63},{8,0},{9,8}... | collective-permute-start | bytes 147464 | tf_op jit(solution)/shard_map/ppermute | solution.py:200
  36.2 0.6 copy-start.10
  58.4 54.9 %copy-start.6 = (bf16[4,384,384]{2,1,0:T(8,128)(2,1)S(1)}, bf16[4,384,384]{2,1,0:T(8,128)(2,1)}, u32[]{:S(2)}) copy-start(bf16[4,384,384]{2,1,0:T(8,128)(2,1)} %inv_ref.1) | copy-start | bytes 3538948
  58.4 54.9 %copy-start.7 = (bf16[4,384,8]{1,2,0:T(8,128)(2,1)S(1)}, bf16[4,384,8]{1,2,0:T(8,128)(2,1)}, u32[]{:S(2)}) copy-start(bf16[4,384,8]{1,2,0:T(8,128)(2,1)} %param.10) | copy-start | bytes 73732

commit v2 on v1

v2 whole, which is shorter than its diff:
```python
import jax
import jax.numpy as jnp
from jax import lax
from jax.experimental import pallas as pl
from jax.experimental.pallas import tpu as pltpu
from jax.sharding import PartitionSpec as P

F32 = jnp.float32
BF16 = jnp.bfloat16
NT = (((1,), (1,)), ((), ()))


def dot_nt(left, right):
    return lax.dot_general(left, right, NT, preferred_element_type=F32)


def slot_of(targets_ref, level, target, per_row):
    slot, found = jnp.int32(0), jnp.int32(0)
    for member in range(per_row):
        hit = targets_ref[level, member] == target
        slot = jnp.where(hit, jnp.int32(member), slot)
        found = jnp.where(hit, jnp.int32(1), found)
    return slot, found


def first_level(targets, rhs_low, inv_low, blocks, rows):
    _, width, loads = rhs_low.shape
    per_row = blocks.shape[1]
    share = loads // rows
    steps = 2
    held = rows // steps

    def body(targets_ref, rhs_ref, inv_ref, block_ref, answer_ref, part_ref):
        answer = jnp.dot(inv_ref[0], rhs_ref[0], preferred_element_type=F32).T.astype(BF16)
        for member in range(held):
            answer_ref[member % 2, member // 2] = answer[member * share : (member + 1) * share]
        _, found = slot_of(targets_ref, 0, 1, per_row)

        @pl.when(found == 1)
        def _():
            part = dot_nt(answer, block_ref[0, 0]).astype(BF16)
            part_ref[...] = part.reshape(held, share, width)

        @pl.when(found == 0)
        def _():
            part_ref[...] = jnp.zeros_like(part_ref)

    return pl.pallas_call(
        body,
        out_shape=(
            jax.ShapeDtypeStruct((2, rows // 2, share, width), BF16),
            jax.ShapeDtypeStruct((rows, share, width), BF16),
        ),
        grid_spec=pltpu.PrefetchScalarGridSpec(
            num_scalar_prefetch=1,
            grid=(steps,),
            in_specs=[
                pl.BlockSpec((1, width, loads // steps), lambda i, t: (0, 0, i)),
                pl.BlockSpec((1, width, width), lambda i, t: (0, 0, 0)),
                pl.BlockSpec(
                    (1, 1, width, width), lambda i, t: (0, slot_of(t, 0, 1, per_row)[0], 0, 0)
                ),
            ],
            out_specs=(
                pl.BlockSpec((2, held // 2, share, width), lambda i, t: (0, i, 0, 0)),
                pl.BlockSpec((held, share, width), lambda i, t: (i, 0, 0)),
            ),
        ),
        compiler_params=pltpu.CompilerParams(vmem_limit_bytes=60 << 20),
        cost_estimate=pl.CostEstimate(
            flops=4 * width * width * loads, bytes_accessed=2_200_000, transcendentals=0
        ),
    )(targets, rhs_low, inv_low, blocks)


def turned_share(place, rhs_low, level, share):
    width = rhs_low.shape[1]
    lanes = max(share, 128)
    per_lanes = lanes // share

    def body(place_ref, rhs_ref, out_ref):
        turned = rhs_ref[0].astype(F32).T
        picked = turned[:share]
        for other in range(1, per_lanes):
            picked = jnp.where(
                place_ref[0] % per_lanes == other,
                turned[other * share : (other + 1) * share],
                picked,
            )
        out_ref[...] = picked.astype(BF16)

    return pl.pallas_call(
        body,
        out_shape=jax.ShapeDtypeStruct((share, width), BF16),
        grid_spec=pltpu.PrefetchScalarGridSpec(
            num_scalar_prefetch=1,
            grid=(1,),
            in_specs=[pl.BlockSpec((1, width, lanes), lambda i, p: (level, 0, p[0] // per_lanes))],
            out_specs=pl.BlockSpec((share, width), lambda i, p: (0, 0)),
        ),
        cost_estimate=pl.CostEstimate(
            flops=width * width * 1000, bytes_accessed=2_000_000, transcendentals=0
        ),
    )(place, rhs_low)


def second_level(place, part, right_side, inv_low, answer0, copies):
    share, width = part.shape

    def body(place_ref, part_ref, rhs_ref, inv_ref, answer0_ref, answer_ref, both_ref):
        residual = (rhs_ref[...].astype(F32) - part_ref[...].astype(F32)).astype(BF16)
        answer = dot_nt(residual, inv_ref[0]).astype(BF16)
        for copy in range(copies):
            answer_ref[copy] = answer
        both_ref[0] = answer0_ref[0, 0]
        both_ref[1] = answer

    return pl.pallas_call(
        body,
        out_shape=(
            jax.ShapeDtypeStruct((copies, share, width), BF16),
            jax.ShapeDtypeStruct((2, share, width), BF16),
        ),
        grid_spec=pltpu.PrefetchScalarGridSpec(
            num_scalar_prefetch=1,
            grid=(1,),
            in_specs=[
                pl.BlockSpec((share, width), lambda i, p: (0, 0)),
                pl.BlockSpec((share, width), lambda i, p: (0, 0)),
                pl.BlockSpec((1, width, width), lambda i, p: (1, 0, 0)),
                pl.BlockSpec((1, 1, share, width), lambda i, p: (p[0] % 2, p[0] // 2, 0, 0)),
            ],
            out_specs=(
                pl.BlockSpec((copies, share, width), lambda i, p: (0, 0, 0)),
                pl.BlockSpec((2, share, width), lambda i, p: (0, 0, 0)),
            ),
        ),
        compiler_params=pltpu.CompilerParams(vmem_limit_bytes=30 << 20),
        cost_estimate=pl.CostEstimate(
            flops=2 * width * width * share, bytes_accessed=600_000, transcendentals=0
        ),
    )(place, part, right_side, inv_low, answer0)


def ancestor_parts(targets, place, answer0, answer1, blocks, flip, first, count):
    _, held, share, width = answer0.shape
    per_row = blocks.shape[1]
    loads = held * share

    def body(targets_ref, place_ref, answer0_ref, answer1_ref, block0_ref, block1_ref, out_ref):
        target = pl.program_id(0) + 2 + first
        _, found0 = slot_of(targets_ref, 0, target, per_row)
        _, found1 = slot_of(targets_ref, 1, target, per_row)
        keep0 = jnp.where(found0 == 1, 1.0, 0.0).astype(F32)
        keep1 = jnp.where(found1 == 1, 1.0, 0.0).astype(F32)
        total = dot_nt(answer0_ref[0].reshape(loads, width), block0_ref[0, 0]) * keep0
        total += dot_nt(answer1_ref[0].reshape(loads, width), block1_ref[0, 0]) * keep1
        out_ref[...] = total.astype(BF16)

    def answer_spec():
        return pl.BlockSpec((1, held, share, width), lambda a, t, p: ((p[1] + flip) % 2, 0, 0, 0))

    def block_spec(level):
        return pl.BlockSpec(
            (1, 1, width, width),
            lambda a, t, p: (level, slot_of(t, level, a + 2 + first, per_row)[0], 0, 0),
        )

    return pl.pallas_call(
        body,
        out_shape=jax.ShapeDtypeStruct((loads, count * width), BF16),
        grid_spec=pltpu.PrefetchScalarGridSpec(
            num_scalar_prefetch=2,
            grid=(count,),
            in_specs=[answer_spec(), answer_spec(), block_spec(0), block_spec(1)],
            out_specs=pl.BlockSpec((loads, width), lambda a, t, p: (0, a)),
        ),
        compiler_params=pltpu.CompilerParams(vmem_limit_bytes=30 << 20),
        cost_estimate=pl.CostEstimate(
            flops=4 * count * width * width * loads, bytes_accessed=5_000_000, transcendentals=0
        ),
    )(targets, place, answer0, answer1, blocks, blocks)


def ancestor_solve(arrived, rhs_anc, inv_anc):
    sources, loads, _ = arrived.shape
    count, _, width = rhs_anc.shape

    def body(arrived_ref, rhs_ref, inv_ref, out_ref):
        total = jnp.sum(arrived_ref[...].astype(F32), axis=0)
        residual = (rhs_ref[0].astype(F32) - total).astype(BF16)
        out_ref[0] = dot_nt(residual, inv_ref[0])

    return pl.pallas_call(
        body,
        out_shape=jax.ShapeDtypeStruct((count, loads, width), F32),
        grid=(count,),
        in_specs=[
            pl.BlockSpec((sources, loads, width), lambda a: (0, 0, a)),
            pl.BlockSpec((1, loads, width), lambda a: (a, 0, 0)),
            pl.BlockSpec((1, width, width), lambda a: (a, 0, 0)),
        ],
        out_specs=pl.BlockSpec((1, loads, width), lambda a: (a, 0, 0)),
        compiler_params=pltpu.CompilerParams(vmem_limit_bytes=40 << 20),
        cost_estimate=pl.CostEstimate(
            flops=2 * count * width * width * loads, bytes_accessed=3_000_000, transcendentals=0
        ),
    )(arrived, rhs_anc, inv_anc)


def on_device(rhs_low, inv_low, blocks, targets, rhs_anc, inv_anc):
    rows, cols = lax.axis_size("row"), lax.axis_size("col")
    rhs_low, inv_low = rhs_low[0, :, 0], inv_low[0, :, 0]
    blocks, targets = blocks[0, 0, 0], targets[0, 0, 0]
    width, loads = rhs_low.shape[1:]
    share = loads // rows
    layers, count = lax.axis_size("layer"), inv_anc.shape[0]
    place = jnp.stack([lax.axis_index("row"), lax.axis_index("layer") & 1]).astype(jnp.int32)

    answer0, part = first_level(targets, rhs_low, inv_low, blocks, rows)
    right_side = turned_share(place, rhs_low, 1, share)
    shares = lax.all_to_all(part, "col", 0, 0, tiled=True)
    summed = shares.astype(F32).sum(axis=0).astype(BF16)
    turn = [
        (row * cols + col, col * cols + (row - 1) % rows)
        for row in range(rows)
        for col in range(cols)
    ]
    summed = lax.ppermute(summed, ("row", "col"), turn)
    pieces, both = second_level(place, summed, right_side, inv_low, answer0, rows // 2)
    lines = [list(range(core, rows, 2)) for core in range(2)]
    chips = [[row, row + 1] for row in range(0, rows, 2)]
    pieces = lax.all_to_all(pieces, "row", 0, 0, axis_index_groups=lines, tiled=True)
    answer1 = lax.all_gather(pieces, "row", axis=0, axis_index_groups=chips)

    half = count // 2
    near = [(layer, layer ^ 1) for layer in range(layers)]
    far = [(layer, (layer + (1 if layer % 2 else -1)) % layers) for layer in range(layers)]
    give_near = ancestor_parts(targets, place, answer0, answer1, blocks, 1, 0, half)
    got_near = lax.ppermute(give_near, "layer", near)
    give_far = ancestor_parts(targets, place, answer0, answer1, blocks, 1, half, count - half)
    got_far = lax.ppermute(give_far, "layer", far)
    kept = ancestor_parts(targets, place, answer0, answer1, blocks, 0, 0, count)
    got = jnp.concatenate([got_near, got_far], axis=1)
    parts = (kept.astype(F32) + got.astype(F32)).astype(BF16)
    groups = [
        [layer * cols + col for layer in range(parity, layers, 2) for col in range(cols)]
        for parity in range(2)
    ]
    members = len(groups[0])
    arrived = lax.all_to_all(
        parts.reshape(members, parts.shape[0] // members, -1),
        ("layer", "col"),
        0,
        0,
        axis_index_groups=groups,
        tiled=True,
    )
    solved = ancestor_solve(arrived, jnp.swapaxes(rhs_anc, 1, 2), inv_anc)
    return (jnp.swapaxes(both, 1, 2)[None, :, None], jnp.swapaxes(solved, 1, 2))


def solution(mesh):
    in_specs = (
        P("layer", None, "col", None, None),
        P("layer", None, "col", None, None),
        P("layer", "row", "col", None, None, None, None),
        P("layer", "row", "col", None, None),
        P("row", None, ("layer", "col")),
        P("row", None, None),
    )
    out_specs = (P("layer", None, "col", None, "row"), P("row", None, ("layer", "col")))
    return jax.shard_map(
        on_device, mesh=mesh, in_specs=in_specs, out_specs=out_specs, check_vma=False
    )
```

time: 116 us -> 113 us (0.974)
  blocking collectives: 91.9 us -> 47.2 us
  starting transfers between devices: 1.92 us -> 25.2 us
  waiting for transfers between devices: 6.01 us -> 20.7 us
  Pallas kernels: 8.82 us -> 15 us
  local copies, waits for them, and re-layouts: 5.91 us -> 1.49 us
  other arithmetic: 0.06 us -> 1.9 us
    all_to_all x2, blocking collectives: 75.7 us -> 45.1 us  [the longest x1 31.4 us: on_device(): lax.all_to_all(parts.reshape(members, parts.shape[0] // members, -1), ('l...]
    all_gather x1, blocking collectives: 16.2 us -> 2.08 us  [on_device(): answer1 = lax.all_gather(pieces, 'row', axis=0, axis_index_groups=chips)]
    ppermute x0 -> x2, starting transfers between devices: none -> 13.4 us  [the longest x1 9.67 us: on_device(): got_far = lax.ppermute(give_far, 'layer', far)]
    all_to_all x0 -> x1, waiting for transfers between devices: none -> 11 us  [on_device(): shares = lax.all_to_all(part, 'col', 0, 0, tiled=True)]
    all_to_all x0 -> x1, starting transfers between devices: none -> 9.93 us  [on_device(): shares = lax.all_to_all(part, 'col', 0, 0, tiled=True)]
    ppermute x0 -> x2, waiting for transfers between devices: none -> 6.64 us  [the longest x1 6.64 us: on_device(): got_far = lax.ppermute(give_far, 'layer', far)]
    unnamed x22 -> x18, local copies, waits for them, and re-layouts: 5.91 us -> 1.49 us
    pallas_call x2 -> x3, Pallas kernels: 3.39 us -> 7.64 us  [the longest x1 3.93 us: first_level(): pl.pallas_call(body, out_shape=(jax.ShapeDtypeStruct((2, rows // 2, share...]
  transfers between devices with their start and end apart: 1 -> 4, of which waited for: 1 -> 3; matrix products, arithmetic and copies ran while one was open for 0% -> 1% of each run, Pallas kernels for 0% -> 4%
where the time goes in v2:
time: 113 us; the launch traced here: 112 us
  blocking collectives  47.2 us (42%)
  starting transfers between devices  25.2 us (22%)
  waiting for transfers between devices  20.7 us (18%)
  Pallas kernels  15 us (13%)
  other arithmetic  1.9 us (2%)
  local copies, waits for them, and re-layouts  1.49 us (1%)
    all_to_all x1, blocking collectives, on_device(): lax.all_to_all(parts.reshape(members, parts.shape[0] // members, -1), ('l...  31.4 us
    all_to_all x1, blocking collectives, on_device(): lax.all_to_all(pieces, 'row', 0, 0, axis_index_groups=lines, tiled=True)  13.7 us
    all_to_all x1, waiting for transfers between devices, on_device(): shares = lax.all_to_all(part, 'col', 0, 0, tiled=True)  11 us
    all_to_all x1, starting transfers between devices, on_device(): shares = lax.all_to_all(part, 'col', 0, 0, tiled=True)  9.93 us
    ppermute x1, starting transfers between devices, on_device(): got_far = lax.ppermute(give_far, 'layer', far)  9.67 us
    ppermute x1, waiting for transfers between devices, on_device(): got_far = lax.ppermute(give_far, 'layer', far)  6.64 us
    pallas_call x3, Pallas kernels, ancestor_parts(): pl.pallas_call(body, out_shape=jax.ShapeDtypeStruct((loads, count * width...  5.44 us
    pallas_call x1, Pallas kernels, first_level(): pl.pallas_call(body, out_shape=(jax.ShapeDtypeStruct((2, rows // 2, share...  3.93 us
  transfers between devices with their start and end apart: 4, of which 3 were waited for; matrix products, arithmetic and copies ran while one was open for 1% of the time, Pallas kernels for 4%

profile of v2, /device:TPU:8, one launch (start us, length us, event | category | flops | bytes accessed | tf_op | source)
XLA Modules:
  0.0 112.3 jit_solution(3904906375634667595)
XLA Ops:
  0.6 3.9 %shard_map.77 = (bf16[2,4,64,384]{3,2,1,0:T(8,128)(2,1)}, bf16[8,64,384]{2,1,0:T(8,128)(2,1)}) custom-call(s32[2,4]{1,0:T(2,128)} %bitcast.29, bf16[2,384,512]{2,1,0:T(8,128)(2,1)} %bitcast.33, bf16[2,384,384]{2,1,0:T(8,128)(2,1)} %bitcast.26, bf16[2,4,384,384]{3,2,1,0:T(8,128)(2,1)} %bitcast.16), custom_call_target="tpu_custom_call" | custom-call | flops 301989888 | bytes 2200000 | tf_op jit(solution)/shard_map/pallas_call | solution.py:48
  4.6 0.0 copy-start.1
  4.6 0.0 copy-start.2
  4.6 9.9 %all-to-all-start = ((bf16[8,64,384]{2,1,0:T(8,128)(2,1)}), bf16[8,64,384]{2,1,0:T(8,128)(2,1)}, u32[]{:S(2)}, u32[]{:S(2)}) async-start(bf16[8,64,384]{2,1,0:T(8,128)(2,1)} %get-tuple-element.6), calls=%async_computation | async-start | bytes 786432 | tf_op jit(solution)/shard_map/all_to_all | solution.py:222
  14.5 0.0 copy-start
  14.5 11.0 %all-to-all-done = bf16[8,64,384]{2,1,0:T(8,128)(2,1)} async-done(((bf16[8,64,384]{2,1,0:T(8,128)(2,1)}), bf16[8,64,384]{2,1,0:T(8,128)(2,1)}, u32[]{:S(2)}, u32[]{:S(2)}) %all-to-all-start) | async-done | bytes 393248 | tf_op jit(solution)/shard_map/all_to_all | solution.py:222
  25.5 1.1 reduce_sum.12
  26.6 1.9 %collective-permute-start = (bf16[64,384]{1,0:T(8,128)(2,1)S(1)}, bf16[64,384]{1,0:T(8,128)(2,1)S(1)}, u32[]{:S(2)}, u32[]{:S(2)}) collective-permute-start(bf16[64,384]{1,0:T(8,128)(2,1)S(1)} %reduce_sum.12), channel_id=1, source_target_pairs={{0,7},{1,15},{2,23},{3,31},{4,39},{5,47},{6,55},{7,63},{8,0},{9,8}... | collective-permute-start | bytes 147464 | tf_op jit(solution)/shard_map/ppermute | solution.py:229
  28.5 0.7 pad_add_fusion.place_ref
  29.2 2.3 %shard_map.78.rhs_ref = bf16[64,384]{1,0:T(8,128)(2,1)} custom-call(s32[2]{0:T(128)} %pad_add_fusion.place_ref, bf16[2,384,512]{2,1,0:T(8,128)(2,1)} %bitcast.34), custom_call_target="tpu_custom_call" | custom-call | flops 147456000 | bytes 2000000 | tf_op jit(solution)/shard_map/pallas_call | solution.py:92
  31.5 3.0 %collective-permute-done.part_ref = bf16[64,384]{1,0:T(8,128)(2,1)S(1)} collective-permute-done((bf16[64,384]{1,0:T(8,128)(2,1)S(1)}, bf16[64,384]{1,0:T(8,128)(2,1)S(1)}, u32[]{:S(2)}, u32[]{:S(2)}) %collective-permute-start) | collective-permute-done | bytes 49184 | tf_op jit(solution)/shard_map/ppermute | solution.py:229
  34.5 0.0 copy-done.1
  34.5 0.0 copy-done.2
  34.5 0.0 copy-start.4
  34.5 0.8 copy-done.4
  35.3 0.0 copy-start.7
  35.3 0.7 copy-done.7
  36.0 0.0 copy-start.6
  36.0 1.4 %shard_map.79 = (bf16[4,64,384]{2,1,0:T(8,128)(2,1)S(1)}, bf16[2,64,384]{2,1,0:T(8,128)(2,1)}) custom-call(s32[2]{0:T(128)S(1)} %copy-done.7, bf16[64,384]{1,0:T(8,128)(2,1)S(1)} %collective-permute-done.part_ref, bf16[64,384]{1,0:T(8,128)(2,1)S(1)} %copy-done.4, bf16[2,384,384]{2,1,0:T(8,128)(2,1)S(1)} %bitcast.27, bf16[2,4,64,384]{3,2,1,0:T(8,128)(2,1)S(1)} %copy-done.1), custom_call_target="tpu_custom_call" | custom-call | flops 18874368 | bytes 600000 | tf_op jit(solution)/shard_map/pallas_call | solution.py:118
  37.4 13.7 %all_to_all.15 = bf16[4,64,384]{2,1,0:T(8,128)(2,1)S(1)} all-to-all(bf16[4,64,384]{2,1,0:T(8,128)(2,1)S(1)} %get-tuple-element.9), channel_id=1, replica_groups={{0,16,32,48},{8,24,40,56},{1,17,33,49},{9,25,41,57},{2,18,34,50},{10,26..., dimensions={0} | all-to-all | bytes 393216 | tf_op jit(solution)/shard_map/all_to_all | solution.py:233
  51.1 2.1 %all-gather = bf16[8,64,384]{2,1,0:T(8,128)(2,1)S(1)} all-gather(bf16[4,64,384]{2,1,0:T(8,128)(2,1)S(1)} %all_to_all.15), channel_id=2, replica_groups={{0,8},{16,24},{32,40},{48,56},{1,9},{17,25},{33,41},{49,57},{2,10},{18,..., dimensions={0}, use_global_device_ids=true | all-gather | bytes 589824 | tf_op jit(solution)/shard_map/all_gather | solution.py:234
  53.2 0.0 copy-done
  53.2 0.0 copy-done.6
  53.2 1.5 %shard_map.82 = bf16[256,768]{1,0:T(8,128)(2,1)S(1)} custom-call(s32[2,4]{1,0:T(2,128)S(1)} %bitcast.30, s32[2]{0:T(128)S(1)} %copy-done.7, bf16[2,4,64,384]{3,2,1,0:T(8,128)(2,1)S(1)} %copy-done.1, bf16[2,4,64,384]{3,2,1,0:T(8,128)(2,1)S(1)} %bitcast.23, bf16[2,4,384,384]{3,2,1,0:T(8,128)(2,1)S(1)} %bitcast.17, bf16[2,4,384,384]{3,2,1,0:T(8,128)(2,1)S(1)} %bitcast.18), custom_call_target="tpu_custom_call" | custom-call | flops 301989888 | bytes 5000000 | tf_op jit(solution)/shard_map/pallas_call | solution.py:169
  54.7 0.0 copy-start.8
  54.7 1.5 %shard_map.81 = bf16[256,768]{1,0:T(8,128)(2,1)S(1)} custom-call(s32[2,4]{1,0:T(2,128)S(1)} %bitcast.31, s32[2]{0:T(128)S(1)} %copy-done.7, bf16[2,4,64,384]{3,2,1,0:T(8,128)(2,1)S(1)} %copy-done.1, bf16[2,4,64,384]{3,2,1,0:T(8,128)(2,1)S(1)} %bitcast.24, bf16[2,4,384,384]{3,2,1,0:T(8,128)(2,1)S(1)} %bitcast.19, bf16[2,4,384,384]{3,2,1,0:T(8,128)(2,1)S(1)} %bitcast.20), custom_call_target="tpu_custom_call" | custom-call | flops 301989888 | bytes 5000000 | tf_op jit(solution)/shard_map/pallas_call | solution.py:169
  56.2 3.7 %collective-permute-start.1 = (bf16[256,768]{1,0:T(8,128)(2,1)S(1)}, bf16[256,768]{1,0:T(8,128)(2,1)S(1)}, u32[]{:S(2)}, u32[]{:S(2)}) collective-permute-start(bf16[256,768]{1,0:T(8,128)(2,1)S(1)} %shard_map.81), channel_id=1, source_target_pairs={{0,64},{64,0},{128,192},{192,128},{256,320},{320,256},{384,448},{4... | collective-permute-start | bytes 1179656 | tf_op jit(solution)/shard_map/ppermute | solution.py:240
  59.9 9.7 %collective-permute-start.2 = (bf16[256,768]{1,0:T(8,128)(2,1)S(1)}, bf16[256,768]{1,0:T(8,128)(2,1)S(1)}, u32[]{:S(2)}, u32[]{:S(2)}) collective-permute-start(bf16[256,768]{1,0:T(8,128)(2,1)S(1)} %shard_map.82), channel_id=1, source_target_pairs={{0,448},{64,128},{128,64},{192,256},{256,192},{320,384},{384,320},... | collective-permute-start | bytes 1179656 | tf_op jit(solution)/shard_map/ppermute | solution.py:242
  69.6 0.0 copy-done.8
  69.6 2.4 %shard_map.80 = bf16[256,1536]{1,0:T(8,128)(2,1)S(1)} custom-call(s32[2,4]{1,0:T(2,128)S(1)} %bitcast.32, s32[2]{0:T(128)S(1)} %copy-done.8, bf16[2,4,64,384]{3,2,1,0:T(8,128)(2,1)S(1)} %copy-done.1, bf16[2,4,64,384]{3,2,1,0:T(8,128)(2,1)S(1)} %bitcast.25, bf16[2,4,384,384]{3,2,1,0:T(8,128)(2,1)S(1)} %bitcast.21, bf16[2,4,384,384]{3,2,1,0:T(8,128)(2,1)S(1)} %bitcast.22), custom_call_target="tpu_custom_call" | custom-call | flops 603979776 | bytes 5000000 | tf_op jit(solution)/shard_map/pallas_call | solution.py:169
  72.1 0.0 copy-start.3
  72.1 0.0 copy-start.5
  72.1 0.0 collective-permute-done.1
  72.1 6.6 %collective-permute-done.2 = bf16[256,768]{1,0:T(8,128)(2,1)S(1)} collective-permute-done((bf16[256,768]{1,0:T(8,128)(2,1)S(1)}, bf16[256,768]{1,0:T(8,128)(2,1)S(1)}, u32[]{:S(2)}, u32[]{:S(2)}) %collective-permute-start.2) | collective-permute-done | bytes 393248 | tf_op jit(solution)/shard_map/ppermute | solution.py:242
  78.7 0.2 fusion
  78.9 31.4 %all_to_all.16.arrived_ref = bf16[32,8,1536]{2,1,0:T(8,128)(2,1)S(1)} all-to-all(bf16[32,8,1536]{2,1,0:T(8,128)(2,1)S(1)} %fusion), channel_id=1, replica_groups={{0,1,2,3,4,5,6,7,128,129,130,131,132,133,134,135,256,257,258,259,260,26..., dimensions={0} | all-to-all | bytes 1572864 | tf_op jit(solution)/shard_map/all_to_all | solution.py:251
  110.3 0.0 copy-done.3
  110.3 0.0 copy-done.5
  110.3 1.9 %shard_map.83 = f32[4,8,384]{2,1,0:T(8,128)} custom-call(bf16[32,8,1536]{2,1,0:T(8,128)(2,1)S(1)} %all_to_all.16.arrived_ref, bf16[4,8,384]{2,1,0:T(8,128)(2,1)S(1)} %bitcast.28, bf16[4,384,384]{2,1,0:T(8,128)(2,1)S(1)} %copy-done.3), custom_call_target="tpu_custom_call" | custom-call | flops 9437184 | bytes 3000000 | tf_op jit(solution)/shard_map/pallas_call | solution.py:194
Async XLA Ops:
  4.6 29.9 %copy-start.1 = (bf16[2,4,64,384]{3,2,1,0:T(8,128)(2,1)S(1)}, bf16[2,4,64,384]{3,2,1,0:T(8,128)(2,1)}, u32[]{:S(2)}) copy-start(bf16[2,4,64,384]{3,2,1,0:T(8,128)(2,1)} %get-tuple-element.7.answer0_ref) | copy-start | bytes 1179652
  4.6 29.9 %copy-start.2 = (bf16[1,2,1,384,384]{4,3,2,1,0:T(8,128)(2,1)S(1)}, bf16[1,2,1,384,384]{4,3,2,1,0:T(8,128)(2,1)}, u32[]{:S(2)}) copy-start(bf16[1,2,1,384,384]{4,3,2,1,0:T(8,128)(2,1)} %param.7) | copy-start | bytes 1769476
  4.6 21.0 %all-to-all-start = ((bf16[8,64,384]{2,1,0:T(8,128)(2,1)}), bf16[8,64,384]{2,1,0:T(8,128)(2,1)}, u32[]{:S(2)}, u32[]{:S(2)}) async-start(bf16[8,64,384]{2,1,0:T(8,128)(2,1)} %get-tuple-element.6), calls=%async_computation | async-start | bytes 786432 | tf_op jit(solution)/shard_map/all_to_all | solution.py:222
  14.5 38.7 %copy-start = (bf16[1,1,1,2,4,384,384]{6,5,4,3,2,1,0:T(8,128)(2,1)S(1)}, bf16[1,1,1,2,4,384,384]{6,5,4,3,2,1,0:T(8,128)(2,1)}, u32[]{:S(2)}) copy-start(bf16[1,1,1,2,4,384,384]{6,5,4,3,2,1,0:T(8,128)(2,1)} %param.8) | copy-start | bytes 7077892
  26.6 7.9 %collective-permute-start = (bf16[64,384]{1,0:T(8,128)(2,1)S(1)}, bf16[64,384]{1,0:T(8,128)(2,1)S(1)}, u32[]{:S(2)}, u32[]{:S(2)}) collective-permute-start(bf16[64,384]{1,0:T(8,128)(2,1)S(1)} %reduce_sum.12), channel_id=1, source_target_pairs={{0,7},{1,15},{2,23},{3,31},{4,39},{5,47},{6,55},{7,63},{8,0},{9,8}... | collective-permute-start | bytes 147464 | tf_op jit(solution)/shard_map/ppermute | solution.py:229
  34.5 0.8 copy-start.4
  35.3 0.7 copy-start.7
  36.0 17.2 %copy-start.6 = (s32[1,1,1,2,4]{4,3,2,1,0:T(2,128)S(1)}, s32[1,1,1,2,4]{4,3,2,1,0:T(2,128)}, u32[]{:S(2)}) copy-start(s32[1,1,1,2,4]{4,3,2,1,0:T(2,128)} %param.9) | copy-start | bytes 100
  54.7 14.9 %copy-start.8 = (s32[2]{0:T(128)S(1)}, s32[2]{0:T(128)}, u32[]{:S(2)}) copy-start(s32[2]{0:T(128)} %pad_add_fusion.place_ref) | copy-start | bytes 28
  56.2 15.9 %collective-permute-start.1 = (bf16[256,768]{1,0:T(8,128)(2,1)S(1)}, bf16[256,768]{1,0:T(8,128)(2,1)S(1)}, u32[]{:S(2)}, u32[]{:S(2)}) collective-permute-start(bf16[256,768]{1,0:T(8,128)(2,1)S(1)} %shard_map.81), channel_id=1, source_target_pairs={{0,64},{64,0},{128,192},{192,128},{256,320},{320,256},{384,448},{4... | collective-permute-start | bytes 1179656 | tf_op jit(solution)/shard_map/ppermute | solution.py:240
  59.9 18.8 %collective-permute-start.2 = (bf16[256,768]{1,0:T(8,128)(2,1)S(1)}, bf16[256,768]{1,0:T(8,128)(2,1)S(1)}, u32[]{:S(2)}, u32[]{:S(2)}) collective-permute-start(bf16[256,768]{1,0:T(8,128)(2,1)S(1)} %shard_map.82), channel_id=1, source_target_pairs={{0,448},{64,128},{128,64},{192,256},{256,192},{320,384},{384,320},... | collective-permute-start | bytes 1179656 | tf_op jit(solution)/shard_map/ppermute | solution.py:242
  72.1 38.3 %copy-start.3 = (bf16[4,384,384]{2,1,0:T(8,128)(2,1)S(1)}, bf16[4,384,384]{2,1,0:T(8,128)(2,1)}, u32[]{:S(2)}) copy-start(bf16[4,384,384]{2,1,0:T(8,128)(2,1)} %inv_ref.1) | copy-start | bytes 3538948
  72.1 38.3 %copy-start.5 = (bf16[4,384,8]{1,2,0:T(8,128)(2,1)S(1)}, bf16[4,384,8]{1,2,0:T(8,128)(2,1)}, u32[]{:S(2)}) copy-start(bf16[4,384,8]{1,2,0:T(8,128)(2,1)} %param.10) | copy-start | bytes 73732

commit v3 on v2

--- a/solution.py
+++ b/solution.py
@@ -7,6 +7,9 @@
 
 F32 = jnp.float32
 BF16 = jnp.bfloat16
+SMALL = 8 << 20
+LARGE = 24 << 20
+FIRST = 60 << 20
 NT = (((1,), (1,)), ((), ()))
 
 
@@ -66,80 +69,66 @@
                 pl.BlockSpec((held, share, width), lambda i, t: (i, 0, 0)),
             ),
         ),
-        compiler_params=pltpu.CompilerParams(vmem_limit_bytes=60 << 20),
+        compiler_params=pltpu.CompilerParams(vmem_limit_bytes=FIRST),
         cost_estimate=pl.CostEstimate(
             flops=4 * width * width * loads, bytes_accessed=2_200_000, transcendentals=0
         ),
     )(targets, rhs_low, inv_low, blocks)
 
 
-def turned_share(place, rhs_low, level, share):
-    width = rhs_low.shape[1]
-    lanes = max(share, 128)
-    per_lanes = lanes // share
-
-    def body(place_ref, rhs_ref, out_ref):
-        turned = rhs_ref[0].astype(F32).T
-        picked = turned[:share]
-        for other in range(1, per_lanes):
-            picked = jnp.where(
-                place_ref[0] % per_lanes == other,
-                turned[other * share : (other + 1) * share],
-                picked,
-            )
-        out_ref[...] = picked.astype(BF16)
-
-    return pl.pallas_call(
-        body,
-        out_shape=jax.ShapeDtypeStruct((share, width), BF16),
+def turned_shares(rhs_low, level, rows):
+    _, width, loads = rhs_low.shape
+    share = loads // rows
+    steps = 2
+    held = rows // steps
+
+    def body(rhs_ref, out_ref):
+        turned = rhs_ref[0].astype(F32).T.astype(BF16)
+        for member in range(held):
+            out_ref[member % 2, member // 2] = turned[member * share : (member + 1) * share]
+
+    return pl.pallas_call(
+        body,
+        out_shape=jax.ShapeDtypeStruct((2, rows // 2, share, width), BF16),
+        grid=(steps,),
+        in_specs=[pl.BlockSpec((1, width, loads // steps), lambda i: (level, 0, i))],
+        out_specs=pl.BlockSpec((2, held // 2, share, width), lambda i: (0, i, 0, 0)),
+        compiler_params=pltpu.CompilerParams(vmem_limit_bytes=SMALL),
+        cost_estimate=pl.CostEstimate(
+            flops=width * width * 1000, bytes_accessed=2_000_000, transcendentals=0
+        ),
+    )(rhs_low)
+
+
+def second_level(place, parts, right_sides, inv_low):
+    hops = len(parts)
+    share, width = parts[0].shape
+
+    def body(place_ref, *refs):
+        parts_refs, (rhs_ref, inv_ref, answer_ref) = refs[:hops], refs[hops:]
+        for hop in range(hops):
+            spot = (place_ref[0] // 2 + hops - hop) % hops
+            residual = (rhs_ref[0, spot].astype(F32) - parts_refs[hop][...].astype(F32)).astype(BF16)
+            answer_ref[spot] = dot_nt(residual, inv_ref[0]).astype(BF16)
+
+    return pl.pallas_call(
+        body,
+        out_shape=jax.ShapeDtypeStruct((hops, share, width), BF16),
         grid_spec=pltpu.PrefetchScalarGridSpec(
             num_scalar_prefetch=1,
             grid=(1,),
-            in_specs=[pl.BlockSpec((1, width, lanes), lambda i, p: (level, 0, p[0] // per_lanes))],
-            out_specs=pl.BlockSpec((share, width), lambda i, p: (0, 0)),
-        ),
-        cost_estimate=pl.CostEstimate(
-            flops=width * width * 1000, bytes_accessed=2_000_000, transcendentals=0
-        ),
-    )(place, rhs_low)
-
-
-def second_level(place, part, right_side, inv_low, answer0, copies):
-    share, width = part.shape
-
-    def body(place_ref, part_ref, rhs_ref, inv_ref, answer0_ref, answer_ref, both_ref):
-        residual = (rhs_ref[...].astype(F32) - part_ref[...].astype(F32)).astype(BF16)
-        answer = dot_nt(residual, inv_ref[0]).astype(BF16)
-        for copy in range(copies):
-            answer_ref[copy] = answer
-        both_ref[0] = answer0_ref[0, 0]
-        both_ref[1] = answer
-
-    return pl.pallas_call(
-        body,
-        out_shape=(
-            jax.ShapeDtypeStruct((copies, share, width), BF16),
-            jax.ShapeDtypeStruct((2, share, width), BF16),
-        ),
-        grid_spec=pltpu.PrefetchScalarGridSpec(
-            num_scalar_prefetch=1,
-            grid=(1,),
-            in_specs=[
-                pl.BlockSpec((share, width), lambda i, p: (0, 0)),
-                pl.BlockSpec((share, width), lambda i, p: (0, 0)),
+            in_specs=[pl.BlockSpec((share, width), lambda i, p: (0, 0))] * hops
+            + [
+                pl.BlockSpec((1, hops, share, width), lambda i, p: (p[0] % 2, 0, 0, 0)),
                 pl.BlockSpec((1, width, width), lambda i, p: (1, 0, 0)),
-                pl.BlockSpec((1, 1, share, width), lambda i, p: (p[0] % 2, p[0] // 2, 0, 0)),
-            ],
-            out_specs=(
-                pl.BlockSpec((copies, share, width), lambda i, p: (0, 0, 0)),
-                pl.BlockSpec((2, share, width), lambda i, p: (0, 0, 0)),
-            ),
-        ),
-        compiler_params=pltpu.CompilerParams(vmem_limit_bytes=30 << 20),
-        cost_estimate=pl.CostEstimate(
-            flops=2 * width * width * share, bytes_accessed=600_000, transcendentals=0
-        ),
-    )(place, part, right_side, inv_low, answer0)
+            ],
+            out_specs=pl.BlockSpec((hops, share, width), lambda i, p: (0, 0, 0)),
+        ),
+        compiler_params=pltpu.CompilerParams(vmem_limit_bytes=SMALL),
+        cost_estimate=pl.CostEstimate(
+            flops=2 * width * width * share * hops, bytes_accessed=900_000, transcendentals=0
+        ),
+    )(place, *parts, right_sides, inv_low)
 
 
 def ancestor_parts(targets, place, answer0, answer1, blocks, flip, first, count):
@@ -175,37 +164,55 @@
             in_specs=[answer_spec(), answer_spec(), block_spec(0), block_spec(1)],
             out_specs=pl.BlockSpec((loads, width), lambda a, t, p: (0, a)),
         ),
-        compiler_params=pltpu.CompilerParams(vmem_limit_bytes=30 << 20),
+        compiler_params=pltpu.CompilerParams(vmem_limit_bytes=LARGE),
         cost_estimate=pl.CostEstimate(
             flops=4 * count * width * width * loads, bytes_accessed=5_000_000, transcendentals=0
         ),
     )(targets, place, answer0, answer1, blocks, blocks)
 
 
-def ancestor_solve(arrived, rhs_anc, inv_anc):
+def ancestor_solve(place, arrived, rhs_anc, inv_anc, answer0, answer1):
     sources, loads, _ = arrived.shape
     count, _, width = rhs_anc.shape
-
-    def body(arrived_ref, rhs_ref, inv_ref, out_ref):
+    share = answer0.shape[2]
+
+    def body(place_ref, arrived_ref, rhs_ref, inv_ref, answer0_ref, answer1_ref, out_ref, both_ref):
         total = jnp.sum(arrived_ref[...].astype(F32), axis=0)
         residual = (rhs_ref[0].astype(F32) - total).astype(BF16)
         out_ref[0] = dot_nt(residual, inv_ref[0])
 
-    return pl.pallas_call(
-        body,
-        out_shape=jax.ShapeDtypeStruct((count, loads, width), F32),
-        grid=(count,),
-        in_specs=[
-            pl.BlockSpec((sources, loads, width), lambda a: (0, 0, a)),
-            pl.BlockSpec((1, loads, width), lambda a: (a, 0, 0)),
-            pl.BlockSpec((1, width, width), lambda a: (a, 0, 0)),
-        ],
-        out_specs=pl.BlockSpec((1, loads, width), lambda a: (a, 0, 0)),
-        compiler_params=pltpu.CompilerParams(vmem_limit_bytes=40 << 20),
+        @pl.when(pl.program_id(0) == 0)
+        def _():
+            both_ref[0] = answer0_ref[0, 0]
+            both_ref[1] = answer1_ref[0, 0]
+
+    own = pl.BlockSpec((1, 1, share, width), lambda a, p: (p[0] % 2, p[0] // 2, 0, 0))
+    return pl.pallas_call(
+        body,
+        out_shape=(
+            jax.ShapeDtypeStruct((count, loads, width), F32),
+            jax.ShapeDtypeStruct((2, share, width), BF16),
+        ),
+        grid_spec=pltpu.PrefetchScalarGridSpec(
+            num_scalar_prefetch=1,
+            grid=(count,),
+            in_specs=[
+                pl.BlockSpec((sources, loads, width), lambda a, p: (0, 0, a)),
+                pl.BlockSpec((1, loads, width), lambda a, p: (a, 0, 0)),
+                pl.BlockSpec((1, width, width), lambda a, p: (a, 0, 0)),
+                own,
+                own,
+            ],
+            out_specs=(
+                pl.BlockSpec((1, loads, width), lambda a, p: (a, 0, 0)),
+                pl.BlockSpec((2, share, width), lambda a, p: (0, 0, 0)),
+            ),
+        ),
+        compiler_params=pltpu.CompilerParams(vmem_limit_bytes=LARGE),
         cost_estimate=pl.CostEstimate(
             flops=2 * count * width * width * loads, bytes_accessed=3_000_000, transcendentals=0
         ),
-    )(arrived, rhs_anc, inv_anc)
+    )(place, arrived, rhs_anc, inv_anc, answer0, answer1)
 
 
 def on_device(rhs_low, inv_low, blocks, targets, rhs_anc, inv_anc):
@@ -213,25 +220,29 @@
     rhs_low, inv_low = rhs_low[0, :, 0], inv_low[0, :, 0]
     blocks, targets = blocks[0, 0, 0], targets[0, 0, 0]
     width, loads = rhs_low.shape[1:]
-    share = loads // rows
     layers, count = lax.axis_size("layer"), inv_anc.shape[0]
     place = jnp.stack([lax.axis_index("row"), lax.axis_index("layer") & 1]).astype(jnp.int32)
 
     answer0, part = first_level(targets, rhs_low, inv_low, blocks, rows)
-    right_side = turned_share(place, rhs_low, 1, share)
+    right_sides = turned_shares(rhs_low, 1, rows)
     shares = lax.all_to_all(part, "col", 0, 0, tiled=True)
     summed = shares.astype(F32).sum(axis=0).astype(BF16)
-    turn = [
-        (row * cols + col, col * cols + (row - 1) % rows)
-        for row in range(rows)
-        for col in range(cols)
+    hops = rows // 2
+    arrived = [
+        lax.ppermute(
+            summed,
+            ("row", "col"),
+            [
+                (row * cols + col, ((col // 2 + hop) % hops * 2 + col % 2) * cols + (row - 1) % rows)
+                for row in range(rows)
+                for col in range(cols)
+            ],
+        )
+        for hop in range(hops)
     ]
-    summed = lax.ppermute(summed, ("row", "col"), turn)
-    pieces, both = second_level(place, summed, right_side, inv_low, answer0, rows // 2)
-    lines = [list(range(core, rows, 2)) for core in range(2)]
+    solved = second_level(place, arrived, right_sides, inv_low)
     chips = [[row, row + 1] for row in range(0, rows, 2)]
-    pieces = lax.all_to_all(pieces, "row", 0, 0, axis_index_groups=lines, tiled=True)
-    answer1 = lax.all_gather(pieces, "row", axis=0, axis_index_groups=chips)
+    answer1 = lax.all_gather(solved, "row", axis=0, axis_index_groups=chips)
 
     half = count // 2
     near = [(layer, layer ^ 1) for layer in range(layers)]
@@ -256,7 +267,9 @@
         axis_index_groups=groups,
         tiled=True,
     )
-    solved = ancestor_solve(arrived, jnp.swapaxes(rhs_anc, 1, 2), inv_anc)
+    solved, both = ancestor_solve(
+        place, arrived, jnp.swapaxes(rhs_anc, 1, 2), inv_anc, answer0, answer1
+    )
     return (jnp.swapaxes(both, 1, 2)[None, :, None], jnp.swapaxes(solved, 1, 2))
 
 

time: 113 us -> 116 us (1.027)
  starting transfers between devices: 25.2 us -> 37.1 us
  blocking collectives: 47.2 us -> 42 us
  other arithmetic: 1.9 us -> 0.32 us
  Pallas kernels: 15 us -> 13.5 us
  local copies, waits for them, and re-layouts: 1.49 us -> 0.03 us
    all_to_all x1 -> x0, blocking collectives: 13.7 us -> none  [on_device(): lax.all_to_all(pieces, 'row', 0, 0, axis_index_groups=lines, tiled=True)]
    ppermute x1 -> x4, starting transfers between devices: 1.92 us -> 14.9 us  [on_device(): lax.ppermute(summed, ('row', 'col'), [(row * cols + col, ((col // 2 + hop...]
    all_to_all x1, blocking collectives: 31.4 us -> 39.9 us  [on_device(): lax.all_to_all(parts.reshape(members, parts.shape[0] // members, -1), ('l...]
    pallas_call x3, Pallas kernels: 5.65 us -> 4.01 us  [the longest x1 2.55 us: ancestor_solve(): pl.pallas_call(body, out_shape=(jax.ShapeDtypeStruct((count, loads, width...]
    unnamed x18 -> x14, local copies, waits for them, and re-layouts: 1.49 us -> 0.03 us
    ppermute x1 -> x4, waiting for transfers between devices: 3.04 us -> 3.27 us  [on_device(): lax.ppermute(summed, ('row', 'col'), [(row * cols + col, ((col // 2 + hop...]
  transfers between devices with their start and end apart: 4 -> 7, of which waited for: 3 -> 4; matrix products, arithmetic and copies ran while one was open for 1% -> 0% of each run, Pallas kernels for 4% -> 2%
where the time goes in v3:
time: 116 us; the launch traced here: 115 us
  blocking collectives  42 us (36%)
  starting transfers between devices  37.1 us (32%)
  waiting for transfers between devices  21.6 us (19%)
  Pallas kernels  13.5 us (12%)
    all_to_all x1, blocking collectives, on_device(): lax.all_to_all(parts.reshape(members, parts.shape[0] // members, -1), ('l...  39.9 us
    ppermute x4, starting transfers between devices, on_device(): lax.ppermute(summed, ('row', 'col'), [(row * cols + col, ((col // 2 + hop...  14.9 us
    all_to_all x1, waiting for transfers between devices, on_device(): shares = lax.all_to_all(part, 'col', 0, 0, tiled=True)  11.6 us
    all_to_all x1, starting transfers between devices, on_device(): shares = lax.all_to_all(part, 'col', 0, 0, tiled=True)  9.31 us
    ppermute x1, starting transfers between devices, on_device(): got_far = lax.ppermute(give_far, 'layer', far)  9.1 us
    ppermute x1, waiting for transfers between devices, on_device(): got_far = lax.ppermute(give_far, 'layer', far)  6.73 us
    pallas_call x3, Pallas kernels, ancestor_parts(): pl.pallas_call(body, out_shape=jax.ShapeDtypeStruct((loads, count * width...  5.45 us
    pallas_call x1, Pallas kernels, first_level(): pl.pallas_call(body, out_shape=(jax.ShapeDtypeStruct((2, rows // 2, share...  4.07 us
  transfers between devices with their start and end apart: 7, of which 4 were waited for; matrix products, arithmetic and copies ran while one was open for 0% of the time, Pallas kernels for 2%

profile of v3, /device:TPU:8, one launch (start us, length us, event | category | flops | bytes accessed | tf_op | source)
XLA Modules:
  0.0 115.3 jit_solution(10939543694513707089)
XLA Ops:
  0.6 0.0 copy-start.2
  0.6 4.1 %shard_map.77 = (bf16[2,4,64,384]{3,2,1,0:T(8,128)(2,1)}, bf16[8,64,384]{2,1,0:T(8,128)(2,1)}) custom-call(s32[2,4]{1,0:T(2,128)} %bitcast.32, bf16[2,384,512]{2,1,0:T(8,128)(2,1)} %bitcast.27, bf16[2,384,384]{2,1,0:T(8,128)(2,1)} %bitcast.29, bf16[2,4,384,384]{3,2,1,0:T(8,128)(2,1)} %bitcast.16), custom_call_target="tpu_custom_call" | custom-call | flops 301989888 | bytes 2200000 | tf_op jit(solution)/shard_map/pallas_call | solution.py:51
  4.7 0.0 copy-start.3
  4.7 9.3 %all-to-all-start = ((bf16[8,64,384]{2,1,0:T(8,128)(2,1)}), bf16[8,64,384]{2,1,0:T(8,128)(2,1)S(1)}, u32[]{:S(2)}, u32[]{:S(2)}) async-start(bf16[8,64,384]{2,1,0:T(8,128)(2,1)} %get-tuple-element.7), calls=%async_computation | async-start | bytes 786432 | tf_op jit(solution)/shard_map/all_to_all | solution.py:228
  14.0 11.6 %all-to-all-done = bf16[8,64,384]{2,1,0:T(8,128)(2,1)S(1)} async-done(((bf16[8,64,384]{2,1,0:T(8,128)(2,1)}), bf16[8,64,384]{2,1,0:T(8,128)(2,1)S(1)}, u32[]{:S(2)}, u32[]{:S(2)}) %all-to-all-start) | async-done | bytes 393248 | tf_op jit(solution)/shard_map/all_to_all | solution.py:228
  25.6 0.1 reduce_sum.12
  25.7 1.9 %collective-permute-start.3 = (bf16[64,384]{1,0:T(8,128)(2,1)S(1)}, bf16[64,384]{1,0:T(8,128)(2,1)S(1)}, u32[]{:S(2)}, u32[]{:S(2)}) collective-permute-start(bf16[64,384]{1,0:T(8,128)(2,1)S(1)} %reduce_sum.12), channel_id=1, source_target_pairs={{0,55},{1,63},{2,7},{3,15},{4,23},{5,31},{6,39},{7,47},{8,48},{9,5... | collective-permute-start | bytes 147464 | tf_op jit(solution)/shard_map/ppermute | solution.py:232
  27.6 4.4 %collective-permute-start.2 = (bf16[64,384]{1,0:T(8,128)(2,1)S(1)}, bf16[64,384]{1,0:T(8,128)(2,1)S(1)}, u32[]{:S(2)}, u32[]{:S(2)}) collective-permute-start(bf16[64,384]{1,0:T(8,128)(2,1)S(1)} %reduce_sum.12), channel_id=1, source_target_pairs={{0,39},{1,47},{2,55},{3,63},{4,7},{5,15},{6,23},{7,31},{8,32},{9,4... | collective-permute-start | bytes 147464 | tf_op jit(solution)/shard_map/ppermute | solution.py:232
  32.0 4.0 %collective-permute-start.1 = (bf16[64,384]{1,0:T(8,128)(2,1)S(1)}, bf16[64,384]{1,0:T(8,128)(2,1)S(1)}, u32[]{:S(2)}, u32[]{:S(2)}) collective-permute-start(bf16[64,384]{1,0:T(8,128)(2,1)S(1)} %reduce_sum.12), channel_id=1, source_target_pairs={{0,23},{1,31},{2,39},{3,47},{4,55},{5,63},{6,7},{7,15},{8,16},{9,2... | collective-permute-start | bytes 147464 | tf_op jit(solution)/shard_map/ppermute | solution.py:232
  36.0 4.6 %collective-permute-start = (bf16[64,384]{1,0:T(8,128)(2,1)S(1)}, bf16[64,384]{1,0:T(8,128)(2,1)S(1)}, u32[]{:S(2)}, u32[]{:S(2)}) collective-permute-start(bf16[64,384]{1,0:T(8,128)(2,1)S(1)} %reduce_sum.12), channel_id=1, source_target_pairs={{0,7},{1,15},{2,23},{3,31},{4,39},{5,47},{6,55},{7,63},{8,0},{9,8}... | collective-permute-start | bytes 147464 | tf_op jit(solution)/shard_map/ppermute | solution.py:232
  40.6 0.1 pad_add_fusion.place_ref
  40.7 0.0 copy-done.2
  40.7 0.0 copy-start
  40.7 0.0 copy-start.1
  40.7 0.0 copy-start.6
  40.7 0.4 shard_map.78.refs_4_
  41.1 0.0 collective-permute-done.3.refs_3_
  41.1 0.0 collective-permute-done.2.refs_2_
  41.1 1.0 collective-permute-done.1.refs_1_
  42.2 2.2 %collective-permute-done.refs_0_ = bf16[64,384]{1,0:T(8,128)(2,1)S(1)} collective-permute-done((bf16[64,384]{1,0:T(8,128)(2,1)S(1)}, bf16[64,384]{1,0:T(8,128)(2,1)S(1)}, u32[]{:S(2)}, u32[]{:S(2)}) %collective-permute-start) | collective-permute-done | bytes 49184 | tf_op jit(solution)/shard_map/ppermute | solution.py:232
  44.4 0.0 copy-done.3
  44.4 1.1 shard_map.79
  45.5 2.1 %all-gather = bf16[8,64,384]{2,1,0:T(8,128)(2,1)S(1)} all-gather(bf16[4,64,384]{2,1,0:T(8,128)(2,1)S(1)} %shard_map.79), channel_id=2, replica_groups={{0,8},{16,24},{32,40},{48,56},{1,9},{17,25},{33,41},{49,57},{2,10},{18,..., dimensions={0}, use_global_device_ids=true | all-gather | bytes 589824 | tf_op jit(solution)/shard_map/all_gather | solution.py:245
  47.6 0.0 copy-done
  47.6 0.0 copy-done.1
  47.6 0.0 copy-done.6
  47.6 1.5 %shard_map.82 = bf16[256,768]{1,0:T(8,128)(2,1)S(1)} custom-call(s32[2,4]{1,0:T(2,128)S(1)} %bitcast.33, s32[2]{0:T(128)S(1)} %pad_add_fusion.place_ref, bf16[2,4,64,384]{3,2,1,0:T(8,128)(2,1)S(1)} %copy-done.1, bf16[2,4,64,384]{3,2,1,0:T(8,128)(2,1)S(1)} %bitcast.23, bf16[2,4,384,384]{3,2,1,0:T(8,128)(2,1)S(1)} %bitcast.17, ...), custom_call_target="tpu_custom_call" | custom-call | flops 301989888 | bytes 5000000 | tf_op jit(solution)/shard_map/pallas_call | solution.py:158
  49.1 1.5 %shard_map.81 = bf16[256,768]{1,0:T(8,128)(2,1)S(1)} custom-call(s32[2,4]{1,0:T(2,128)S(1)} %bitcast.34, s32[2]{0:T(128)S(1)} %pad_add_fusion.place_ref, bf16[2,4,64,384]{3,2,1,0:T(8,128)(2,1)S(1)} %copy-done.1, bf16[2,4,64,384]{3,2,1,0:T(8,128)(2,1)S(1)} %bitcast.24, bf16[2,4,384,384]{3,2,1,0:T(8,128)(2,1)S(1)} %bitcast.19, ...), custom_call_target="tpu_custom_call" | custom-call | flops 301989888 | bytes 5000000 | tf_op jit(solution)/shard_map/pallas_call | solution.py:158
  50.6 3.7 %collective-permute-start.4 = (bf16[256,768]{1,0:T(8,128)(2,1)S(1)}, bf16[256,768]{1,0:T(8,128)(2,1)S(1)}, u32[]{:S(2)}, u32[]{:S(2)}) collective-permute-start(bf16[256,768]{1,0:T(8,128)(2,1)S(1)} %shard_map.81), channel_id=1, source_target_pairs={{0,64},{64,0},{128,192},{192,128},{256,320},{320,256},{384,448},{4... | collective-permute-start | bytes 1179656 | tf_op jit(solution)/shard_map/ppermute | solution.py:251
  54.3 9.1 %collective-permute-start.5 = (bf16[256,768]{1,0:T(8,128)(2,1)S(1)}, bf16[256,768]{1,0:T(8,128)(2,1)S(1)}, u32[]{:S(2)}, u32[]{:S(2)}) collective-permute-start(bf16[256,768]{1,0:T(8,128)(2,1)S(1)} %shard_map.82), channel_id=1, source_target_pairs={{0,448},{64,128},{128,64},{192,256},{256,192},{320,384},{384,320},... | collective-permute-start | bytes 1179656 | tf_op jit(solution)/shard_map/ppermute | solution.py:253
  63.4 2.4 %shard_map.80 = bf16[256,1536]{1,0:T(8,128)(2,1)S(1)} custom-call(s32[2,4]{1,0:T(2,128)S(1)} %bitcast.35, s32[2]{0:T(128)S(1)} %pad_add_fusion.place_ref, bf16[2,4,64,384]{3,2,1,0:T(8,128)(2,1)S(1)} %copy-done.1, bf16[2,4,64,384]{3,2,1,0:T(8,128)(2,1)S(1)} %bitcast.25, bf16[2,4,384,384]{3,2,1,0:T(8,128)(2,1)S(1)} %bitcast.21, ...), custom_call_target="tpu_custom_call" | custom-call | flops 603979776 | bytes 5000000 | tf_op jit(solution)/shard_map/pallas_call | solution.py:158
  65.9 0.0 copy-start.4
  65.9 0.0 copy-start.5
  65.9 0.0 collective-permute-done.4
  65.9 6.7 %collective-permute-done.5 = bf16[256,768]{1,0:T(8,128)(2,1)S(1)} collective-permute-done((bf16[256,768]{1,0:T(8,128)(2,1)S(1)}, bf16[256,768]{1,0:T(8,128)(2,1)S(1)}, u32[]{:S(2)}, u32[]{:S(2)}) %collective-permute-start.5) | collective-permute-done | bytes 393248 | tf_op jit(solution)/shard_map/ppermute | solution.py:253
  72.6 0.2 fusion
  72.8 39.9 %all_to_all.10.arrived_ref = bf16[32,8,1536]{2,1,0:T(8,128)(2,1)S(1)} all-to-all(bf16[32,8,1536]{2,1,0:T(8,128)(2,1)S(1)} %fusion), channel_id=1, replica_groups={{0,1,2,3,4,5,6,7,128,129,130,131,132,133,134,135,256,257,258,259,260,26..., dimensions={0} | all-to-all | bytes 1572864 | tf_op jit(solution)/shard_map/all_to_all | solution.py:262
  112.7 0.0 copy-done.4
  112.7 0.0 copy-done.5
  112.7 2.6 %shard_map.83 = (f32[4,8,384]{2,1,0:T(8,128)}, bf16[2,64,384]{2,1,0:T(8,128)(2,1)}) custom-call(s32[2]{0:T(128)S(1)} %pad_add_fusion.place_ref, bf16[32,8,1536]{2,1,0:T(8,128)(2,1)S(1)} %all_to_all.10.arrived_ref, bf16[4,8,384]{2,1,0:T(8,128)(2,1)S(1)} %bitcast.31, bf16[4,384,384]{2,1,0:T(8,128)(2,1)S(1)} %copy-done.4, ...), custom_call_target="tpu_custom_call" | custom-call | flops 9437184 | bytes 3000000 | tf_op jit(solution)/shard_map/pallas_call | solution.py:190
Async XLA Ops:
  0.6 40.1 %copy-start.2 = (bf16[1,2,1,384,512]{4,3,2,1,0:T(8,128)(2,1)S(1)}, bf16[1,2,1,384,512]{4,3,2,1,0:T(8,128)(2,1)}, u32[]{:S(2)}) copy-start(bf16[1,2,1,384,512]{4,3,2,1,0:T(8,128)(2,1)} %param.6) | copy-start | bytes 2359300
  4.7 39.7 %copy-start.3 = (bf16[1,2,1,384,384]{4,3,2,1,0:T(8,128)(2,1)S(1)}, bf16[1,2,1,384,384]{4,3,2,1,0:T(8,128)(2,1)}, u32[]{:S(2)}) copy-start(bf16[1,2,1,384,384]{4,3,2,1,0:T(8,128)(2,1)} %param.7) | copy-start | bytes 1769476
  4.7 20.9 %all-to-all-start = ((bf16[8,64,384]{2,1,0:T(8,128)(2,1)}), bf16[8,64,384]{2,1,0:T(8,128)(2,1)S(1)}, u32[]{:S(2)}, u32[]{:S(2)}) async-start(bf16[8,64,384]{2,1,0:T(8,128)(2,1)} %get-tuple-element.7), calls=%async_computation | async-start | bytes 786432 | tf_op jit(solution)/shard_map/all_to_all | solution.py:228
  25.7 15.4 %collective-permute-start.3 = (bf16[64,384]{1,0:T(8,128)(2,1)S(1)}, bf16[64,384]{1,0:T(8,128)(2,1)S(1)}, u32[]{:S(2)}, u32[]{:S(2)}) collective-permute-start(bf16[64,384]{1,0:T(8,128)(2,1)S(1)} %reduce_sum.12), channel_id=1, source_target_pairs={{0,55},{1,63},{2,7},{3,15},{4,23},{5,31},{6,39},{7,47},{8,48},{9,5... | collective-permute-start | bytes 147464 | tf_op jit(solution)/shard_map/ppermute | solution.py:232
  27.6 13.5 %collective-permute-start.2 = (bf16[64,384]{1,0:T(8,128)(2,1)S(1)}, bf16[64,384]{1,0:T(8,128)(2,1)S(1)}, u32[]{:S(2)}, u32[]{:S(2)}) collective-permute-start(bf16[64,384]{1,0:T(8,128)(2,1)S(1)} %reduce_sum.12), channel_id=1, source_target_pairs={{0,39},{1,47},{2,55},{3,63},{4,7},{5,15},{6,23},{7,31},{8,32},{9,4... | collective-permute-start | bytes 147464 | tf_op jit(solution)/shard_map/ppermute | solution.py:232
  32.0 10.1 %collective-permute-start.1 = (bf16[64,384]{1,0:T(8,128)(2,1)S(1)}, bf16[64,384]{1,0:T(8,128)(2,1)S(1)}, u32[]{:S(2)}, u32[]{:S(2)}) collective-permute-start(bf16[64,384]{1,0:T(8,128)(2,1)S(1)} %reduce_sum.12), channel_id=1, source_target_pairs={{0,23},{1,31},{2,39},{3,47},{4,55},{5,63},{6,7},{7,15},{8,16},{9,2... | collective-permute-start | bytes 147464 | tf_op jit(solution)/shard_map/ppermute | solution.py:232
  36.0 8.4 %collective-permute-start = (bf16[64,384]{1,0:T(8,128)(2,1)S(1)}, bf16[64,384]{1,0:T(8,128)(2,1)S(1)}, u32[]{:S(2)}, u32[]{:S(2)}) collective-permute-start(bf16[64,384]{1,0:T(8,128)(2,1)S(1)} %reduce_sum.12), channel_id=1, source_target_pairs={{0,7},{1,15},{2,23},{3,31},{4,39},{5,47},{6,55},{7,63},{8,0},{9,8}... | collective-permute-start | bytes 147464 | tf_op jit(solution)/shard_map/ppermute | solution.py:232
  40.7 6.9 %copy-start = (bf16[1,1,1,2,4,384,384]{6,5,4,3,2,1,0:T(8,128)(2,1)S(1)}, bf16[1,1,1,2,4,384,384]{6,5,4,3,2,1,0:T(8,128)(2,1)}, u32[]{:S(2)}) copy-start(bf16[1,1,1,2,4,384,384]{6,5,4,3,2,1,0:T(8,128)(2,1)} %param.8) | copy-start | bytes 7077892
  40.7 6.9 %copy-start.1 = (bf16[2,4,64,384]{3,2,1,0:T(8,128)(2,1)S(1)}, bf16[2,4,64,384]{3,2,1,0:T(8,128)(2,1)}, u32[]{:S(2)}) copy-start(bf16[2,4,64,384]{3,2,1,0:T(8,128)(2,1)} %get-tuple-element.6.answer0_ref) | copy-start | bytes 1179652
  40.7 6.9 %copy-start.6 = (s32[1,1,1,2,4]{4,3,2,1,0:T(2,128)S(1)}, s32[1,1,1,2,4]{4,3,2,1,0:T(2,128)}, u32[]{:S(2)}) copy-start(s32[1,1,1,2,4]{4,3,2,1,0:T(2,128)} %param.9) | copy-start | bytes 100
  50.6 15.3 %collective-permute-start.4 = (bf16[256,768]{1,0:T(8,128)(2,1)S(1)}, bf16[256,768]{1,0:T(8,128)(2,1)S(1)}, u32[]{:S(2)}, u32[]{:S(2)}) collective-permute-start(bf16[256,768]{1,0:T(8,128)(2,1)S(1)} %shard_map.81), channel_id=1, source_target_pairs={{0,64},{64,0},{128,192},{192,128},{256,320},{320,256},{384,448},{4... | collective-permute-start | bytes 1179656 | tf_op jit(solution)/shard_map/ppermute | solution.py:251
  54.3 18.3 %collective-permute-start.5 = (bf16[256,768]{1,0:T(8,128)(2,1)S(1)}, bf16[256,768]{1,0:T(8,128)(2,1)S(1)}, u32[]{:S(2)}, u32[]{:S(2)}) collective-permute-start(bf16[256,768]{1,0:T(8,128)(2,1)S(1)} %shard_map.82), channel_id=1, source_target_pairs={{0,448},{64,128},{128,64},{192,256},{256,192},{320,384},{384,320},... | collective-permute-start | bytes 1179656 | tf_op jit(solution)/shard_map/ppermute | solution.py:253
  65.9 46.8 %copy-start.4 = (bf16[4,384,384]{2,1,0:T(8,128)(2,1)S(1)}, bf16[4,384,384]{2,1,0:T(8,128)(2,1)}, u32[]{:S(2)}) copy-start(bf16[4,384,384]{2,1,0:T(8,128)(2,1)} %inv_ref.1) | copy-start | bytes 3538948
  65.9 46.8 %copy-start.5 = (bf16[4,384,8]{1,2,0:T(8,128)(2,1)S(1)}, bf16[4,384,8]{1,2,0:T(8,128)(2,1)}, u32[]{:S(2)}) copy-start(bf16[4,384,8]{1,2,0:T(8,128)(2,1)} %param.10) | copy-start | bytes 73732

commit v4 on v2

--- a/solution.py
+++ b/solution.py
@@ -7,6 +7,9 @@
 
 F32 = jnp.float32
 BF16 = jnp.bfloat16
+SMALL = 8 << 20
+LARGE = 24 << 20
+FIRST = 60 << 20
 NT = (((1,), (1,)), ((), ()))
 
 
@@ -24,16 +27,37 @@
 
 
 def first_level(targets, rhs_low, inv_low, blocks, rows):
-    _, width, loads = rhs_low.shape
+    levels, width, loads = rhs_low.shape
     per_row = blocks.shape[1]
     share = loads // rows
     steps = 2
     held = rows // steps
-
-    def body(targets_ref, rhs_ref, inv_ref, block_ref, answer_ref, part_ref):
+    half = rows // 2
+
+    def body(targets_ref, rhs_ref, inv_ref, block_ref, answer_ref, part_ref, give_ref):
+        step = pl.program_id(0)
+        kept = lax.axis_index("layer") % 2
         answer = jnp.dot(inv_ref[0], rhs_ref[0], preferred_element_type=F32).T.astype(BF16)
+        pieces = [answer[member * share : (member + 1) * share] for member in range(held)]
         for member in range(held):
-            answer_ref[member % 2, member // 2] = answer[member * share : (member + 1) * share]
+            answer_ref[member % 2, member // 2] = pieces[member]
+        for parity in range(2):
+
+            @pl.when(kept == 1 - parity)
+            def _(parity=parity):
+                for member in range(parity, held, 2):
+                    give_ref[step * (held // 2) + member // 2] = pieces[member]
+
+        @pl.when(step == 0)
+        def _():
+            row = lax.broadcasted_iota(jnp.int32, (share, width), 0)
+            table = jnp.zeros((share, width), F32)
+            for level in range(levels):
+                for member in range(per_row):
+                    value = targets_ref[level, member].astype(F32)
+                    table = jnp.where(row == level * per_row + member, value, table)
+            give_ref[half] = table.astype(BF16)
+
         _, found = slot_of(targets_ref, 0, 1, per_row)
 
         @pl.when(found == 1)
@@ -48,8 +72,9 @@
     return pl.pallas_call(
         body,
         out_shape=(
-            jax.ShapeDtypeStruct((2, rows // 2, share, width), BF16),
+            jax.ShapeDtypeStruct((2, half, share, width), BF16),
             jax.ShapeDtypeStruct((rows, share, width), BF16),
+            jax.ShapeDtypeStruct((half + 1, share, width), BF16),
         ),
         grid_spec=pltpu.PrefetchScalarGridSpec(
             num_scalar_prefetch=1,
@@ -64,9 +89,10 @@
             out_specs=(
                 pl.BlockSpec((2, held // 2, share, width), lambda i, t: (0, i, 0, 0)),
                 pl.BlockSpec((held, share, width), lambda i, t: (i, 0, 0)),
+                pl.BlockSpec((half + 1, share, width), lambda i, t: (0, 0, 0)),
             ),
         ),
-        compiler_params=pltpu.CompilerParams(vmem_limit_bytes=60 << 20),
+        compiler_params=pltpu.CompilerParams(vmem_limit_bytes=FIRST),
         cost_estimate=pl.CostEstimate(
             flops=4 * width * width * loads, bytes_accessed=2_200_000, transcendentals=0
         ),
@@ -98,6 +124,7 @@
             in_specs=[pl.BlockSpec((1, width, lanes), lambda i, p: (level, 0, p[0] // per_lanes))],
             out_specs=pl.BlockSpec((share, width), lambda i, p: (0, 0)),
         ),
+        compiler_params=pltpu.CompilerParams(vmem_limit_bytes=SMALL),
         cost_estimate=pl.CostEstimate(
             flops=width * width * 1000, bytes_accessed=2_000_000, transcendentals=0
         ),
@@ -135,51 +162,78 @@
                 pl.BlockSpec((2, share, width), lambda i, p: (0, 0, 0)),
             ),
         ),
-        compiler_params=pltpu.CompilerParams(vmem_limit_bytes=30 << 20),
+        compiler_params=pltpu.CompilerParams(vmem_limit_bytes=FIRST),
         cost_estimate=pl.CostEstimate(
             flops=2 * width * width * share, bytes_accessed=600_000, transcendentals=0
         ),
     )(place, part, right_side, inv_low, answer0)
 
 
-def ancestor_parts(targets, place, answer0, answer1, blocks, flip, first, count):
-    _, held, share, width = answer0.shape
-    per_row = blocks.shape[1]
+def ancestor_parts(targets, place, own, near, table, before=None):
+    _, count, width, _ = near[0][1].shape
+    held, share = table.shape[0] - 1, table.shape[1]
     loads = held * share
-
-    def body(targets_ref, place_ref, answer0_ref, answer1_ref, block0_ref, block1_ref, out_ref):
-        target = pl.program_id(0) + 2 + first
-        _, found0 = slot_of(targets_ref, 0, target, per_row)
-        _, found1 = slot_of(targets_ref, 1, target, per_row)
-        keep0 = jnp.where(found0 == 1, 1.0, 0.0).astype(F32)
-        keep1 = jnp.where(found1 == 1, 1.0, 0.0).astype(F32)
-        total = dot_nt(answer0_ref[0].reshape(loads, width), block0_ref[0, 0]) * keep0
-        total += dot_nt(answer1_ref[0].reshape(loads, width), block1_ref[0, 0]) * keep1
+    terms = len(own) + len(near)
+
+    def body(targets_ref, place_ref, *refs):
+        answers, blocks = refs[:terms], refs[terms : 2 * terms]
+        table_ref, out_ref = refs[2 * terms], refs[-1]
+        target = pl.program_id(0) + 2
+        total = None
+        for index in range(terms):
+            if index < len(own):
+                _, found = slot_of(targets_ref, own[index][0], target, count)
+                value = answers[index][0].reshape(loads, width)
+                product = dot_nt(value, blocks[index][0, 0])
+                product = product * jnp.where(found == 1, 1.0, 0.0).astype(F32)
+            else:
+                level = near[index - len(own)][0]
+                lists = table_ref[0].astype(F32)
+                block = jnp.zeros((width, width), BF16)
+                for member in range(count):
+                    named = lists[level * count + member :][:1] == target.astype(F32)
+                    block += blocks[index][0, member] * jnp.where(named, 1.0, 0.0).astype(BF16)
+                value = answers[index][:held].reshape(loads, width)
+                product = dot_nt(value, block)
+            total = product if total is None else total + product
+        if before is not None:
+            total += refs[2 * terms + 1][...].astype(F32)
         out_ref[...] = total.astype(BF16)
 
-    def answer_spec():
-        return pl.BlockSpec((1, held, share, width), lambda a, t, p: ((p[1] + flip) % 2, 0, 0, 0))
-
-    def block_spec(level):
+    def own_block(level):
         return pl.BlockSpec(
             (1, 1, width, width),
-            lambda a, t, p: (level, slot_of(t, level, a + 2 + first, per_row)[0], 0, 0),
+            lambda a, t, p: (level, slot_of(t, level, a + 2, count)[0], 0, 0),
         )
 
+    def near_block(level):
+        return pl.BlockSpec((1, count, width, width), lambda a, t, p: (level, 0, 0, 0))
+
+    def near_answer(answer):
+        return pl.BlockSpec(answer.shape, lambda a, t, p: (0, 0, 0))
+
+    out_spec = pl.BlockSpec((loads, width), lambda a, t, p: (0, a))
+    in_specs = [pl.BlockSpec((1, held, share, width), lambda a, t, p: (p[1], 0, 0, 0)) for _ in own]
+    in_specs += [near_answer(term[2]) for term in near]
+    in_specs += [own_block(term[0]) for term in own] + [near_block(term[0]) for term in near]
+    in_specs.append(pl.BlockSpec((1, share, width), lambda a, t, p: (held, 0, 0)))
+    operands = [term[2] for term in (*own, *near)] + [term[1] for term in (*own, *near)] + [table]
+    if before is not None:
+        in_specs.append(out_spec)
+        operands.append(before)
     return pl.pallas_call(
         body,
         out_shape=jax.ShapeDtypeStruct((loads, count * width), BF16),
         grid_spec=pltpu.PrefetchScalarGridSpec(
-            num_scalar_prefetch=2,
-            grid=(count,),
-            in_specs=[answer_spec(), answer_spec(), block_spec(0), block_spec(1)],
-            out_specs=pl.BlockSpec((loads, width), lambda a, t, p: (0, a)),
-        ),
-        compiler_params=pltpu.CompilerParams(vmem_limit_bytes=30 << 20),
-        cost_estimate=pl.CostEstimate(
-            flops=4 * count * width * width * loads, bytes_accessed=5_000_000, transcendentals=0
-        ),
-    )(targets, place, answer0, answer1, blocks, blocks)
+            num_scalar_prefetch=2, grid=(count,), in_specs=in_specs, out_specs=out_spec
+        ),
+        compiler_params=pltpu.CompilerParams(vmem_limit_bytes=LARGE),
+        cost_estimate=pl.CostEstimate(
+            flops=2 * terms * count * width * width * loads,
+            bytes_accessed=5_000_000,
+            transcendentals=0,
+        ),
+    )(targets, place, *operands)
 
 
 def ancestor_solve(arrived, rhs_anc, inv_anc):
@@ -201,7 +255,7 @@
             pl.BlockSpec((1, width, width), lambda a: (a, 0, 0)),
         ],
         out_specs=pl.BlockSpec((1, loads, width), lambda a: (a, 0, 0)),
-        compiler_params=pltpu.CompilerParams(vmem_limit_bytes=40 << 20),
+        compiler_params=pltpu.CompilerParams(vmem_limit_bytes=LARGE),
         cost_estimate=pl.CostEstimate(
             flops=2 * count * width * width * loads, bytes_accessed=3_000_000, transcendentals=0
         ),
@@ -213,13 +267,28 @@
     rhs_low, inv_low = rhs_low[0, :, 0], inv_low[0, :, 0]
     blocks, targets = blocks[0, 0, 0], targets[0, 0, 0]
     width, loads = rhs_low.shape[1:]
-    share = loads // rows
-    layers, count = lax.axis_size("layer"), inv_anc.shape[0]
+    layers, share = lax.axis_size("layer"), loads // rows
     place = jnp.stack([lax.axis_index("row"), lax.axis_index("layer") & 1]).astype(jnp.int32)
 
-    answer0, part = first_level(targets, rhs_low, inv_low, blocks, rows)
+    answer0, part, give0 = first_level(targets, rhs_low, inv_low, blocks, rows)
     right_side = turned_share(place, rhs_low, 1, share)
     shares = lax.all_to_all(part, "col", 0, 0, tiled=True)
+
+    def neighbour(layer, row):
+        ahead = (layer + row) % 2 == 0
+        return (layer + (1 if ahead else -1)) % layers
+
+    pairs = [
+        (layer * rows + row, neighbour(layer, row) * rows + row)
+        for layer in range(layers)
+        for row in range(rows)
+    ]
+
+    def swap(value):
+        return lax.ppermute(value, ("layer", "row"), pairs)
+
+    near_blocks, near_answer0 = swap(blocks), swap(give0)
+
     summed = shares.astype(F32).sum(axis=0).astype(BF16)
     turn = [
         (row * cols + col, col * cols + (row - 1) % rows)
@@ -233,16 +302,11 @@
     pieces = lax.all_to_all(pieces, "row", 0, 0, axis_index_groups=lines, tiled=True)
     answer1 = lax.all_gather(pieces, "row", axis=0, axis_index_groups=chips)
 
-    half = count // 2
-    near = [(layer, layer ^ 1) for layer in range(layers)]
-    far = [(layer, (layer + (1 if layer % 2 else -1)) % layers) for layer in range(layers)]
-    give_near = ancestor_parts(targets, place, answer0, answer1, blocks, 1, 0, half)
-    got_near = lax.ppermute(give_near, "layer", near)
-    give_far = ancestor_parts(targets, place, answer0, answer1, blocks, 1, half, count - half)
-    got_far = lax.ppermute(give_far, "layer", far)
-    kept = ancestor_parts(targets, place, answer0, answer1, blocks, 0, 0, count)
-    got = jnp.concatenate([got_near, got_far], axis=1)
-    parts = (kept.astype(F32) + got.astype(F32)).astype(BF16)
+    near_answer1 = swap(lax.dynamic_index_in_dim(answer1, 1 - place[1], 0, keepdims=False))
+    own = [(0, blocks, answer0), (1, blocks, answer1)]
+    parts = ancestor_parts(targets, place, own, [(0, near_blocks, near_answer0)], near_answer0)
+    late = [(1, near_blocks, near_answer1)]
+    parts = ancestor_parts(targets, place, [], late, near_answer0, parts)
     groups = [
         [layer * cols + col for layer in range(parity, layers, 2) for col in range(cols)]
         for parity in range(2)

time: 113 us -> 110 us (0.973)
  starting transfers between devices: 25.2 us -> 35 us
  waiting for transfers between devices: 20.7 us -> 11.7 us
  blocking collectives: 47.2 us -> 40.7 us
  Pallas kernels: 15 us -> 17 us
    all_to_all x1 -> x0, blocking collectives: 13.7 us -> none  [on_device(): lax.all_to_all(pieces, 'row', 0, 0, axis_index_groups=lines, tiled=True)]
    ppermute x2 -> x3, waiting for transfers between devices: 6.64 us -> 0.01 us  [swap(): return lax.ppermute(value, ('layer', 'row'), pairs)]
    all_to_all x0 -> x1, starting transfers between devices: none -> 5.88 us  [on_device(): lax.all_to_all(pieces, 'row', 0, 0, axis_index_groups=lines, tiled=True)]
    all_to_all x1, blocking collectives: 31.4 us -> 36.6 us  [on_device(): lax.all_to_all(parts.reshape(members, parts.shape[0] // members, -1), ('l...]
    ppermute x1, starting transfers between devices: 1.92 us -> 7 us  [on_device(): summed = lax.ppermute(summed, ('row', 'col'), turn)]
    pallas_call x3 -> x2, Pallas kernels: 5.44 us -> 7.62 us  [ancestor_parts(): pl.pallas_call(body, out_shape=jax.ShapeDtypeStruct((loads, count * width...]
    ppermute x1, waiting for transfers between devices: 3.04 us -> 0.88 us  [on_device(): summed = lax.ppermute(summed, ('row', 'col'), turn)]
    all_to_all x1, starting transfers between devices: 9.93 us -> 7.82 us  [on_device(): shares = lax.all_to_all(part, 'col', 0, 0, tiled=True)]
  transfers between devices with their start and end apart: 4 -> 6, of which waited for: 3 -> 3; matrix products, arithmetic and copies ran while one was open for 1% -> 2% of each run, Pallas kernels for 4% -> 11%
where the time goes in v4:
time: 110 us; the launch traced here: 109 us
  blocking collectives  40.7 us (37%)
  starting transfers between devices  35 us (32%)
  Pallas kernels  17 us (15%)
  waiting for transfers between devices  11.7 us (11%)
  local copies, waits for them, and re-layouts  1.89 us (2%)
  other arithmetic  1.76 us (2%)
    all_to_all x1, blocking collectives, on_device(): lax.all_to_all(parts.reshape(members, parts.shape[0] // members, -1), ('l...  36.6 us
    ppermute x3, starting transfers between devices, swap(): return lax.ppermute(value, ('layer', 'row'), pairs)  14.3 us
    all_to_all x1, waiting for transfers between devices, on_device(): shares = lax.all_to_all(part, 'col', 0, 0, tiled=True)  10.5 us
    all_to_all x1, starting transfers between devices, on_device(): shares = lax.all_to_all(part, 'col', 0, 0, tiled=True)  7.82 us
    pallas_call x2, Pallas kernels, ancestor_parts(): pl.pallas_call(body, out_shape=jax.ShapeDtypeStruct((loads, count * width...  7.62 us
    ppermute x1, starting transfers between devices, on_device(): summed = lax.ppermute(summed, ('row', 'col'), turn)  7 us
    all_to_all x1, starting transfers between devices, on_device(): lax.all_to_all(pieces, 'row', 0, 0, axis_index_groups=lines, tiled=True)  5.88 us
    pallas_call x1, Pallas kernels, first_level(): pl.pallas_call(body, out_shape=(jax.ShapeDtypeStruct((2, half, share, wid...  4.17 us
  transfers between devices with their start and end apart: 6, of which 3 were waited for; matrix products, arithmetic and copies ran while one was open for 2% of the time, Pallas kernels for 11%

profile of v4, /device:TPU:8, one launch (start us, length us, event | category | flops | bytes accessed | tf_op | source)
XLA Modules:
  0.0 108.9 jit_solution(14175200012575492662)
XLA Ops:
  0.6 4.3 %collective-permute-start.2 = (bf16[2,4,384,384]{3,2,1,0:T(8,128)(2,1)}, bf16[2,4,384,384]{3,2,1,0:T(8,128)(2,1)}, u32[]{:S(2)}, u32[]{:S(2)}) collective-permute-start(bf16[2,4,384,384]{3,2,1,0:T(8,128)(2,1)} %bitcast.17), channel_id=1, source_target_pairs={{0,64},{8,456},{16,80},{24,472},{32,96},{40,488},{48,112},{56,504}... | collective-permute-start | bytes 7077896 | tf_op jit(solution)/shard_map/ppermute | solution.py:288
  4.9 0.0 copy-start.1
  4.9 4.2 %shard_map.77 = (bf16[2,4,64,384]{3,2,1,0:T(8,128)(2,1)}, bf16[8,64,384]{2,1,0:T(8,128)(2,1)}, bf16[5,64,384]{2,1,0:T(8,128)(2,1)}) custom-call(s32[2,4]{1,0:T(2,128)} %bitcast.27, bf16[2,384,512]{2,1,0:T(8,128)(2,1)} %bitcast.22, bf16[2,384,384]{2,1,0:T(8,128)(2,1)} %bitcast.30, bf16[2,4,384,384]{3,2,1,0:T(8,128)(2,1)} %bitcast.18), custom_call_target="tpu_custom_call" | custom-call | flops 301989888 | bytes 2200000 | tf_op jit(solution)/shard_map/pallas_call | solution.py:72
  9.1 0.0 copy-start
  9.1 0.0 copy-start.2
  9.1 0.0 copy-start.6
  9.1 7.8 %all-to-all-start = ((bf16[8,64,384]{2,1,0:T(8,128)(2,1)}), bf16[8,64,384]{2,1,0:T(8,128)(2,1)}, u32[]{:S(2)}, u32[]{:S(2)}) async-start(bf16[8,64,384]{2,1,0:T(8,128)(2,1)} %get-tuple-element.7), calls=%async_computation | async-start | bytes 786432 | tf_op jit(solution)/shard_map/all_to_all | solution.py:275
  17.0 10.5 %all-to-all-done = bf16[8,64,384]{2,1,0:T(8,128)(2,1)} async-done(((bf16[8,64,384]{2,1,0:T(8,128)(2,1)}), bf16[8,64,384]{2,1,0:T(8,128)(2,1)}, u32[]{:S(2)}, u32[]{:S(2)}) %all-to-all-start) | async-done | bytes 393248 | tf_op jit(solution)/shard_map/all_to_all | solution.py:275
  27.5 1.7 %reduce_sum.12 = bf16[64,384]{1,0:T(8,128)(2,1)} reduce(bf16[8,64,384]{2,1,0:T(8,128)(2,1)} %all-to-all-done, bf16[]{:T(256)} %constant.18.clone.1), dimensions={0}, to_apply=%region_0.0 | reduce | flops 172032 | bytes 442370 | tf_op jit(solution)/shard_map/reduce_sum | solution.py:292
  29.2 7.0 %collective-permute-start = (bf16[64,384]{1,0:T(8,128)(2,1)}, bf16[64,384]{1,0:T(8,128)(2,1)S(1)}, u32[]{:S(2)}, u32[]{:S(2)}) collective-permute-start(bf16[64,384]{1,0:T(8,128)(2,1)} %reduce_sum.12), channel_id=1, source_target_pairs={{0,7},{1,15},{2,23},{3,31},{4,39},{5,47},{6,55},{7,63},{8,0},{9,8}... | collective-permute-start | bytes 147464 | tf_op jit(solution)/shard_map/ppermute | solution.py:298
  36.2 0.1 pad_add_fusion.place_ref
  36.3 0.0 copy-done.1
  36.3 0.0 copy-start.7
  36.3 0.7 shard_map.78.rhs_ref
  36.9 0.0 copy-start.4
  37.0 0.6 copy-done.4
  37.6 0.9 collective-permute-done.part_ref
  38.4 0.0 copy-start.9
  38.4 0.0 copy-done.7
  38.4 0.6 copy-done.9
  39.1 2.6 %shard_map.79 = (bf16[4,64,384]{2,1,0:T(8,128)(2,1)}, bf16[2,64,384]{2,1,0:T(8,128)(2,1)}) custom-call(s32[2]{0:T(128)} %copy-done.7, bf16[64,384]{1,0:T(8,128)(2,1)} %copy-done.9, bf16[64,384]{1,0:T(8,128)(2,1)} %copy-done.4, bf16[2,384,384]{2,1,0:T(8,128)(2,1)} %bitcast.31, bf16[2,4,64,384]{3,2,1,0:T(8,128)(2,1)} %get-tuple-element.8.answer0_ref.refs_0_), custom_call_target="tpu_custom_call" | custom-call | flops 18874368 | bytes 600000 | tf_op jit(solution)/shard_map/pallas_call | solution.py:145
  41.7 5.9 %all-to-all-start.1 = ((bf16[4,64,384]{2,1,0:T(8,128)(2,1)}), bf16[4,64,384]{2,1,0:T(8,128)(2,1)S(1)}, u32[]{:S(2)}, u32[]{:S(2)}) async-start(bf16[4,64,384]{2,1,0:T(8,128)(2,1)} %get-tuple-element.10), calls=%async_computation.1 | async-start | bytes 393216 | tf_op jit(solution)/shard_map/all_to_all | solution.py:302
  47.6 6.0 %collective-permute-start.3 = (bf16[5,64,384]{2,1,0:T(8,128)(2,1)}, bf16[5,64,384]{2,1,0:T(8,128)(2,1)S(1)}, u32[]{:S(2)}, u32[]{:S(2)}) collective-permute-start(bf16[5,64,384]{2,1,0:T(8,128)(2,1)} %get-tuple-element.11), channel_id=1, source_target_pairs={{0,64},{8,456},{16,80},{24,472},{32,96},{40,488},{48,112},{56,504}... | collective-permute-start | bytes 737288 | tf_op jit(solution)/shard_map/ppermute | solution.py:288
  53.6 0.3 all-to-all-done.1
  53.9 4.1 %all-gather = bf16[8,64,384]{2,1,0:T(8,128)(2,1)S(1)} all-gather(bf16[4,64,384]{2,1,0:T(8,128)(2,1)S(1)} %all-to-all-done.1), channel_id=2, replica_groups={{0,8},{16,24},{32,40},{48,56},{1,9},{17,25},{33,41},{49,57},{2,10},{18,..., dimensions={0}, use_global_device_ids=true | all-gather | bytes 589824 | tf_op jit(solution)/shard_map/all_gather | solution.py:303
  58.0 4.0 %collective-permute-start.1 = (bf16[4,64,384]{2,1,0:T(8,128)(2,1)S(1)}, bf16[4,64,384]{2,1,0:T(8,128)(2,1)S(1)}, u32[]{:S(2)}, u32[]{:S(2)}) collective-permute-start(bf16[4,64,384]{2,1,0:T(8,128)(2,1)S(1)} %dynamic-slice_bitcast_fusion), channel_id=1, source_target_pairs={{0,64},{8,456},{16,80},{24,472},{32,96},{40,488},{48,112},{56,504}... | collective-permute-start | bytes 589832 | tf_op jit(solution)/shard_map/ppermute | solution.py:288
  62.0 0.0 collective-permute-done.3.refs_2_.refs_6_
  62.0 0.0 collective-permute-done.2.refs_5_.refs_1_
  62.0 0.0 copy-done
  62.1 0.0 copy-done.2
  62.1 0.0 copy-done.6
  62.1 0.0 copy-start.8
  62.1 0.6 copy-done.8
  62.7 4.3 %shard_map.80.refs_3_ = bf16[256,1536]{1,0:T(8,128)(2,1)S(1)} custom-call(s32[2,4]{1,0:T(2,128)S(1)} %bitcast.28, s32[2]{0:T(128)S(1)} %copy-done.8, bf16[2,4,64,384]{3,2,1,0:T(8,128)(2,1)S(1)} %copy-done.2, bf16[2,4,64,384]{3,2,1,0:T(8,128)(2,1)S(1)} %bitcast.25, bf16[5,64,384]{2,1,0:T(8,128)(2,1)S(1)} %collective-permute-done.3.refs_2_.refs_6_, ...), custom_call_target="tpu_custom_call" | custom-call | flops 905969664 | bytes 5000000 | tf_op jit(solution)/shard_map/pallas_call | solution.py:224
  67.0 0.0 copy-start.3
  67.0 0.0 copy-start.5
  67.0 0.0 collective-permute-done.1.refs_0_
  67.0 3.4 %shard_map.81 = bf16[256,1536]{1,0:T(8,128)(2,1)S(1)} custom-call(s32[2,4]{1,0:T(2,128)S(1)} %bitcast.29, s32[2]{0:T(128)S(1)} %copy-done.8, bf16[4,64,384]{2,1,0:T(8,128)(2,1)S(1)} %collective-permute-done.1.refs_0_, bf16[2,4,384,384]{3,2,1,0:T(8,128)(2,1)} %collective-permute-done.2.refs_5_.refs_1_, ...), custom_call_target="tpu_custom_call" | custom-call | flops 301989888 | bytes 5000000 | tf_op jit(solution)/shard_map/pallas_call | solution.py:224
  70.4 36.6 %all_to_all.15.arrived_ref = bf16[32,8,1536]{2,1,0:T(8,128)(2,1)S(1)} all-to-all(bf16[32,8,1536]{2,1,0:T(8,128)(2,1)S(1)} %bitcast.21), channel_id=1, replica_groups={{0,1,2,3,4,5,6,7,128,129,130,131,132,133,134,135,256,257,258,259,260,26..., dimensions={0} | all-to-all | bytes 1572864 | tf_op jit(solution)/shard_map/all_to_all | solution.py:315
  106.9 0.0 copy-done.3
  106.9 0.0 copy-done.5
  106.9 2.0 %shard_map.82 = f32[4,8,384]{2,1,0:T(8,128)} custom-call(bf16[32,8,1536]{2,1,0:T(8,128)(2,1)S(1)} %all_to_all.15.arrived_ref, bf16[4,8,384]{2,1,0:T(8,128)(2,1)S(1)} %bitcast.26, bf16[4,384,384]{2,1,0:T(8,128)(2,1)S(1)} %copy-done.3), custom_call_target="tpu_custom_call" | custom-call | flops 9437184 | bytes 3000000 | tf_op jit(solution)/shard_map/pallas_call | solution.py:248
  (1 shorter events, 0.0 us)
Async XLA Ops:
  0.6 61.4 %collective-permute-start.2 = (bf16[2,4,384,384]{3,2,1,0:T(8,128)(2,1)}, bf16[2,4,384,384]{3,2,1,0:T(8,128)(2,1)}, u32[]{:S(2)}, u32[]{:S(2)}) collective-permute-start(bf16[2,4,384,384]{3,2,1,0:T(8,128)(2,1)} %bitcast.17), channel_id=1, source_target_pairs={{0,64},{8,456},{16,80},{24,472},{32,96},{40,488},{48,112},{56,504}... | collective-permute-start | bytes 7077896 | tf_op jit(solution)/shard_map/ppermute | solution.py:288
  4.9 31.4 %copy-start.1 = (bf16[1,2,1,384,512]{4,3,2,1,0:T(8,128)(2,1)S(1)}, bf16[1,2,1,384,512]{4,3,2,1,0:T(8,128)(2,1)}, u32[]{:S(2)}) copy-start(bf16[1,2,1,384,512]{4,3,2,1,0:T(8,128)(2,1)} %param.6) | copy-start | bytes 2359300
  9.1 52.9 %copy-start = (bf16[1,1,1,2,4,384,384]{6,5,4,3,2,1,0:T(8,128)(2,1)S(1)}, bf16[1,1,1,2,4,384,384]{6,5,4,3,2,1,0:T(8,128)(2,1)}, u32[]{:S(2)}) copy-start(bf16[1,1,1,2,4,384,384]{6,5,4,3,2,1,0:T(8,128)(2,1)} %param.8) | copy-start | bytes 7077892
  9.1 52.9 %copy-start.2 = (bf16[2,4,64,384]{3,2,1,0:T(8,128)(2,1)S(1)}, bf16[2,4,64,384]{3,2,1,0:T(8,128)(2,1)}, u32[]{:S(2)}) copy-start(bf16[2,4,64,384]{3,2,1,0:T(8,128)(2,1)} %get-tuple-element.8.answer0_ref.refs_0_) | copy-start | bytes 1179652
  9.1 52.9 %copy-start.6 = (s32[1,1,1,2,4]{4,3,2,1,0:T(2,128)S(1)}, s32[1,1,1,2,4]{4,3,2,1,0:T(2,128)}, u32[]{:S(2)}) copy-start(s32[1,1,1,2,4]{4,3,2,1,0:T(2,128)} %param.9) | copy-start | bytes 100
  9.1 18.4 %all-to-all-start = ((bf16[8,64,384]{2,1,0:T(8,128)(2,1)}), bf16[8,64,384]{2,1,0:T(8,128)(2,1)}, u32[]{:S(2)}, u32[]{:S(2)}) async-start(bf16[8,64,384]{2,1,0:T(8,128)(2,1)} %get-tuple-element.7), calls=%async_computation | async-start | bytes 786432 | tf_op jit(solution)/shard_map/all_to_all | solution.py:275
  29.2 9.2 %collective-permute-start = (bf16[64,384]{1,0:T(8,128)(2,1)}, bf16[64,384]{1,0:T(8,128)(2,1)S(1)}, u32[]{:S(2)}, u32[]{:S(2)}) collective-permute-start(bf16[64,384]{1,0:T(8,128)(2,1)} %reduce_sum.12), channel_id=1, source_target_pairs={{0,7},{1,15},{2,23},{3,31},{4,39},{5,47},{6,55},{7,63},{8,0},{9,8}... | collective-permute-start | bytes 147464 | tf_op jit(solution)/shard_map/ppermute | solution.py:298
  36.3 2.2 %copy-start.7 = (s32[2]{0:T(128)}, s32[2]{0:T(128)S(1)}, u32[]{:S(2)}) copy-start(s32[2]{0:T(128)S(1)} %pad_add_fusion.place_ref) | copy-start | bytes 28
  36.9 0.6 copy-start.4
  38.4 0.6 copy-start.9
  41.7 12.2 %all-to-all-start.1 = ((bf16[4,64,384]{2,1,0:T(8,128)(2,1)}), bf16[4,64,384]{2,1,0:T(8,128)(2,1)S(1)}, u32[]{:S(2)}, u32[]{:S(2)}) async-start(bf16[4,64,384]{2,1,0:T(8,128)(2,1)} %get-tuple-element.10), calls=%async_computation.1 | async-start | bytes 393216 | tf_op jit(solution)/shard_map/all_to_all | solution.py:302
  47.6 14.5 %collective-permute-start.3 = (bf16[5,64,384]{2,1,0:T(8,128)(2,1)}, bf16[5,64,384]{2,1,0:T(8,128)(2,1)S(1)}, u32[]{:S(2)}, u32[]{:S(2)}) collective-permute-start(bf16[5,64,384]{2,1,0:T(8,128)(2,1)} %get-tuple-element.11), channel_id=1, source_target_pairs={{0,64},{8,456},{16,80},{24,472},{32,96},{40,488},{48,112},{56,504}... | collective-permute-start | bytes 737288 | tf_op jit(solution)/shard_map/ppermute | solution.py:288
  58.0 9.0 %collective-permute-start.1 = (bf16[4,64,384]{2,1,0:T(8,128)(2,1)S(1)}, bf16[4,64,384]{2,1,0:T(8,128)(2,1)S(1)}, u32[]{:S(2)}, u32[]{:S(2)}) collective-permute-start(bf16[4,64,384]{2,1,0:T(8,128)(2,1)S(1)} %dynamic-slice_bitcast_fusion), channel_id=1, source_target_pairs={{0,64},{8,456},{16,80},{24,472},{32,96},{40,488},{48,112},{56,504}... | collective-permute-start | bytes 589832 | tf_op jit(solution)/shard_map/ppermute | solution.py:288
  62.1 0.6 copy-start.8
  67.0 40.0 %copy-start.3 = (bf16[4,384,384]{2,1,0:T(8,128)(2,1)S(1)}, bf16[4,384,384]{2,1,0:T(8,128)(2,1)}, u32[]{:S(2)}) copy-start(bf16[4,384,384]{2,1,0:T(8,128)(2,1)} %inv_ref.1) | copy-start | bytes 3538948
  67.0 40.0 %copy-start.5 = (bf16[4,384,8]{1,2,0:T(8,128)(2,1)S(1)}, bf16[4,384,8]{1,2,0:T(8,128)(2,1)}, u32[]{:S(2)}) copy-start(bf16[4,384,8]{1,2,0:T(8,128)(2,1)} %param.10) | copy-start | bytes 73732

commit v5 on v4

v5 whole, which is shorter than its diff:
```python
import jax
import jax.numpy as jnp
from jax import lax
from jax.experimental import pallas as pl
from jax.experimental.pallas import tpu as pltpu
from jax.sharding import PartitionSpec as P

F32 = jnp.float32
BF16 = jnp.bfloat16
SMALL = 8 << 20
LARGE = 24 << 20
FIRST = 60 << 20
NT = (((1,), (1,)), ((), ()))


def dot_nt(left, right):
    return lax.dot_general(left, right, NT, preferred_element_type=F32)


def slot_of(targets_ref, level, target, per_row):
    slot, found = jnp.int32(0), jnp.int32(0)
    for member in range(per_row):
        hit = targets_ref[level, member] == target
        slot = jnp.where(hit, jnp.int32(member), slot)
        found = jnp.where(hit, jnp.int32(1), found)
    return slot, found


def first_level(targets, rhs_low, inv_low, blocks, rows):
    levels, width, loads = rhs_low.shape
    per_row = blocks.shape[1]
    share = loads // rows
    steps = 2
    held, half = rows // steps, rows // 2
    slots = levels * per_row

    def body(
        targets_ref, rhs_ref, inv_ref, blocks_ref, answer_ref, part_ref, give_ref,
        rhs_in, inv_in, block_in, zeros, half_out, in_sems, out_sems,
    ):
        kept = lax.axis_index("layer") % 2
        slot, found = slot_of(targets_ref, 0, 1, per_row)
        inv_copy = pltpu.make_async_copy(inv_ref.at[0], inv_in, in_sems.at[steps])
        block_copy = pltpu.make_async_copy(blocks_ref.at[0, slot], block_in, in_sems.at[steps + 1])
        rhs_copies = [
            pltpu.make_async_copy(
                rhs_ref.at[0, :, pl.ds(step * (loads // steps), loads // steps)],
                rhs_in.at[step],
                in_sems.at[step],
            )
            for step in range(steps)
        ]
        inv_copy.start()
        for copy in rhs_copies:
            copy.start()
        block_copy.start()
        zeros[...] = jnp.zeros_like(zeros)

        def give(index):
            return give_ref.at[pl.ds(index * width, width)]

        for index in range(slots):
            level, ancestor = index // per_row, index % per_row
            source, named = slot_of(targets_ref, level, ancestor + 2, per_row)

            @pl.when(named == 1)
            def _(index=index, level=level, source=source):
                pltpu.make_async_copy(
                    blocks_ref.at[level, source], give(index), out_sems.at[index]
                ).start()

            @pl.when(named == 0)
            def _(index=index):
                pltpu.make_async_copy(zeros, give(index), out_sems.at[index]).start()

        inv_copy.wait()
        answers = []
        for step in range(steps):
            rhs_copies[step].wait()
            answer = jnp.dot(inv_in[...], rhs_in[step], preferred_element_type=F32).T.astype(BF16)
            answers.append(answer)
            pieces = [answer[member * share : (member + 1) * share] for member in range(held)]
            for member in range(held):
                answer_ref[member % 2, step * (held // 2) + member // 2] = pieces[member]
            for member in range(0, held, 2):
                start = (step * (held // 2) + member // 2) * share

                @pl.when(kept == 1)
                def _(start=start, piece=pieces[member]):
                    half_out[start : start + share] = piece

                @pl.when(kept == 0)
                def _(start=start, piece=pieces[member + 1]):
                    half_out[start : start + share] = piece

        half_copy = pltpu.make_async_copy(
            half_out, give_ref.at[pl.ds(slots * width, half * share)], out_sems.at[slots]
        )
        half_copy.start()
        block_copy.wait()

        @pl.when(found == 1)
        def _():
            for step in range(steps):
                part = dot_nt(answers[step], block_in[...]).astype(BF16)
                part_ref[step * held : (step + 1) * held] = part.reshape(held, share, width)

        @pl.when(found == 0)
        def _():
            part_ref[...] = jnp.zeros_like(part_ref)

        for index in range(slots):
            pltpu.make_async_copy(zeros, give(index), out_sems.at[index]).wait()
        half_copy.wait()

    any_spec, vmem = pl.BlockSpec(memory_space=pl.ANY), pl.BlockSpec(memory_space=pltpu.VMEM)
    return pl.pallas_call(
        body,
        out_shape=(
            jax.ShapeDtypeStruct((2, half, share, width), BF16),
            jax.ShapeDtypeStruct((rows, share, width), BF16),
            jax.ShapeDtypeStruct((slots * width + half * share, width), BF16),
        ),
        in_specs=[pl.BlockSpec(memory_space=pltpu.SMEM), any_spec, any_spec, any_spec],
        out_specs=(vmem, vmem, any_spec),
        scratch_shapes=[
            pltpu.VMEM((steps, width, loads // steps), BF16),
            pltpu.VMEM((width, width), BF16),
            pltpu.VMEM((width, width), BF16),
            pltpu.VMEM((width, width), BF16),
            pltpu.VMEM((half * share, width), BF16),
            pltpu.SemaphoreType.DMA((steps + 2,)),
            pltpu.SemaphoreType.DMA((slots + 1,)),
        ],
        compiler_params=pltpu.CompilerParams(vmem_limit_bytes=FIRST),
        cost_estimate=pl.CostEstimate(
            flops=4 * width * width * loads, bytes_accessed=2_200_000, transcendentals=0
        ),
    )(targets, rhs_low, inv_low, blocks)


def prepared(place, rhs_low, inv_low, answer0, level):
    _, held, share, width = answer0.shape
    lanes = max(share, 128)
    per_lanes = lanes // share

    def body(place_ref, rhs_ref, inv_ref, answer0_ref, out_ref, inverse_ref, first_ref):
        turned = rhs_ref[0].astype(F32).T
        picked = turned[:share]
        for other in range(1, per_lanes):
            picked = jnp.where(
                place_ref[0] % per_lanes == other,
                turned[other * share : (other + 1) * share],
                picked,
            )
        out_ref[...] = picked.astype(BF16)
        inverse_ref[...] = inv_ref[0]
        first_ref[...] = answer0_ref[0, 0]

    return pl.pallas_call(
        body,
        out_shape=(
            jax.ShapeDtypeStruct((share, width), BF16),
            jax.ShapeDtypeStruct((width, width), BF16),
            jax.ShapeDtypeStruct((share, width), BF16),
        ),
        grid_spec=pltpu.PrefetchScalarGridSpec(
            num_scalar_prefetch=1,
            grid=(1,),
            in_specs=[
                pl.BlockSpec((1, width, lanes), lambda i, p: (level, 0, p[0] // per_lanes)),
                pl.BlockSpec((1, width, width), lambda i, p: (level, 0, 0)),
                pl.BlockSpec((1, 1, share, width), lambda i, p: (p[0] % 2, p[0] // 2, 0, 0)),
            ],
            out_specs=(
                pl.BlockSpec((share, width), lambda i, p: (0, 0)),
                pl.BlockSpec((width, width), lambda i, p: (0, 0)),
                pl.BlockSpec((share, width), lambda i, p: (0, 0)),
            ),
        ),
        compiler_params=pltpu.CompilerParams(vmem_limit_bytes=SMALL),
        cost_estimate=pl.CostEstimate(
            flops=width * width * 1000, bytes_accessed=2_000_000, transcendentals=0
        ),
    )(place, rhs_low, inv_low, answer0)


def second_level(part, right_side, inverse, first, copies):
    share, width = part.shape

    def body(part_ref, rhs_ref, inv_ref, first_ref, answer_ref, both_ref):
        residual = (rhs_ref[...].astype(F32) - part_ref[...].astype(F32)).astype(BF16)
        answer = dot_nt(residual, inv_ref[...]).astype(BF16)
        for copy in range(copies):
            answer_ref[copy] = answer
        both_ref[0] = first_ref[...]
        both_ref[1] = answer

    return pl.pallas_call(
        body,
        out_shape=(
            jax.ShapeDtypeStruct((copies, share, width), BF16),
            jax.ShapeDtypeStruct((2, share, width), BF16),
        ),
        compiler_params=pltpu.CompilerParams(vmem_limit_bytes=SMALL),
        cost_estimate=pl.CostEstimate(
            flops=2 * width * width * share, bytes_accessed=600_000, transcendentals=0
        ),
    )(part, right_side, inverse, first)


def ancestor_parts(targets, place, own, near, before=None):
    loads, width = near[0][4], near[0][1].shape[-1]
    count = near[0][5]
    terms = len(own) + len(near)

    def body(targets_ref, place_ref, *refs):
        answers, blocks, rest = refs[:terms], refs[terms : 2 * terms], refs[2 * terms :]
        total = None
        for index in range(terms):
            if index < len(own):
                _, found = slot_of(targets_ref, own[index][0], pl.program_id(0) + 2, count)
                value = answers[index][0].reshape(loads, width)
                product = dot_nt(value, blocks[index][0, 0])
                product = product * jnp.where(found == 1, 1.0, 0.0).astype(F32)
            else:
                product = dot_nt(answers[index][...], blocks[index][...])
            total = product if total is None else total + product
        if before is not None:
            total += rest[0][...].astype(F32)
        rest[-1][...] = total.astype(BF16)

    def own_answer(answer):
        return pl.BlockSpec((1, *answer.shape[1:]), lambda a, t, p: (p[1], 0, 0, 0))

    def own_block(level):
        return pl.BlockSpec(
            (1, 1, width, width),
            lambda a, t, p: (level, slot_of(t, level, a + 2, count)[0], 0, 0),
        )

    def near_answer(spot):
        return pl.BlockSpec((loads, width), lambda a, t, p: (spot, 0))

    def near_block(level):
        return pl.BlockSpec((width, width), lambda a, t, p: (level * count + a, 0))

    out_spec = pl.BlockSpec((loads, width), lambda a, t, p: (0, a))
    in_specs = [own_answer(term[2]) for term in own] + [near_answer(term[3]) for term in near]
    in_specs += [own_block(term[0]) for term in own] + [near_block(term[0]) for term in near]
    operands = [term[2] for term in (*own, *near)] + [term[1] for term in (*own, *near)]
    if before is not None:
        in_specs.append(out_spec)
        operands.append(before)
    return pl.pallas_call(
        body,
        out_shape=jax.ShapeDtypeStruct((loads, count * width), BF16),
        grid_spec=pltpu.PrefetchScalarGridSpec(
            num_scalar_prefetch=2, grid=(count,), in_specs=in_specs, out_specs=out_spec
        ),
        compiler_params=pltpu.CompilerParams(vmem_limit_bytes=LARGE),
        cost_estimate=pl.CostEstimate(
            flops=2 * terms * count * width * width * loads,
            bytes_accessed=5_000_000,
            transcendentals=0,
        ),
    )(targets, place, *operands)


def ancestor_solve(arrived, rhs_anc, inv_anc):
    sources, loads, _ = arrived.shape
    count, _, width = rhs_anc.shape

    def body(arrived_ref, rhs_ref, inv_ref, out_ref):
        total = jnp.sum(arrived_ref[...].astype(F32), axis=0)
        residual = (rhs_ref[0].astype(F32) - total).astype(BF16)
        out_ref[0] = dot_nt(residual, inv_ref[0])

    return pl.pallas_call(
        body,
        out_shape=jax.ShapeDtypeStruct((count, loads, width), F32),
        grid=(count,),
        in_specs=[
            pl.BlockSpec((sources, loads, width), lambda a: (0, 0, a)),
            pl.BlockSpec((1, loads, width), lambda a: (a, 0, 0)),
            pl.BlockSpec((1, width, width), lambda a: (a, 0, 0)),
        ],
        out_specs=pl.BlockSpec((1, loads, width), lambda a: (a, 0, 0)),
        compiler_params=pltpu.CompilerParams(vmem_limit_bytes=LARGE),
        cost_estimate=pl.CostEstimate(
            flops=2 * count * width * width * loads, bytes_accessed=3_000_000, transcendentals=0
        ),
    )(arrived, rhs_anc, inv_anc)


def on_device(rhs_low, inv_low, blocks, targets, rhs_anc, inv_anc):
    rows, cols = lax.axis_size("row"), lax.axis_size("col")
    rhs_low, inv_low = rhs_low[0, :, 0], inv_low[0, :, 0]
    blocks, targets = blocks[0, 0, 0], targets[0, 0, 0]
    width, loads = rhs_low.shape[1:]
    layers = lax.axis_size("layer")
    place = jnp.stack([lax.axis_index("row"), lax.axis_index("layer") & 1]).astype(jnp.int32)

    answer0, part, give = first_level(targets, rhs_low, inv_low, blocks, rows)
    ready = prepared(place, rhs_low, inv_low, answer0, 1)
    shares = lax.all_to_all(part, "col", 0, 0, tiled=True)

    def neighbour(layer, row):
        ahead = (layer + row) % 2 == 0
        return (layer + (1 if ahead else -1)) % layers

    pairs = [
        (layer * rows + row, neighbour(layer, row) * rows + row)
        for layer in range(layers)
        for row in range(rows)
    ]

    def swap(value):
        return lax.ppermute(value, ("layer", "row"), pairs)

    near = swap(give)

    summed = shares.astype(F32).sum(axis=0).astype(BF16)
    turn = [
        (row * cols + col, col * cols + (row - 1) % rows)
        for row in range(rows)
        for col in range(cols)
    ]
    summed = lax.ppermute(summed, ("row", "col"), turn)
    pieces, both = second_level(summed, *ready, rows // 2)
    lines = [list(range(core, rows, 2)) for core in range(2)]
    chips = [[row, row + 1] for row in range(0, rows, 2)]
    pieces = lax.all_to_all(pieces, "row", 0, 0, axis_index_groups=lines, tiled=True)
    answer1 = lax.all_gather(pieces, "row", axis=0, axis_index_groups=chips)

    near_answer1 = swap(lax.dynamic_index_in_dim(answer1, 1 - place[1], 0, keepdims=False))
    wanted, count = loads // 2, inv_anc.shape[0]
    near_answer1 = near_answer1.reshape(wanted, width)
    own = [(0, blocks, answer0), (1, blocks, answer1)]
    early = (0, near, near, near.shape[0] // wanted - 1, wanted, count)
    late = (1, near, near_answer1, 0, wanted, count)
    parts = ancestor_parts(targets, place, own, [early])
    parts = ancestor_parts(targets, place, [], [late], parts)
    groups = [
        [layer * cols + col for layer in range(parity, layers, 2) for col in range(cols)]
        for parity in range(2)
    ]
    members = len(groups[0])
    arrived = lax.all_to_all(
        parts.reshape(members, parts.shape[0] // members, -1),
        ("layer", "col"),
        0,
        0,
        axis_index_groups=groups,
        tiled=True,
    )
    solved = ancestor_solve(arrived, jnp.swapaxes(rhs_anc, 1, 2), inv_anc)
    return (jnp.swapaxes(both, 1, 2)[None, :, None], jnp.swapaxes(solved, 1, 2))


def solution(mesh):
    in_specs = (
        P("layer", None, "col", None, None),
        P("layer", None, "col", None, None),
        P("layer", "row", "col", None, None, None, None),
        P("layer", "row", "col", None, None),
        P("row", None, ("layer", "col")),
        P("row", None, None),
    )
    out_specs = (P("layer", None, "col", None, "row"), P("row", None, ("layer", "col")))
    return jax.shard_map(
        on_device, mesh=mesh, in_specs=in_specs, out_specs=out_specs, check_vma=False
    )
```

time: 110 us -> 174 us (1.58)
  Pallas kernels: 17 us -> 82.9 us
  starting transfers between devices: 35 us -> 25.5 us
  waiting for transfers between devices: 11.7 us -> 16.9 us
  local copies, waits for them, and re-layouts: 1.89 us -> 4.76 us
    pallas_call x1, Pallas kernels: 4.17 us -> 74.4 us  [first_level(): pl.pallas_call(body, out_shape=(jax.ShapeDtypeStruct((2, half, share, wid...]
    ppermute x3 -> x2, starting transfers between devices: 14.3 us -> 3.84 us  [swap(): return lax.ppermute(value, ('layer', 'row'), pairs)]
    all_to_all x1, waiting for transfers between devices: 0.3 us -> 6.33 us  [on_device(): lax.all_to_all(pieces, 'row', 0, 0, axis_index_groups=lines, tiled=True)]
    unnamed x20 -> x16, local copies, waits for them, and re-layouts: 1.87 us -> 4.74 us
    pallas_call x2, Pallas kernels: 7.62 us -> 4.9 us  [ancestor_parts(): pl.pallas_call(body, out_shape=jax.ShapeDtypeStruct((loads, count * width...]
    ppermute x1, starting transfers between devices: 7 us -> 9.05 us  [on_device(): summed = lax.ppermute(summed, ('row', 'col'), turn)]
  transfers between devices with their start and end apart: 6 -> 5, of which waited for: 3 -> 2; matrix products, arithmetic and copies ran while one was open for 2% -> 1% of each run, Pallas kernels for 11% -> 3%
where the time goes in v5:
time: 174 us
  Pallas kernels  82.9 us (48%)
  blocking collectives  41.7 us (24%)
  starting transfers between devices  25.5 us (15%)
  waiting for transfers between devices  16.9 us (10%)
  local copies, waits for them, and re-layouts  4.76 us (3%)
    pallas_call x1, Pallas kernels, first_level(): pl.pallas_call(body, out_shape=(jax.ShapeDtypeStruct((2, half, share, wid...  74.4 us
    all_to_all x1, blocking collectives, on_device(): lax.all_to_all(parts.reshape(members, parts.shape[0] // members, -1), ('l...  38 us
    all_to_all x1, waiting for transfers between devices, on_device(): shares = lax.all_to_all(part, 'col', 0, 0, tiled=True)  10.5 us
    ppermute x1, starting transfers between devices, on_device(): summed = lax.ppermute(summed, ('row', 'col'), turn)  9.05 us
    all_to_all x1, starting transfers between devices, on_device(): shares = lax.all_to_all(part, 'col', 0, 0, tiled=True)  6.68 us
    all_to_all x1, waiting for transfers between devices, on_device(): lax.all_to_all(pieces, 'row', 0, 0, axis_index_groups=lines, tiled=True)  6.33 us
    all_to_all x1, starting transfers between devices, on_device(): lax.all_to_all(pieces, 'row', 0, 0, axis_index_groups=lines, tiled=True)  5.89 us
    pallas_call x2, Pallas kernels, ancestor_parts(): pl.pallas_call(body, out_shape=jax.ShapeDtypeStruct((loads, count * width...  4.9 us
  transfers between devices with their start and end apart: 5, of which 2 were waited for; matrix products, arithmetic and copies ran while one was open for 1% of the time, Pallas kernels for 3%

profile of v5, /device:TPU:8, one launch (start us, length us, event | category | flops | bytes accessed | tf_op | source)
XLA Modules:
  0.0 173.6 jit_solution(10402687884978662805)
XLA Ops:
  0.6 0.0 copy-start.1
  0.6 74.4 %shard_map.77 = (bf16[2,4,64,384]{3,2,1,0:T(8,128)(2,1)}, bf16[8,64,384]{2,1,0:T(8,128)(2,1)}, bf16[3328,384]{1,0:T(8,128)(2,1)}) custom-call(s32[2,4]{1,0:T(2,128)} %bitcast.30, bf16[2,384,512]{2,1,0:T(8,128)(2,1)} %bitcast.22, bf16[2,384,384]{2,1,0:T(8,128)(2,1)} %bitcast.26, bf16[2,4,384,384]{3,2,1,0:T(8,128)(2,1)} %bitcast.18), custom_call_target="tpu_custom_call" | custom-call | flops 301989888 | bytes 2200000 | tf_op jit(solution)/shard_map/pallas_call | solution.py:117
  75.1 0.0 copy-start.7
  75.1 1.9 %collective-permute-start.2 = (bf16[3328,384]{1,0:T(8,128)(2,1)}, bf16[3328,384]{1,0:T(8,128)(2,1)S(1)}, u32[]{:S(2)}, u32[]{:S(2)}) collective-permute-start(bf16[3328,384]{1,0:T(8,128)(2,1)} %get-tuple-element.17), channel_id=1, source_target_pairs={{0,64},{8,456},{16,80},{24,472},{32,96},{40,488},{48,112},{56,504}... | collective-permute-start | bytes 7667720 | tf_op jit(solution)/shard_map/ppermute | solution.py:319
  77.0 6.7 %all-to-all-start = ((bf16[8,64,384]{2,1,0:T(8,128)(2,1)}), bf16[8,64,384]{2,1,0:T(8,128)(2,1)}, u32[]{:S(2)}, u32[]{:S(2)}) async-start(bf16[8,64,384]{2,1,0:T(8,128)(2,1)} %get-tuple-element.10), calls=%async_computation | async-start | bytes 786432 | tf_op jit(solution)/shard_map/all_to_all | solution.py:306
  83.7 10.5 %all-to-all-done = bf16[8,64,384]{2,1,0:T(8,128)(2,1)} async-done(((bf16[8,64,384]{2,1,0:T(8,128)(2,1)}), bf16[8,64,384]{2,1,0:T(8,128)(2,1)}, u32[]{:S(2)}, u32[]{:S(2)}) %all-to-all-start) | async-done | bytes 393248 | tf_op jit(solution)/shard_map/all_to_all | solution.py:306
  94.2 1.1 reduce_sum.12
  95.3 9.1 %collective-permute-start = (bf16[64,384]{1,0:T(8,128)(2,1)S(1)}, bf16[64,384]{1,0:T(8,128)(2,1)S(1)}, u32[]{:S(2)}, u32[]{:S(2)}) collective-permute-start(bf16[64,384]{1,0:T(8,128)(2,1)S(1)} %reduce_sum.12), channel_id=1, source_target_pairs={{0,7},{1,15},{2,23},{3,31},{4,39},{5,47},{6,55},{7,63},{8,0},{9,8}... | collective-permute-start | bytes 147464 | tf_op jit(solution)/shard_map/ppermute | solution.py:329
  104.4 0.1 pad_add_fusion.place_ref
  104.4 0.0 copy-done.1
  104.4 0.0 copy-start.2
  104.4 1.1 copy-done.2
  105.5 0.0 copy-start.3
  105.5 1.0 copy-done.3
  106.5 0.7 shard_map.78
  107.2 0.0 collective-permute-done.part_ref
  107.2 0.9 shard_map.79
  108.1 5.9 %all-to-all-start.1 = ((bf16[4,64,384]{2,1,0:T(8,128)(2,1)}), bf16[4,64,384]{2,1,0:T(8,128)(2,1)S(1)}, u32[]{:S(2)}, u32[]{:S(2)}) async-start(bf16[4,64,384]{2,1,0:T(8,128)(2,1)} %get-tuple-element.16), calls=%async_computation.1 | async-start | bytes 393216 | tf_op jit(solution)/shard_map/all_to_all | solution.py:333
  114.0 6.3 %all-to-all-done.1 = bf16[4,64,384]{2,1,0:T(8,128)(2,1)S(1)} async-done(((bf16[4,64,384]{2,1,0:T(8,128)(2,1)}), bf16[4,64,384]{2,1,0:T(8,128)(2,1)S(1)}, u32[]{:S(2)}, u32[]{:S(2)}) %all-to-all-start.1) | async-done | bytes 196640 | tf_op jit(solution)/shard_map/all_to_all | solution.py:333
  120.4 3.7 %all-gather = bf16[8,64,384]{2,1,0:T(8,128)(2,1)S(1)} all-gather(bf16[4,64,384]{2,1,0:T(8,128)(2,1)S(1)} %all-to-all-done.1), channel_id=2, replica_groups={{0,8},{16,24},{32,40},{48,56},{1,9},{17,25},{33,41},{49,57},{2,10},{18,..., dimensions={0}, use_global_device_ids=true | all-gather | bytes 589824 | tf_op jit(solution)/shard_map/all_gather | solution.py:334
  124.1 1.9 %collective-permute-start.1 = (bf16[4,64,384]{2,1,0:T(8,128)(2,1)S(1)}, bf16[4,64,384]{2,1,0:T(8,128)(2,1)S(1)}, u32[]{:S(2)}, u32[]{:S(2)}) collective-permute-start(bf16[4,64,384]{2,1,0:T(8,128)(2,1)S(1)} %dynamic-slice_bitcast_fusion), channel_id=1, source_target_pairs={{0,64},{8,456},{16,80},{24,472},{32,96},{40,488},{48,112},{56,504}... | collective-permute-start | bytes 589832 | tf_op jit(solution)/shard_map/ppermute | solution.py:319
  126.0 0.0 collective-permute-done.2.refs_2_.refs_5_.refs_1_
  126.0 0.0 copy-done.7
  126.0 0.0 copy-start
  126.0 1.7 copy-done
  127.7 0.0 copy-start.4
  127.7 1.0 copy-done.4
  128.7 2.9 %shard_map.80.refs_2_ = bf16[256,1536]{1,0:T(8,128)(2,1)S(1)} custom-call(s32[2,4]{1,0:T(2,128)S(1)} %bitcast.31, s32[2]{0:T(128)S(1)} %pad_add_fusion.place_ref, bf16[2,4,64,384]{3,2,1,0:T(8,128)(2,1)S(1)} %copy-done.4, bf16[2,4,64,384]{3,2,1,0:T(8,128)(2,1)S(1)} %bitcast.25, bf16[3328,384]{1,0:T(8,128)(2,1)S(1)} %collective-permute-done.2.refs_2_.refs_5_.refs_1_, ...), custom_call_target="tpu_custom_call" | custom-call | flops 905969664 | bytes 5000000 | tf_op jit(solution)/shard_map/pallas_call | solution.py:255
  131.6 0.0 collective-permute-done.1
  131.6 0.0 copy-start.5
  131.7 0.0 copy-start.6
  131.7 2.0 %shard_map.81 = bf16[256,1536]{1,0:T(8,128)(2,1)S(1)} custom-call(s32[2,4]{1,0:T(2,128)S(1)} %bitcast.32, s32[2]{0:T(128)S(1)} %pad_add_fusion.place_ref, bf16[256,384]{1,0:T(8,128)(2,1)S(1)} %bitcast.28, bf16[3328,384]{1,0:T(8,128)(2,1)S(1)} %collective-permute-done.2.refs_2_.refs_5_.refs_1_, bf16[256,1536]{1,0:T(8,128)(2,1)S(1)} %shard_map.80.refs_2_), custom_call_target="tpu_custom_call" | custom-call | flops 301989888 | bytes 5000000 | tf_op jit(solution)/shard_map/pallas_call | solution.py:255
  133.6 38.0 %all_to_all.15.arrived_ref = bf16[32,8,1536]{2,1,0:T(8,128)(2,1)S(1)} all-to-all(bf16[32,8,1536]{2,1,0:T(8,128)(2,1)S(1)} %bitcast.21), channel_id=1, replica_groups={{0,1,2,3,4,5,6,7,128,129,130,131,132,133,134,135,256,257,258,259,260,26..., dimensions={0} | all-to-all | bytes 1572864 | tf_op jit(solution)/shard_map/all_to_all | solution.py:349
  171.7 0.0 copy-done.5
  171.7 0.0 copy-done.6
  171.7 1.9 %shard_map.82 = f32[4,8,384]{2,1,0:T(8,128)} custom-call(bf16[32,8,1536]{2,1,0:T(8,128)(2,1)S(1)} %all_to_all.15.arrived_ref, bf16[4,8,384]{2,1,0:T(8,128)(2,1)S(1)} %bitcast.29, bf16[4,384,384]{2,1,0:T(8,128)(2,1)S(1)} %copy-done.5), custom_call_target="tpu_custom_call" | custom-call | flops 9437184 | bytes 3000000 | tf_op jit(solution)/shard_map/pallas_call | solution.py:279
  (1 shorter events, 0.0 us)
Async XLA Ops:
  0.6 103.8 %copy-start.1 = (bf16[1,2,1,384,512]{4,3,2,1,0:T(8,128)(2,1)S(1)}, bf16[1,2,1,384,512]{4,3,2,1,0:T(8,128)(2,1)}, u32[]{:S(2)}) copy-start(bf16[1,2,1,384,512]{4,3,2,1,0:T(8,128)(2,1)} %param.6) | copy-start | bytes 2359300
  75.1 50.9 %copy-start.7 = (s32[1,1,1,2,4]{4,3,2,1,0:T(2,128)S(1)}, s32[1,1,1,2,4]{4,3,2,1,0:T(2,128)}, u32[]{:S(2)}) copy-start(s32[1,1,1,2,4]{4,3,2,1,0:T(2,128)} %param.9) | copy-start | bytes 100
  75.1 50.9 %collective-permute-start.2 = (bf16[3328,384]{1,0:T(8,128)(2,1)}, bf16[3328,384]{1,0:T(8,128)(2,1)S(1)}, u32[]{:S(2)}, u32[]{:S(2)}) collective-permute-start(bf16[3328,384]{1,0:T(8,128)(2,1)} %get-tuple-element.17), channel_id=1, source_target_pairs={{0,64},{8,456},{16,80},{24,472},{32,96},{40,488},{48,112},{56,504}... | collective-permute-start | bytes 7667720 | tf_op jit(solution)/shard_map/ppermute | solution.py:319
  77.0 17.2 %all-to-all-start = ((bf16[8,64,384]{2,1,0:T(8,128)(2,1)}), bf16[8,64,384]{2,1,0:T(8,128)(2,1)}, u32[]{:S(2)}, u32[]{:S(2)}) async-start(bf16[8,64,384]{2,1,0:T(8,128)(2,1)} %get-tuple-element.10), calls=%async_computation | async-start | bytes 786432 | tf_op jit(solution)/shard_map/all_to_all | solution.py:306
  95.3 11.9 %collective-permute-start = (bf16[64,384]{1,0:T(8,128)(2,1)S(1)}, bf16[64,384]{1,0:T(8,128)(2,1)S(1)}, u32[]{:S(2)}, u32[]{:S(2)}) collective-permute-start(bf16[64,384]{1,0:T(8,128)(2,1)S(1)} %reduce_sum.12), channel_id=1, source_target_pairs={{0,7},{1,15},{2,23},{3,31},{4,39},{5,47},{6,55},{7,63},{8,0},{9,8}... | collective-permute-start | bytes 147464 | tf_op jit(solution)/shard_map/ppermute | solution.py:329
  104.4 1.1 copy-start.2
  105.5 1.0 copy-start.3
  108.1 12.2 %all-to-all-start.1 = ((bf16[4,64,384]{2,1,0:T(8,128)(2,1)}), bf16[4,64,384]{2,1,0:T(8,128)(2,1)S(1)}, u32[]{:S(2)}, u32[]{:S(2)}) async-start(bf16[4,64,384]{2,1,0:T(8,128)(2,1)} %get-tuple-element.16), calls=%async_computation.1 | async-start | bytes 393216 | tf_op jit(solution)/shard_map/all_to_all | solution.py:333
  124.1 7.6 %collective-permute-start.1 = (bf16[4,64,384]{2,1,0:T(8,128)(2,1)S(1)}, bf16[4,64,384]{2,1,0:T(8,128)(2,1)S(1)}, u32[]{:S(2)}, u32[]{:S(2)}) collective-permute-start(bf16[4,64,384]{2,1,0:T(8,128)(2,1)S(1)} %dynamic-slice_bitcast_fusion), channel_id=1, source_target_pairs={{0,64},{8,456},{16,80},{24,472},{32,96},{40,488},{48,112},{56,504}... | collective-permute-start | bytes 589832 | tf_op jit(solution)/shard_map/ppermute | solution.py:319
  126.0 1.7 copy-start
  127.7 1.0 copy-start.4
  131.6 40.0 %copy-start.5 = (bf16[4,384,384]{2,1,0:T(8,128)(2,1)S(1)}, bf16[4,384,384]{2,1,0:T(8,128)(2,1)}, u32[]{:S(2)}) copy-start(bf16[4,384,384]{2,1,0:T(8,128)(2,1)} %inv_ref.1) | copy-start | bytes 3538948
  131.7 40.0 %copy-start.6 = (bf16[4,384,8]{1,2,0:T(8,128)(2,1)S(1)}, bf16[4,384,8]{1,2,0:T(8,128)(2,1)}, u32[]{:S(2)}) copy-start(bf16[4,384,8]{1,2,0:T(8,128)(2,1)} %param.10) | copy-start | bytes 73732

commit v6 on v5

--- a/solution.py
+++ b/solution.py
@@ -36,12 +36,10 @@
 
     def body(
         targets_ref, rhs_ref, inv_ref, blocks_ref, answer_ref, part_ref, give_ref,
-        rhs_in, inv_in, block_in, zeros, half_out, in_sems, out_sems,
+        rhs_in, inv_in, blocks_in, zeros, half_out, in_sems, blocks_sems, out_sems,
     ):
         kept = lax.axis_index("layer") % 2
-        slot, found = slot_of(targets_ref, 0, 1, per_row)
         inv_copy = pltpu.make_async_copy(inv_ref.at[0], inv_in, in_sems.at[steps])
-        block_copy = pltpu.make_async_copy(blocks_ref.at[0, slot], block_in, in_sems.at[steps + 1])
         rhs_copies = [
             pltpu.make_async_copy(
                 rhs_ref.at[0, :, pl.ds(step * (loads // steps), loads // steps)],
@@ -50,29 +48,17 @@
             )
             for step in range(steps)
         ]
-        inv_copy.start()
-        for copy in rhs_copies:
+        blocks_copies = [
+            pltpu.make_async_copy(
+                blocks_ref.at[index // per_row, index % per_row],
+                blocks_in.at[index // per_row, index % per_row],
+                blocks_sems.at[index],
+            )
+            for index in range(slots)
+        ]
+        for copy in (inv_copy, *rhs_copies, *blocks_copies):
             copy.start()
-        block_copy.start()
         zeros[...] = jnp.zeros_like(zeros)
-
-        def give(index):
-            return give_ref.at[pl.ds(index * width, width)]
-
-        for index in range(slots):
-            level, ancestor = index // per_row, index % per_row
-            source, named = slot_of(targets_ref, level, ancestor + 2, per_row)
-
-            @pl.when(named == 1)
-            def _(index=index, level=level, source=source):
-                pltpu.make_async_copy(
-                    blocks_ref.at[level, source], give(index), out_sems.at[index]
-                ).start()
-
-            @pl.when(named == 0)
-            def _(index=index):
-                pltpu.make_async_copy(zeros, give(index), out_sems.at[index]).start()
-
         inv_copy.wait()
         answers = []
         for step in range(steps):
@@ -97,12 +83,32 @@
             half_out, give_ref.at[pl.ds(slots * width, half * share)], out_sems.at[slots]
         )
         half_copy.start()
-        block_copy.wait()
+        for copy in blocks_copies:
+            copy.wait()
+
+        def give(index):
+            return give_ref.at[pl.ds(index * width, width)]
+
+        for index in range(slots):
+            level, ancestor = index // per_row, index % per_row
+            source, named = slot_of(targets_ref, level, ancestor + 2, per_row)
+
+            @pl.when(named == 1)
+            def _(index=index, level=level, source=source):
+                pltpu.make_async_copy(
+                    blocks_in.at[level, source], give(index), out_sems.at[index]
+                ).start()
+
+            @pl.when(named == 0)
+            def _(index=index):
+                pltpu.make_async_copy(zeros, give(index), out_sems.at[index]).start()
+
+        slot, found = slot_of(targets_ref, 0, 1, per_row)
 
         @pl.when(found == 1)
         def _():
             for step in range(steps):
-                part = dot_nt(answers[step], block_in[...]).astype(BF16)
+                part = dot_nt(answers[step], blocks_in[0, slot]).astype(BF16)
                 part_ref[step * held : (step + 1) * held] = part.reshape(held, share, width)
 
         @pl.when(found == 0)
@@ -126,10 +132,11 @@
         scratch_shapes=[
             pltpu.VMEM((steps, width, loads // steps), BF16),
             pltpu.VMEM((width, width), BF16),
-            pltpu.VMEM((width, width), BF16),
+            pltpu.VMEM(blocks.shape, BF16),
             pltpu.VMEM((width, width), BF16),
             pltpu.VMEM((half * share, width), BF16),
-            pltpu.SemaphoreType.DMA((steps + 2,)),
+            pltpu.SemaphoreType.DMA((steps + 1,)),
+            pltpu.SemaphoreType.DMA((slots,)),
             pltpu.SemaphoreType.DMA((slots + 1,)),
         ],
         compiler_params=pltpu.CompilerParams(vmem_limit_bytes=FIRST),

time: 174 us -> 107 us (0.61)
  Pallas kernels: 82.9 us -> 14.3 us
  starting transfers between devices: 25.5 us -> 28.4 us
    pallas_call x1, Pallas kernels: 74.4 us -> 5.8 us  [first_level(): pl.pallas_call(body, out_shape=(jax.ShapeDtypeStruct((2, half, share, wid...]
    ppermute x2, starting transfers between devices: 3.84 us -> 8.28 us  [swap(): return lax.ppermute(value, ('layer', 'row'), pairs)]
    ppermute x1, starting transfers between devices: 9.05 us -> 7.01 us  [on_device(): summed = lax.ppermute(summed, ('row', 'col'), turn)]
  transfers between devices with their start and end apart: 5 -> 5, of which waited for: 2 -> 2; matrix products, arithmetic and copies ran while one was open for 1% -> 1% of each run, Pallas kernels for 3% -> 4%
where the time goes in v6:
time: 107 us; the launch traced here: 106 us
  blocking collectives  40.2 us (38%)
  starting transfers between devices  28.4 us (27%)
  waiting for transfers between devices  16.9 us (16%)
  Pallas kernels  14.3 us (13%)
  local copies, waits for them, and re-layouts  4.76 us (4%)
  other arithmetic  1.13 us (1%)
    all_to_all x1, blocking collectives, on_device(): lax.all_to_all(parts.reshape(members, parts.shape[0] // members, -1), ('l...  36.6 us
    all_to_all x1, waiting for transfers between devices, on_device(): shares = lax.all_to_all(part, 'col', 0, 0, tiled=True)  10.5 us
    ppermute x2, starting transfers between devices, swap(): return lax.ppermute(value, ('layer', 'row'), pairs)  8.28 us
    all_to_all x1, starting transfers between devices, on_device(): shares = lax.all_to_all(part, 'col', 0, 0, tiled=True)  7.56 us
    ppermute x1, starting transfers between devices, on_device(): summed = lax.ppermute(summed, ('row', 'col'), turn)  7.01 us
    all_to_all x1, waiting for transfers between devices, on_device(): lax.all_to_all(pieces, 'row', 0, 0, axis_index_groups=lines, tiled=True)  6.33 us
    pallas_call x1, Pallas kernels, first_level(): pl.pallas_call(body, out_shape=(jax.ShapeDtypeStruct((2, half, share, wid...  5.8 us
    all_to_all x1, starting transfers between devices, on_device(): lax.all_to_all(pieces, 'row', 0, 0, axis_index_groups=lines, tiled=True)  5.58 us
  transfers between devices with their start and end apart: 5, of which 2 were waited for; matrix products, arithmetic and copies ran while one was open for 1% of the time, Pallas kernels for 4%

profile of v6, /device:TPU:8, one launch (start us, length us, event | category | flops | bytes accessed | tf_op | source)
XLA Modules:
  0.0 106.4 jit_solution(10177945049407523365)
XLA Ops:
  0.6 0.0 copy-start.1
  0.6 5.8 %shard_map.77 = (bf16[2,4,64,384]{3,2,1,0:T(8,128)(2,1)}, bf16[8,64,384]{2,1,0:T(8,128)(2,1)}, bf16[3328,384]{1,0:T(8,128)(2,1)}) custom-call(s32[2,4]{1,0:T(2,128)} %bitcast.30, bf16[2,384,512]{2,1,0:T(8,128)(2,1)} %bitcast.22, bf16[2,384,384]{2,1,0:T(8,128)(2,1)} %bitcast.26, bf16[2,4,384,384]{3,2,1,0:T(8,128)(2,1)} %bitcast.18), custom_call_target="tpu_custom_call" | custom-call | flops 301989888 | bytes 2200000 | tf_op jit(solution)/shard_map/pallas_call | solution.py:123
  6.4 0.0 copy-start.7
  6.5 4.3 %collective-permute-start.2 = (bf16[3328,384]{1,0:T(8,128)(2,1)}, bf16[3328,384]{1,0:T(8,128)(2,1)S(1)}, u32[]{:S(2)}, u32[]{:S(2)}) collective-permute-start(bf16[3328,384]{1,0:T(8,128)(2,1)} %get-tuple-element.17), channel_id=1, source_target_pairs={{0,64},{8,456},{16,80},{24,472},{32,96},{40,488},{48,112},{56,504}... | collective-permute-start | bytes 7667720 | tf_op jit(solution)/shard_map/ppermute | solution.py:326
  10.7 7.6 %all-to-all-start = ((bf16[8,64,384]{2,1,0:T(8,128)(2,1)}), bf16[8,64,384]{2,1,0:T(8,128)(2,1)}, u32[]{:S(2)}, u32[]{:S(2)}) async-start(bf16[8,64,384]{2,1,0:T(8,128)(2,1)} %get-tuple-element.10), calls=%async_computation | async-start | bytes 786432 | tf_op jit(solution)/shard_map/all_to_all | solution.py:313
  18.3 10.5 %all-to-all-done = bf16[8,64,384]{2,1,0:T(8,128)(2,1)} async-done(((bf16[8,64,384]{2,1,0:T(8,128)(2,1)}), bf16[8,64,384]{2,1,0:T(8,128)(2,1)}, u32[]{:S(2)}, u32[]{:S(2)}) %all-to-all-start) | async-done | bytes 393248 | tf_op jit(solution)/shard_map/all_to_all | solution.py:313
  28.9 1.1 reduce_sum.12
  29.9 7.0 %collective-permute-start = (bf16[64,384]{1,0:T(8,128)(2,1)S(1)}, bf16[64,384]{1,0:T(8,128)(2,1)S(1)}, u32[]{:S(2)}, u32[]{:S(2)}) collective-permute-start(bf16[64,384]{1,0:T(8,128)(2,1)S(1)} %reduce_sum.12), channel_id=1, source_target_pairs={{0,7},{1,15},{2,23},{3,31},{4,39},{5,47},{6,55},{7,63},{8,0},{9,8}... | collective-permute-start | bytes 147464 | tf_op jit(solution)/shard_map/ppermute | solution.py:336
  36.9 0.1 pad_add_fusion.place_ref
  37.0 0.0 copy-done.1
  37.0 0.0 copy-start.2
  37.0 1.1 copy-done.2
  38.1 0.0 copy-start.3
  38.1 1.0 copy-done.3
  39.1 0.7 shard_map.78
  39.7 0.0 collective-permute-done.part_ref
  39.8 0.9 shard_map.79
  40.7 5.6 %all-to-all-start.1 = ((bf16[4,64,384]{2,1,0:T(8,128)(2,1)}), bf16[4,64,384]{2,1,0:T(8,128)(2,1)S(1)}, u32[]{:S(2)}, u32[]{:S(2)}) async-start(bf16[4,64,384]{2,1,0:T(8,128)(2,1)} %get-tuple-element.16), calls=%async_computation.1 | async-start | bytes 393216 | tf_op jit(solution)/shard_map/all_to_all | solution.py:340
  46.3 6.3 %all-to-all-done.1 = bf16[4,64,384]{2,1,0:T(8,128)(2,1)S(1)} async-done(((bf16[4,64,384]{2,1,0:T(8,128)(2,1)}), bf16[4,64,384]{2,1,0:T(8,128)(2,1)S(1)}, u32[]{:S(2)}, u32[]{:S(2)}) %all-to-all-start.1) | async-done | bytes 196640 | tf_op jit(solution)/shard_map/all_to_all | solution.py:340
  52.6 3.6 %all-gather = bf16[8,64,384]{2,1,0:T(8,128)(2,1)S(1)} all-gather(bf16[4,64,384]{2,1,0:T(8,128)(2,1)S(1)} %all-to-all-done.1), channel_id=2, replica_groups={{0,8},{16,24},{32,40},{48,56},{1,9},{17,25},{33,41},{49,57},{2,10},{18,..., dimensions={0}, use_global_device_ids=true | all-gather | bytes 589824 | tf_op jit(solution)/shard_map/all_gather | solution.py:341
  56.2 4.0 %collective-permute-start.1 = (bf16[4,64,384]{2,1,0:T(8,128)(2,1)S(1)}, bf16[4,64,384]{2,1,0:T(8,128)(2,1)S(1)}, u32[]{:S(2)}, u32[]{:S(2)}) collective-permute-start(bf16[4,64,384]{2,1,0:T(8,128)(2,1)S(1)} %dynamic-slice_bitcast_fusion), channel_id=1, source_target_pairs={{0,64},{8,456},{16,80},{24,472},{32,96},{40,488},{48,112},{56,504}... | collective-permute-start | bytes 589832 | tf_op jit(solution)/shard_map/ppermute | solution.py:326
  60.3 0.0 collective-permute-done.2.refs_2_.refs_5_.refs_1_
  60.3 0.0 copy-done.7
  60.3 0.0 copy-start
  60.3 1.7 %copy-done = bf16[1,1,1,2,4,384,384]{6,5,4,3,2,1,0:T(8,128)(2,1)S(1)} copy-done((bf16[1,1,1,2,4,384,384]{6,5,4,3,2,1,0:T(8,128)(2,1)S(1)}, bf16[1,1,1,2,4,384,384]{6,5,4,3,2,1,0:T(8,128)(2,1)}, u32[]{:S(2)}) %copy-start) | copy-done | bytes 2359320
  61.9 0.0 copy-start.4
  62.0 1.0 copy-done.4
  62.9 2.9 %shard_map.80.refs_2_ = bf16[256,1536]{1,0:T(8,128)(2,1)S(1)} custom-call(s32[2,4]{1,0:T(2,128)S(1)} %bitcast.31, s32[2]{0:T(128)S(1)} %pad_add_fusion.place_ref, bf16[2,4,64,384]{3,2,1,0:T(8,128)(2,1)S(1)} %copy-done.4, bf16[2,4,64,384]{3,2,1,0:T(8,128)(2,1)S(1)} %bitcast.25, bf16[3328,384]{1,0:T(8,128)(2,1)S(1)} %collective-permute-done.2.refs_2_.refs_5_.refs_1_, ...), custom_call_target="tpu_custom_call" | custom-call | flops 905969664 | bytes 5000000 | tf_op jit(solution)/shard_map/pallas_call | solution.py:262
  65.9 0.0 collective-permute-done.1
  65.9 0.0 copy-start.5
  65.9 0.0 copy-start.6
  65.9 2.0 %shard_map.81 = bf16[256,1536]{1,0:T(8,128)(2,1)S(1)} custom-call(s32[2,4]{1,0:T(2,128)S(1)} %bitcast.32, s32[2]{0:T(128)S(1)} %pad_add_fusion.place_ref, bf16[256,384]{1,0:T(8,128)(2,1)S(1)} %bitcast.28, bf16[3328,384]{1,0:T(8,128)(2,1)S(1)} %collective-permute-done.2.refs_2_.refs_5_.refs_1_, bf16[256,1536]{1,0:T(8,128)(2,1)S(1)} %shard_map.80.refs_2_), custom_call_target="tpu_custom_call" | custom-call | flops 301989888 | bytes 5000000 | tf_op jit(solution)/shard_map/pallas_call | solution.py:262
  67.9 36.6 %all_to_all.15.arrived_ref = bf16[32,8,1536]{2,1,0:T(8,128)(2,1)S(1)} all-to-all(bf16[32,8,1536]{2,1,0:T(8,128)(2,1)S(1)} %bitcast.21), channel_id=1, replica_groups={{0,1,2,3,4,5,6,7,128,129,130,131,132,133,134,135,256,257,258,259,260,26..., dimensions={0} | all-to-all | bytes 1572864 | tf_op jit(solution)/shard_map/all_to_all | solution.py:356
  104.5 0.0 copy-done.5
  104.5 0.0 copy-done.6
  104.5 1.9 %shard_map.82 = f32[4,8,384]{2,1,0:T(8,128)} custom-call(bf16[32,8,1536]{2,1,0:T(8,128)(2,1)S(1)} %all_to_all.15.arrived_ref, bf16[4,8,384]{2,1,0:T(8,128)(2,1)S(1)} %bitcast.29, bf16[4,384,384]{2,1,0:T(8,128)(2,1)S(1)} %copy-done.5), custom_call_target="tpu_custom_call" | custom-call | flops 9437184 | bytes 3000000 | tf_op jit(solution)/shard_map/pallas_call | solution.py:286
  (1 shorter events, 0.0 us)
Async XLA Ops:
  0.6 36.4 %copy-start.1 = (bf16[1,2,1,384,512]{4,3,2,1,0:T(8,128)(2,1)S(1)}, bf16[1,2,1,384,512]{4,3,2,1,0:T(8,128)(2,1)}, u32[]{:S(2)}) copy-start(bf16[1,2,1,384,512]{4,3,2,1,0:T(8,128)(2,1)} %param.6) | copy-start | bytes 2359300
  6.4 53.8 %copy-start.7 = (s32[1,1,1,2,4]{4,3,2,1,0:T(2,128)S(1)}, s32[1,1,1,2,4]{4,3,2,1,0:T(2,128)}, u32[]{:S(2)}) copy-start(s32[1,1,1,2,4]{4,3,2,1,0:T(2,128)} %param.9) | copy-start | bytes 100
  6.5 53.8 %collective-permute-start.2 = (bf16[3328,384]{1,0:T(8,128)(2,1)}, bf16[3328,384]{1,0:T(8,128)(2,1)S(1)}, u32[]{:S(2)}, u32[]{:S(2)}) collective-permute-start(bf16[3328,384]{1,0:T(8,128)(2,1)} %get-tuple-element.17), channel_id=1, source_target_pairs={{0,64},{8,456},{16,80},{24,472},{32,96},{40,488},{48,112},{56,504}... | collective-permute-start | bytes 7667720 | tf_op jit(solution)/shard_map/ppermute | solution.py:326
  10.7 18.1 %all-to-all-start = ((bf16[8,64,384]{2,1,0:T(8,128)(2,1)}), bf16[8,64,384]{2,1,0:T(8,128)(2,1)}, u32[]{:S(2)}, u32[]{:S(2)}) async-start(bf16[8,64,384]{2,1,0:T(8,128)(2,1)} %get-tuple-element.10), calls=%async_computation | async-start | bytes 786432 | tf_op jit(solution)/shard_map/all_to_all | solution.py:313
  29.9 9.8 %collective-permute-start = (bf16[64,384]{1,0:T(8,128)(2,1)S(1)}, bf16[64,384]{1,0:T(8,128)(2,1)S(1)}, u32[]{:S(2)}, u32[]{:S(2)}) collective-permute-start(bf16[64,384]{1,0:T(8,128)(2,1)S(1)} %reduce_sum.12), channel_id=1, source_target_pairs={{0,7},{1,15},{2,23},{3,31},{4,39},{5,47},{6,55},{7,63},{8,0},{9,8}... | collective-permute-start | bytes 147464 | tf_op jit(solution)/shard_map/ppermute | solution.py:336
  37.0 1.1 %copy-start.2 = (bf16[1,2,1,384,384]{4,3,2,1,0:T(8,128)(2,1)S(1)}, bf16[1,2,1,384,384]{4,3,2,1,0:T(8,128)(2,1)}, u32[]{:S(2)}) copy-start(bf16[1,2,1,384,384]{4,3,2,1,0:T(8,128)(2,1)} %param.7) | copy-start | bytes 1769476
  38.1 1.0 copy-start.3
  40.7 11.9 %all-to-all-start.1 = ((bf16[4,64,384]{2,1,0:T(8,128)(2,1)}), bf16[4,64,384]{2,1,0:T(8,128)(2,1)S(1)}, u32[]{:S(2)}, u32[]{:S(2)}) async-start(bf16[4,64,384]{2,1,0:T(8,128)(2,1)} %get-tuple-element.16), calls=%async_computation.1 | async-start | bytes 393216 | tf_op jit(solution)/shard_map/all_to_all | solution.py:340
  56.2 9.6 %collective-permute-start.1 = (bf16[4,64,384]{2,1,0:T(8,128)(2,1)S(1)}, bf16[4,64,384]{2,1,0:T(8,128)(2,1)S(1)}, u32[]{:S(2)}, u32[]{:S(2)}) collective-permute-start(bf16[4,64,384]{2,1,0:T(8,128)(2,1)S(1)} %dynamic-slice_bitcast_fusion), channel_id=1, source_target_pairs={{0,64},{8,456},{16,80},{24,472},{32,96},{40,488},{48,112},{56,504}... | collective-permute-start | bytes 589832 | tf_op jit(solution)/shard_map/ppermute | solution.py:326
  60.3 1.7 %copy-start = (bf16[1,1,1,2,4,384,384]{6,5,4,3,2,1,0:T(8,128)(2,1)S(1)}, bf16[1,1,1,2,4,384,384]{6,5,4,3,2,1,0:T(8,128)(2,1)}, u32[]{:S(2)}) copy-start(bf16[1,1,1,2,4,384,384]{6,5,4,3,2,1,0:T(8,128)(2,1)} %param.8) | copy-start | bytes 7077892
  61.9 1.0 copy-start.4
  65.9 38.6 %copy-start.5 = (bf16[4,384,384]{2,1,0:T(8,128)(2,1)S(1)}, bf16[4,384,384]{2,1,0:T(8,128)(2,1)}, u32[]{:S(2)}) copy-start(bf16[4,384,384]{2,1,0:T(8,128)(2,1)} %inv_ref.1) | copy-start | bytes 3538948
  65.9 38.6 %copy-start.6 = (bf16[4,384,8]{1,2,0:T(8,128)(2,1)S(1)}, bf16[4,384,8]{1,2,0:T(8,128)(2,1)}, u32[]{:S(2)}) copy-start(bf16[4,384,8]{1,2,0:T(8,128)(2,1)} %param.10) | copy-start | bytes 73732

commit v7 on v6

--- a/solution.py
+++ b/solution.py
@@ -9,7 +9,7 @@
 BF16 = jnp.bfloat16
 SMALL = 8 << 20
 LARGE = 24 << 20
-FIRST = 60 << 20
+FIRST = 58 << 20
 NT = (((1,), (1,)), ((), ()))
 
 
@@ -49,19 +49,37 @@
             for step in range(steps)
         ]
         blocks_copies = [
-            pltpu.make_async_copy(
-                blocks_ref.at[index // per_row, index % per_row],
-                blocks_in.at[index // per_row, index % per_row],
-                blocks_sems.at[index],
-            )
-            for index in range(slots)
+            pltpu.make_async_copy(blocks_ref.at[level], blocks_in.at[level], blocks_sems.at[level])
+            for level in range(levels)
         ]
+
+        def give(index):
+            return give_ref.at[pl.ds(index * width, width)]
+
+        def pass_on(level):
+            blocks_copies[level].wait()
+            for ancestor in range(per_row):
+                index = level * per_row + ancestor
+                source, named = slot_of(targets_ref, level, ancestor + 2, per_row)
+
+                @pl.when(named == 1)
+                def _(index=index, source=source):
+                    pltpu.make_async_copy(
+                        blocks_in.at[level, source], give(index), out_sems.at[index]
+                    ).start()
+
+                @pl.when(named == 0)
+                def _(index=index):
+                    pltpu.make_async_copy(zeros, give(index), out_sems.at[index]).start()
+
         for copy in (inv_copy, *rhs_copies, *blocks_copies):
             copy.start()
         zeros[...] = jnp.zeros_like(zeros)
         inv_copy.wait()
         answers = []
         for step in range(steps):
+            if step > 0:
+                pass_on(step - 1)
             rhs_copies[step].wait()
             answer = jnp.dot(inv_in[...], rhs_in[step], preferred_element_type=F32).T.astype(BF16)
             answers.append(answer)
@@ -83,26 +101,8 @@
             half_out, give_ref.at[pl.ds(slots * width, half * share)], out_sems.at[slots]
         )
         half_copy.start()
-        for copy in blocks_copies:
-            copy.wait()
-
-        def give(index):
-            return give_ref.at[pl.ds(index * width, width)]
-
-        for index in range(slots):
-            level, ancestor = index // per_row, index % per_row
-            source, named = slot_of(targets_ref, level, ancestor + 2, per_row)
-
-            @pl.when(named == 1)
-            def _(index=index, level=level, source=source):
-                pltpu.make_async_copy(
-                    blocks_in.at[level, source], give(index), out_sems.at[index]
-                ).start()
-
-            @pl.when(named == 0)
-            def _(index=index):
-                pltpu.make_async_copy(zeros, give(index), out_sems.at[index]).start()
-
+        for level in range(steps - 1, levels):
+            pass_on(level)
         slot, found = slot_of(targets_ref, 0, 1, per_row)
 
         @pl.when(found == 1)
@@ -136,7 +136,7 @@
             pltpu.VMEM((width, width), BF16),
             pltpu.VMEM((half * share, width), BF16),
             pltpu.SemaphoreType.DMA((steps + 1,)),
-            pltpu.SemaphoreType.DMA((slots,)),
+            pltpu.SemaphoreType.DMA((levels,)),
             pltpu.SemaphoreType.DMA((slots + 1,)),
         ],
         compiler_params=pltpu.CompilerParams(vmem_limit_bytes=FIRST),
@@ -216,45 +216,34 @@
     )(part, right_side, inverse, first)
 
 
-def ancestor_parts(targets, place, own, near, before=None):
-    loads, width = near[0][4], near[0][1].shape[-1]
-    count = near[0][5]
+def ancestor_parts(place, own, near, room, before=None):
+    loads, width, count = near[0][4], near[0][1].shape[-1], near[0][5]
     terms = len(own) + len(near)
 
-    def body(targets_ref, place_ref, *refs):
+    def body(place_ref, *refs):
         answers, blocks, rest = refs[:terms], refs[terms : 2 * terms], refs[2 * terms :]
         total = None
         for index in range(terms):
-            if index < len(own):
-                _, found = slot_of(targets_ref, own[index][0], pl.program_id(0) + 2, count)
-                value = answers[index][0].reshape(loads, width)
-                product = dot_nt(value, blocks[index][0, 0])
-                product = product * jnp.where(found == 1, 1.0, 0.0).astype(F32)
-            else:
-                product = dot_nt(answers[index][...], blocks[index][...])
+            value = answers[index]
+            value = value[0].reshape(loads, width) if index < len(own) else value[...]
+            product = dot_nt(value, blocks[index][...])
             total = product if total is None else total + product
         if before is not None:
             total += rest[0][...].astype(F32)
         rest[-1][...] = total.astype(BF16)
 
     def own_answer(answer):
-        return pl.BlockSpec((1, *answer.shape[1:]), lambda a, t, p: (p[1], 0, 0, 0))
-
-    def own_block(level):
-        return pl.BlockSpec(
-            (1, 1, width, width),
-            lambda a, t, p: (level, slot_of(t, level, a + 2, count)[0], 0, 0),
-        )
+        return pl.BlockSpec((1, *answer.shape[1:]), lambda a, p: (p[1], 0, 0, 0))
 
     def near_answer(spot):
-        return pl.BlockSpec((loads, width), lambda a, t, p: (spot, 0))
-
-    def near_block(level):
-        return pl.BlockSpec((width, width), lambda a, t, p: (level * count + a, 0))
-
-    out_spec = pl.BlockSpec((loads, width), lambda a, t, p: (0, a))
+        return pl.BlockSpec((loads, width), lambda a, p: (spot, 0))
+
+    def block(level):
+        return pl.BlockSpec((width, width), lambda a, p: (level * count + a, 0))
+
+    out_spec = pl.BlockSpec((loads, width), lambda a, p: (0, a))
     in_specs = [own_answer(term[2]) for term in own] + [near_answer(term[3]) for term in near]
-    in_specs += [own_block(term[0]) for term in own] + [near_block(term[0]) for term in near]
+    in_specs += [block(term[0]) for term in (*own, *near)]
     operands = [term[2] for term in (*own, *near)] + [term[1] for term in (*own, *near)]
     if before is not None:
         in_specs.append(out_spec)
@@ -263,15 +252,15 @@
         body,
         out_shape=jax.ShapeDtypeStruct((loads, count * width), BF16),
         grid_spec=pltpu.PrefetchScalarGridSpec(
-            num_scalar_prefetch=2, grid=(count,), in_specs=in_specs, out_specs=out_spec
-        ),
-        compiler_params=pltpu.CompilerParams(vmem_limit_bytes=LARGE),
+            num_scalar_prefetch=1, grid=(count,), in_specs=in_specs, out_specs=out_spec
+        ),
+        compiler_params=pltpu.CompilerParams(vmem_limit_bytes=room),
         cost_estimate=pl.CostEstimate(
             flops=2 * terms * count * width * width * loads,
             bytes_accessed=5_000_000,
             transcendentals=0,
         ),
-    )(targets, place, *operands)
+    )(place, *operands)
 
 
 def ancestor_solve(arrived, rhs_anc, inv_anc):
@@ -343,11 +332,11 @@
     near_answer1 = swap(lax.dynamic_index_in_dim(answer1, 1 - place[1], 0, keepdims=False))
     wanted, count = loads // 2, inv_anc.shape[0]
     near_answer1 = near_answer1.reshape(wanted, width)
-    own = [(0, blocks, answer0), (1, blocks, answer1)]
+    own = [(0, give, answer0), (1, give, answer1)]
     early = (0, near, near, near.shape[0] // wanted - 1, wanted, count)
     late = (1, near, near_answer1, 0, wanted, count)
-    parts = ancestor_parts(targets, place, own, [early])
-    parts = ancestor_parts(targets, place, [], [late], parts)
+    parts = ancestor_parts(place, own, [early], FIRST)
+    parts = ancestor_parts(place, [], [late], FIRST, parts)
     groups = [
         [layer * cols + col for layer in range(parity, layers, 2) for col in range(cols)]
         for parity in range(2)

time: 107 us -> 110 us (1.028)
  Pallas kernels: 14.3 us -> 19.1 us
  local copies, waits for them, and re-layouts: 4.76 us -> 1.7 us
    pallas_call x2, Pallas kernels: 4.9 us -> 10.7 us  [ancestor_parts(): pl.pallas_call(body, out_shape=jax.ShapeDtypeStruct((loads, count * width...]
    unnamed x16, local copies, waits for them, and re-layouts: 4.74 us -> 1.68 us
  transfers between devices with their start and end apart: 5 -> 5, of which waited for: 2 -> 3; matrix products, arithmetic and copies ran while one was open for 1% -> 0% of each run, Pallas kernels for 4% -> 7%
where the time goes in v7:
time: 110 us; the launch traced here: 109 us
  blocking collectives  41.1 us (37%)
  starting transfers between devices  29.3 us (27%)
  Pallas kernels  19.1 us (17%)
  waiting for transfers between devices  17 us (15%)
  local copies, waits for them, and re-layouts  1.7 us (2%)
    all_to_all x1, blocking collectives, on_device(): lax.all_to_all(parts.reshape(members, parts.shape[0] // members, -1), ('l...  37.5 us
    pallas_call x2, Pallas kernels, ancestor_parts(): pl.pallas_call(body, out_shape=jax.ShapeDtypeStruct((loads, count * width...  10.7 us
    all_to_all x1, waiting for transfers between devices, on_device(): shares = lax.all_to_all(part, 'col', 0, 0, tiled=True)  10.4 us
    ppermute x2, starting transfers between devices, swap(): return lax.ppermute(value, ('layer', 'row'), pairs)  8.29 us
    all_to_all x1, starting transfers between devices, on_device(): shares = lax.all_to_all(part, 'col', 0, 0, tiled=True)  7.56 us
    ppermute x1, starting transfers between devices, on_device(): summed = lax.ppermute(summed, ('row', 'col'), turn)  7.01 us
    all_to_all x1, starting transfers between devices, on_device(): lax.all_to_all(pieces, 'row', 0, 0, axis_index_groups=lines, tiled=True)  6.48 us
    all_to_all x1, waiting for transfers between devices, on_device(): lax.all_to_all(pieces, 'row', 0, 0, axis_index_groups=lines, tiled=True)  6.33 us
  transfers between devices with their start and end apart: 5, of which 3 were waited for; matrix products, arithmetic and copies ran while one was open for 0% of the time, Pallas kernels for 7%

profile of v7, /device:TPU:8, one launch (start us, length us, event | category | flops | bytes accessed | tf_op | source)
XLA Modules:
  0.0 109.1 jit_solution(5553486208177435014)
XLA Ops:
  0.6 0.0 copy-start
  0.6 0.0 copy-start.1
  0.7 4.9 %shard_map.77 = (bf16[2,4,64,384]{3,2,1,0:T(8,128)(2,1)}, bf16[8,64,384]{2,1,0:T(8,128)(2,1)}, bf16[3328,384]{1,0:T(8,128)(2,1)}) custom-call(s32[2,4]{1,0:T(2,128)} %bitcast.29, bf16[2,384,512]{2,1,0:T(8,128)(2,1)} %bitcast.18, bf16[2,384,384]{2,1,0:T(8,128)(2,1)} %bitcast.20, bf16[2,4,384,384]{3,2,1,0:T(8,128)(2,1)} %bitcast.26), custom_call_target="tpu_custom_call" | custom-call | flops 301989888 | bytes 2200000 | tf_op jit(solution)/shard_map/pallas_call | solution.py:123
  5.5 4.3 %collective-permute-start.2 = (bf16[3328,384]{1,0:T(8,128)(2,1)}, bf16[3328,384]{1,0:T(8,128)(2,1)}, u32[]{:S(2)}, u32[]{:S(2)}) collective-permute-start(bf16[3328,384]{1,0:T(8,128)(2,1)} %get-tuple-element.17.refs_3_.refs_4_), channel_id=1, source_target_pairs={{0,64},{8,456},{16,80},{24,472},{32,96},{40,488},{48,112},{56,504}... | collective-permute-start | bytes 7667720 | tf_op jit(solution)/shard_map/ppermute | solution.py:315
  9.8 7.6 %all-to-all-start = ((bf16[8,64,384]{2,1,0:T(8,128)(2,1)}), bf16[8,64,384]{2,1,0:T(8,128)(2,1)S(1)}, u32[]{:S(2)}, u32[]{:S(2)}) async-start(bf16[8,64,384]{2,1,0:T(8,128)(2,1)} %get-tuple-element.10), calls=%async_computation | async-start | bytes 786432 | tf_op jit(solution)/shard_map/all_to_all | solution.py:302
  17.4 10.4 %all-to-all-done = bf16[8,64,384]{2,1,0:T(8,128)(2,1)S(1)} async-done(((bf16[8,64,384]{2,1,0:T(8,128)(2,1)}), bf16[8,64,384]{2,1,0:T(8,128)(2,1)S(1)}, u32[]{:S(2)}, u32[]{:S(2)}) %all-to-all-start) | async-done | bytes 393248 | tf_op jit(solution)/shard_map/all_to_all | solution.py:302
  27.8 0.1 reduce_sum.12
  27.9 7.0 %collective-permute-start = (bf16[64,384]{1,0:T(8,128)(2,1)S(1)}, bf16[64,384]{1,0:T(8,128)(2,1)S(1)}, u32[]{:S(2)}, u32[]{:S(2)}) collective-permute-start(bf16[64,384]{1,0:T(8,128)(2,1)S(1)} %reduce_sum.12), channel_id=1, source_target_pairs={{0,7},{1,15},{2,23},{3,31},{4,39},{5,47},{6,55},{7,63},{8,0},{9,8}... | collective-permute-start | bytes 147464 | tf_op jit(solution)/shard_map/ppermute | solution.py:325
  34.9 0.1 pad_add_fusion.place_ref
  35.0 0.0 copy-start.5
  35.0 0.0 copy-done
  35.0 0.0 copy-done.1
  35.0 0.0 copy-start.2
  35.0 1.0 copy-done.2
  36.0 0.7 shard_map.78
  36.6 0.2 collective-permute-done.part_ref
  36.8 0.9 shard_map.79
  37.8 6.5 %all-to-all-start.1 = ((bf16[4,64,384]{2,1,0:T(8,128)(2,1)}), bf16[4,64,384]{2,1,0:T(8,128)(2,1)S(1)}, u32[]{:S(2)}, u32[]{:S(2)}) async-start(bf16[4,64,384]{2,1,0:T(8,128)(2,1)} %get-tuple-element.16), calls=%async_computation.1 | async-start | bytes 393216 | tf_op jit(solution)/shard_map/all_to_all | solution.py:329
  44.2 6.3 %all-to-all-done.1 = bf16[4,64,384]{2,1,0:T(8,128)(2,1)S(1)} async-done(((bf16[4,64,384]{2,1,0:T(8,128)(2,1)}), bf16[4,64,384]{2,1,0:T(8,128)(2,1)S(1)}, u32[]{:S(2)}, u32[]{:S(2)}) %all-to-all-start.1) | async-done | bytes 196640 | tf_op jit(solution)/shard_map/all_to_all | solution.py:329
  50.6 3.6 %all-gather = bf16[8,64,384]{2,1,0:T(8,128)(2,1)S(1)} all-gather(bf16[4,64,384]{2,1,0:T(8,128)(2,1)S(1)} %all-to-all-done.1), channel_id=2, replica_groups={{0,8},{16,24},{32,40},{48,56},{1,9},{17,25},{33,41},{49,57},{2,10},{18,..., dimensions={0}, use_global_device_ids=true | all-gather | bytes 589824 | tf_op jit(solution)/shard_map/all_gather | solution.py:330
  54.2 0.0 copy-start.6
  54.2 4.0 %collective-permute-start.1 = (bf16[4,64,384]{2,1,0:T(8,128)(2,1)S(1)}, bf16[4,64,384]{2,1,0:T(8,128)(2,1)S(1)}, u32[]{:S(2)}, u32[]{:S(2)}) collective-permute-start(bf16[4,64,384]{2,1,0:T(8,128)(2,1)S(1)} %dynamic-slice_bitcast_fusion), channel_id=1, source_target_pairs={{0,64},{8,456},{16,80},{24,472},{32,96},{40,488},{48,112},{56,504}... | collective-permute-start | bytes 589832 | tf_op jit(solution)/shard_map/ppermute | solution.py:315
  58.2 0.0 collective-permute-done.2.refs_2_.refs_5_.refs_1_
  58.2 0.0 copy-done.5
  58.2 0.0 copy-done.6
  58.2 5.7 %shard_map.80.refs_2_ = bf16[256,1536]{1,0:T(8,128)(2,1)} custom-call(s32[2]{0:T(128)} %copy-done.5, bf16[2,4,64,384]{3,2,1,0:T(8,128)(2,1)} %get-tuple-element.11.answer0_ref.refs_0_, bf16[2,4,64,384]{3,2,1,0:T(8,128)(2,1)} %bitcast.25, bf16[3328,384]{1,0:T(8,128)(2,1)} %collective-permute-done.2.refs_2_.refs_5_.refs_1_, ...), custom_call_target="tpu_custom_call" | custom-call | flops 905969664 | bytes 5000000 | tf_op jit(solution)/shard_map/pallas_call | solution.py:251
  63.9 0.0 collective-permute-done.1
  63.9 0.0 copy-start.7
  64.0 0.7 copy-done.7
  64.6 0.0 copy-start.3
  64.6 0.0 copy-start.4
  64.6 5.0 %shard_map.81 = bf16[256,1536]{1,0:T(8,128)(2,1)} custom-call(s32[2]{0:T(128)} %copy-done.5, bf16[256,384]{1,0:T(8,128)(2,1)} %bitcast.27, bf16[3328,384]{1,0:T(8,128)(2,1)} %collective-permute-done.2.refs_2_.refs_5_.refs_1_, bf16[256,1536]{1,0:T(8,128)(2,1)} %shard_map.80.refs_2_), custom_call_target="tpu_custom_call" | custom-call | flops 301989888 | bytes 5000000 | tf_op jit(solution)/shard_map/pallas_call | solution.py:251
  69.6 37.5 %all_to_all.15.arrived_ref = bf16[32,8,1536]{2,1,0:T(8,128)(2,1)S(1)} all-to-all(bf16[32,8,1536]{2,1,0:T(8,128)(2,1)} %bitcast.23), channel_id=1, replica_groups={{0,1,2,3,4,5,6,7,128,129,130,131,132,133,134,135,256,257,258,259,260,26..., dimensions={0} | all-to-all | bytes 1572864 | tf_op jit(solution)/shard_map/all_to_all | solution.py:345
  107.1 0.0 copy-done.3
  107.1 0.0 copy-done.4
  107.1 1.9 %shard_map.82 = f32[4,8,384]{2,1,0:T(8,128)} custom-call(bf16[32,8,1536]{2,1,0:T(8,128)(2,1)S(1)} %all_to_all.15.arrived_ref, bf16[4,8,384]{2,1,0:T(8,128)(2,1)S(1)} %bitcast.22, bf16[4,384,384]{2,1,0:T(8,128)(2,1)S(1)} %copy-done.3), custom_call_target="tpu_custom_call" | custom-call | flops 9437184 | bytes 3000000 | tf_op jit(solution)/shard_map/pallas_call | solution.py:275
  (1 shorter events, 0.0 us)
Async XLA Ops:
  0.6 34.3 %copy-start = (bf16[1,2,1,384,512]{4,3,2,1,0:T(8,128)(2,1)S(1)}, bf16[1,2,1,384,512]{4,3,2,1,0:T(8,128)(2,1)}, u32[]{:S(2)}) copy-start(bf16[1,2,1,384,512]{4,3,2,1,0:T(8,128)(2,1)} %param.6) | copy-start | bytes 2359300
  0.6 34.3 %copy-start.1 = (bf16[1,2,1,384,384]{4,3,2,1,0:T(8,128)(2,1)S(1)}, bf16[1,2,1,384,384]{4,3,2,1,0:T(8,128)(2,1)}, u32[]{:S(2)}) copy-start(bf16[1,2,1,384,384]{4,3,2,1,0:T(8,128)(2,1)} %param.7) | copy-start | bytes 1769476
  5.5 52.7 %collective-permute-start.2 = (bf16[3328,384]{1,0:T(8,128)(2,1)}, bf16[3328,384]{1,0:T(8,128)(2,1)}, u32[]{:S(2)}, u32[]{:S(2)}) collective-permute-start(bf16[3328,384]{1,0:T(8,128)(2,1)} %get-tuple-element.17.refs_3_.refs_4_), channel_id=1, source_target_pairs={{0,64},{8,456},{16,80},{24,472},{32,96},{40,488},{48,112},{56,504}... | collective-permute-start | bytes 7667720 | tf_op jit(solution)/shard_map/ppermute | solution.py:315
  9.8 18.0 %all-to-all-start = ((bf16[8,64,384]{2,1,0:T(8,128)(2,1)}), bf16[8,64,384]{2,1,0:T(8,128)(2,1)S(1)}, u32[]{:S(2)}, u32[]{:S(2)}) async-start(bf16[8,64,384]{2,1,0:T(8,128)(2,1)} %get-tuple-element.10), calls=%async_computation | async-start | bytes 786432 | tf_op jit(solution)/shard_map/all_to_all | solution.py:302
  27.9 9.0 %collective-permute-start = (bf16[64,384]{1,0:T(8,128)(2,1)S(1)}, bf16[64,384]{1,0:T(8,128)(2,1)S(1)}, u32[]{:S(2)}, u32[]{:S(2)}) collective-permute-start(bf16[64,384]{1,0:T(8,128)(2,1)S(1)} %reduce_sum.12), channel_id=1, source_target_pairs={{0,7},{1,15},{2,23},{3,31},{4,39},{5,47},{6,55},{7,63},{8,0},{9,8}... | collective-permute-start | bytes 147464 | tf_op jit(solution)/shard_map/ppermute | solution.py:325
  35.0 23.3 %copy-start.5 = (s32[2]{0:T(128)}, s32[2]{0:T(128)S(1)}, u32[]{:S(2)}) copy-start(s32[2]{0:T(128)S(1)} %pad_add_fusion.place_ref) | copy-start | bytes 28
  35.0 1.0 copy-start.2
  37.8 12.8 %all-to-all-start.1 = ((bf16[4,64,384]{2,1,0:T(8,128)(2,1)}), bf16[4,64,384]{2,1,0:T(8,128)(2,1)S(1)}, u32[]{:S(2)}, u32[]{:S(2)}) async-start(bf16[4,64,384]{2,1,0:T(8,128)(2,1)} %get-tuple-element.16), calls=%async_computation.1 | async-start | bytes 393216 | tf_op jit(solution)/shard_map/all_to_all | solution.py:329
  54.2 4.1 %copy-start.6 = (bf16[8,64,384]{2,1,0:T(8,128)(2,1)}, bf16[8,64,384]{2,1,0:T(8,128)(2,1)S(1)}, u32[]{:S(2)}) copy-start(bf16[8,64,384]{2,1,0:T(8,128)(2,1)S(1)} %all-gather) | copy-start | bytes 1179652
  54.2 9.7 %collective-permute-start.1 = (bf16[4,64,384]{2,1,0:T(8,128)(2,1)S(1)}, bf16[4,64,384]{2,1,0:T(8,128)(2,1)S(1)}, u32[]{:S(2)}, u32[]{:S(2)}) collective-permute-start(bf16[4,64,384]{2,1,0:T(8,128)(2,1)S(1)} %dynamic-slice_bitcast_fusion), channel_id=1, source_target_pairs={{0,64},{8,456},{16,80},{24,472},{32,96},{40,488},{48,112},{56,504}... | collective-permute-start | bytes 589832 | tf_op jit(solution)/shard_map/ppermute | solution.py:315
  63.9 0.7 copy-start.7
  64.6 42.5 %copy-start.3 = (bf16[4,384,384]{2,1,0:T(8,128)(2,1)S(1)}, bf16[4,384,384]{2,1,0:T(8,128)(2,1)}, u32[]{:S(2)}) copy-start(bf16[4,384,384]{2,1,0:T(8,128)(2,1)} %inv_ref.1) | copy-start | bytes 3538948
  64.6 42.5 %copy-start.4 = (bf16[4,384,8]{1,2,0:T(8,128)(2,1)S(1)}, bf16[4,384,8]{1,2,0:T(8,128)(2,1)}, u32[]{:S(2)}) copy-start(bf16[4,384,8]{1,2,0:T(8,128)(2,1)} %param.10) | copy-start | bytes 73732

commit v8 on v7

--- a/solution.py
+++ b/solution.py
@@ -9,7 +9,7 @@
 BF16 = jnp.bfloat16
 SMALL = 8 << 20
 LARGE = 24 << 20
-FIRST = 58 << 20
+FIRST = 60 << 20
 NT = (((1,), (1,)), ((), ()))
 
 
@@ -151,7 +151,9 @@
     lanes = max(share, 128)
     per_lanes = lanes // share
 
-    def body(place_ref, rhs_ref, inv_ref, answer0_ref, out_ref, inverse_ref, first_ref):
+    def body(
+        place_ref, rhs_ref, inv_ref, answer0_ref, kept_ref, out_ref, inverse_ref, first_ref, half_ref
+    ):
         turned = rhs_ref[0].astype(F32).T
         picked = turned[:share]
         for other in range(1, per_lanes):
@@ -163,6 +165,7 @@
         out_ref[...] = picked.astype(BF16)
         inverse_ref[...] = inv_ref[0]
         first_ref[...] = answer0_ref[0, 0]
+        half_ref[...] = kept_ref[0].reshape(held * share, width)
 
     return pl.pallas_call(
         body,
@@ -170,6 +173,7 @@
             jax.ShapeDtypeStruct((share, width), BF16),
             jax.ShapeDtypeStruct((width, width), BF16),
             jax.ShapeDtypeStruct((share, width), BF16),
+            jax.ShapeDtypeStruct((held * share, width), BF16),
         ),
         grid_spec=pltpu.PrefetchScalarGridSpec(
             num_scalar_prefetch=1,
@@ -178,18 +182,32 @@
                 pl.BlockSpec((1, width, lanes), lambda i, p: (level, 0, p[0] // per_lanes)),
                 pl.BlockSpec((1, width, width), lambda i, p: (level, 0, 0)),
                 pl.BlockSpec((1, 1, share, width), lambda i, p: (p[0] % 2, p[0] // 2, 0, 0)),
+                pl.BlockSpec((1, held, share, width), lambda i, p: (p[1], 0, 0, 0)),
             ],
             out_specs=(
                 pl.BlockSpec((share, width), lambda i, p: (0, 0)),
                 pl.BlockSpec((width, width), lambda i, p: (0, 0)),
                 pl.BlockSpec((share, width), lambda i, p: (0, 0)),
+                pl.BlockSpec((held * share, width), lambda i, p: (0, 0)),
             ),
         ),
         compiler_params=pltpu.CompilerParams(vmem_limit_bytes=SMALL),
         cost_estimate=pl.CostEstimate(
             flops=width * width * 1000, bytes_accessed=2_000_000, transcendentals=0
         ),
-    )(place, rhs_low, inv_low, answer0)
+    )(place, rhs_low, inv_low, answer0, answer0)
+
+
+def summed_up(shares):
+    def body(shares_ref, out_ref):
+        out_ref[...] = jnp.sum(shares_ref[...].astype(F32), axis=0).astype(BF16)
+
+    return pl.pallas_call(
+        body,
+        out_shape=jax.ShapeDtypeStruct(shares.shape[1:], BF16),
+        compiler_params=pltpu.CompilerParams(vmem_limit_bytes=SMALL),
+        cost_estimate=pl.CostEstimate(flops=200_000, bytes_accessed=450_000, transcendentals=0),
+    )(shares)
 
 
 def second_level(part, right_side, inverse, first, copies):
@@ -216,35 +234,31 @@
     )(part, right_side, inverse, first)
 
 
-def ancestor_parts(place, own, near, room, before=None):
-    loads, width, count = near[0][4], near[0][1].shape[-1], near[0][5]
-    terms = len(own) + len(near)
+def ancestor_parts(place, terms, count, loads, before=None):
+    width = terms[0][1].shape[-1]
 
     def body(place_ref, *refs):
-        answers, blocks, rest = refs[:terms], refs[terms : 2 * terms], refs[2 * terms :]
+        answers, blocks, rest = refs[: len(terms)], refs[len(terms) : 2 * len(terms)], refs[2 * len(terms) :]
         total = None
-        for index in range(terms):
-            value = answers[index]
-            value = value[0].reshape(loads, width) if index < len(own) else value[...]
-            product = dot_nt(value, blocks[index][...])
+        for answer, block in zip(answers, blocks):
+            product = dot_nt(answer[...].reshape(loads, width), block[...])
             total = product if total is None else total + product
         if before is not None:
             total += rest[0][...].astype(F32)
         rest[-1][...] = total.astype(BF16)
 
-    def own_answer(answer):
-        return pl.BlockSpec((1, *answer.shape[1:]), lambda a, p: (p[1], 0, 0, 0))
-
-    def near_answer(spot):
+    def answer_spec(answer, spot):
+        if spot is None:
+            return pl.BlockSpec((1, *answer.shape[1:]), lambda a, p: (p[1], 0, 0, 0))
         return pl.BlockSpec((loads, width), lambda a, p: (spot, 0))
 
-    def block(level):
+    def block_spec(level):
         return pl.BlockSpec((width, width), lambda a, p: (level * count + a, 0))
 
     out_spec = pl.BlockSpec((loads, width), lambda a, p: (0, a))
-    in_specs = [own_answer(term[2]) for term in own] + [near_answer(term[3]) for term in near]
-    in_specs += [block(term[0]) for term in (*own, *near)]
-    operands = [term[2] for term in (*own, *near)] + [term[1] for term in (*own, *near)]
+    in_specs = [answer_spec(term[2], term[3]) for term in terms]
+    in_specs += [block_spec(term[0]) for term in terms]
+    operands = [term[2] for term in terms] + [term[1] for term in terms]
     if before is not None:
         in_specs.append(out_spec)
         operands.append(before)
@@ -254,9 +268,9 @@
         grid_spec=pltpu.PrefetchScalarGridSpec(
             num_scalar_prefetch=1, grid=(count,), in_specs=in_specs, out_specs=out_spec
         ),
-        compiler_params=pltpu.CompilerParams(vmem_limit_bytes=room),
-        cost_estimate=pl.CostEstimate(
-            flops=2 * terms * count * width * width * loads,
+        compiler_params=pltpu.CompilerParams(vmem_limit_bytes=LARGE),
+        cost_estimate=pl.CostEstimate(
+            flops=2 * len(terms) * count * width * width * loads,
             bytes_accessed=5_000_000,
             transcendentals=0,
         ),
@@ -298,7 +312,7 @@
     place = jnp.stack([lax.axis_index("row"), lax.axis_index("layer") & 1]).astype(jnp.int32)
 
     answer0, part, give = first_level(targets, rhs_low, inv_low, blocks, rows)
-    ready = prepared(place, rhs_low, inv_low, answer0, 1)
+    *ready, kept0 = prepared(place, rhs_low, inv_low, answer0, 1)
     shares = lax.all_to_all(part, "col", 0, 0, tiled=True)
 
     def neighbour(layer, row):
@@ -316,7 +330,7 @@
 
     near = swap(give)
 
-    summed = shares.astype(F32).sum(axis=0).astype(BF16)
+    summed = summed_up(shares)
     turn = [
         (row * cols + col, col * cols + (row - 1) % rows)
         for row in range(rows)
@@ -332,11 +346,10 @@
     near_answer1 = swap(lax.dynamic_index_in_dim(answer1, 1 - place[1], 0, keepdims=False))
     wanted, count = loads // 2, inv_anc.shape[0]
     near_answer1 = near_answer1.reshape(wanted, width)
-    own = [(0, give, answer0), (1, give, answer1)]
-    early = (0, near, near, near.shape[0] // wanted - 1, wanted, count)
-    late = (1, near, near_answer1, 0, wanted, count)
-    parts = ancestor_parts(place, own, [early], FIRST)
-    parts = ancestor_parts(place, [], [late], FIRST, parts)
+    own = [(0, give, kept0, 0), (1, give, answer1, None)]
+    parts = ancestor_parts(place, own, count, wanted)
+    far = [(0, near, near, near.shape[0] // wanted - 1), (1, near, near_answer1, 0)]
+    parts = ancestor_parts(place, far, count, wanted, parts)
     groups = [
         [layer * cols + col for layer in range(parity, layers, 2) for col in range(cols)]
         for parity in range(2)

time: 110 us -> 105 us (0.955)
  Pallas kernels: 19.1 us -> 14.2 us
  local copies, waits for them, and re-layouts: 1.7 us -> 3.81 us
    pallas_call x2, Pallas kernels: 10.7 us -> 4.75 us  [ancestor_parts(): pl.pallas_call(body, out_shape=jax.ShapeDtypeStruct((loads, count * width...]
    unnamed x16 -> x12, local copies, waits for them, and re-layouts: 1.68 us -> 3.79 us
  transfers between devices with their start and end apart: 5 -> 5, of which waited for: 3 -> 2; matrix products, arithmetic and copies ran while one was open for 0% -> 0% of each run, Pallas kernels for 7% -> 5%
where the time goes in v8:
time: 105 us
  blocking collectives  40.4 us (38%)
  starting transfers between devices  28.4 us (27%)
  waiting for transfers between devices  16.9 us (16%)
  Pallas kernels  14.2 us (14%)
  local copies, waits for them, and re-layouts  3.81 us (4%)
    all_to_all x1, blocking collectives, on_device(): lax.all_to_all(parts.reshape(members, parts.shape[0] // members, -1), ('l...  36.7 us
    all_to_all x1, waiting for transfers between devices, on_device(): shares = lax.all_to_all(part, 'col', 0, 0, tiled=True)  10.5 us
    ppermute x2, starting transfers between devices, swap(): return lax.ppermute(value, ('layer', 'row'), pairs)  8.28 us
    all_to_all x1, starting transfers between devices, on_device(): shares = lax.all_to_all(part, 'col', 0, 0, tiled=True)  7.56 us
    ppermute x1, starting transfers between devices, on_device(): summed = lax.ppermute(summed, ('row', 'col'), turn)  7.01 us
    all_to_all x1, waiting for transfers between devices, on_device(): lax.all_to_all(pieces, 'row', 0, 0, axis_index_groups=lines, tiled=True)  6.33 us
    all_to_all x1, starting transfers between devices, on_device(): lax.all_to_all(pieces, 'row', 0, 0, axis_index_groups=lines, tiled=True)  5.58 us
    pallas_call x1, Pallas kernels, first_level(): pl.pallas_call(body, out_shape=(jax.ShapeDtypeStruct((2, half, share, wid...  4.85 us
  transfers between devices with their start and end apart: 5, of which 2 were waited for; matrix products, arithmetic and copies ran while one was open for 0% of the time, Pallas kernels for 5%

profile of v8, /device:TPU:8, one launch (start us, length us, event | category | flops | bytes accessed | tf_op | source)
XLA Modules:
  0.0 104.5 jit_solution(3386264730772752121)
XLA Ops:
  0.6 0.0 copy-start.1
  0.6 4.8 %shard_map.77 = (bf16[2,4,64,384]{3,2,1,0:T(8,128)(2,1)}, bf16[8,64,384]{2,1,0:T(8,128)(2,1)}, bf16[3328,384]{1,0:T(8,128)(2,1)}) custom-call(s32[2,4]{1,0:T(2,128)} %bitcast.29, bf16[2,384,512]{2,1,0:T(8,128)(2,1)} %bitcast.19, bf16[2,384,384]{2,1,0:T(8,128)(2,1)} %bitcast.23, bf16[2,4,384,384]{3,2,1,0:T(8,128)(2,1)} %bitcast.27), custom_call_target="tpu_custom_call" | custom-call | flops 301989888 | bytes 2200000 | tf_op jit(solution)/shard_map/pallas_call | solution.py:123
  5.5 4.3 %collective-permute-start.1 = (bf16[3328,384]{1,0:T(8,128)(2,1)}, bf16[3328,384]{1,0:T(8,128)(2,1)S(1)}, u32[]{:S(2)}, u32[]{:S(2)}) collective-permute-start(bf16[3328,384]{1,0:T(8,128)(2,1)} %get-tuple-element.17.refs_2_.refs_3_), channel_id=1, source_target_pairs={{0,64},{8,456},{16,80},{24,472},{32,96},{40,488},{48,112},{56,504}... | collective-permute-start | bytes 7667720 | tf_op jit(solution)/shard_map/ppermute | solution.py:329
  9.8 7.6 %all-to-all-start = ((bf16[8,64,384]{2,1,0:T(8,128)(2,1)}), bf16[8,64,384]{2,1,0:T(8,128)(2,1)}, u32[]{:S(2)}, u32[]{:S(2)}) async-start(bf16[8,64,384]{2,1,0:T(8,128)(2,1)} %get-tuple-element.11), calls=%async_computation | async-start | bytes 786432 | tf_op jit(solution)/shard_map/all_to_all | solution.py:316
  17.3 10.5 %all-to-all-done.shares_ref = bf16[8,64,384]{2,1,0:T(8,128)(2,1)} async-done(((bf16[8,64,384]{2,1,0:T(8,128)(2,1)}), bf16[8,64,384]{2,1,0:T(8,128)(2,1)}, u32[]{:S(2)}, u32[]{:S(2)}) %all-to-all-start) | async-done | bytes 393248 | tf_op jit(solution)/shard_map/all_to_all | solution.py:316
  27.9 1.1 %shard_map.78 = bf16[64,384]{1,0:T(8,128)(2,1)S(1)} custom-call(bf16[8,64,384]{2,1,0:T(8,128)(2,1)} %all-to-all-done.shares_ref), custom_call_target="tpu_custom_call" | custom-call | flops 200000 | bytes 450000 | tf_op jit(solution)/shard_map/pallas_call | solution.py:205
  28.9 7.0 %collective-permute-start = (bf16[64,384]{1,0:T(8,128)(2,1)S(1)}, bf16[64,384]{1,0:T(8,128)(2,1)S(1)}, u32[]{:S(2)}, u32[]{:S(2)}) collective-permute-start(bf16[64,384]{1,0:T(8,128)(2,1)S(1)} %shard_map.78), channel_id=1, source_target_pairs={{0,7},{1,15},{2,23},{3,31},{4,39},{5,47},{6,55},{7,63},{8,0},{9,8}... | collective-permute-start | bytes 147464 | tf_op jit(solution)/shard_map/ppermute | solution.py:339
  36.0 0.1 pad_add_fusion.place_ref
  36.0 0.0 copy-done.1
  36.0 0.0 copy-start.2
  36.0 1.1 %copy-done.2 = bf16[1,2,1,384,384]{4,3,2,1,0:T(8,128)(2,1)S(1)} copy-done((bf16[1,2,1,384,384]{4,3,2,1,0:T(8,128)(2,1)S(1)}, bf16[1,2,1,384,384]{4,3,2,1,0:T(8,128)(2,1)}, u32[]{:S(2)}) %copy-start.2) | copy-done | bytes 589848
  37.1 0.0 copy-start.3
  37.1 1.0 copy-done.3
  38.1 0.7 shard_map.79
  38.8 0.0 collective-permute-done.part_ref
  38.8 0.9 shard_map.80
  39.7 5.6 %all-to-all-start.1 = ((bf16[4,64,384]{2,1,0:T(8,128)(2,1)}), bf16[4,64,384]{2,1,0:T(8,128)(2,1)S(1)}, u32[]{:S(2)}, u32[]{:S(2)}) async-start(bf16[4,64,384]{2,1,0:T(8,128)(2,1)} %get-tuple-element.18), calls=%async_computation.1 | async-start | bytes 393216 | tf_op jit(solution)/shard_map/all_to_all | solution.py:343
  45.3 6.3 %all-to-all-done.1 = bf16[4,64,384]{2,1,0:T(8,128)(2,1)S(1)} async-done(((bf16[4,64,384]{2,1,0:T(8,128)(2,1)}), bf16[4,64,384]{2,1,0:T(8,128)(2,1)S(1)}, u32[]{:S(2)}, u32[]{:S(2)}) %all-to-all-start.1) | async-done | bytes 196640 | tf_op jit(solution)/shard_map/all_to_all | solution.py:343
  51.6 3.6 %all-gather = bf16[8,64,384]{2,1,0:T(8,128)(2,1)S(1)} all-gather(bf16[4,64,384]{2,1,0:T(8,128)(2,1)S(1)} %all-to-all-done.1), channel_id=2, replica_groups={{0,8},{16,24},{32,40},{48,56},{1,9},{17,25},{33,41},{49,57},{2,10},{18,..., dimensions={0}, use_global_device_ids=true | all-gather | bytes 589824 | tf_op jit(solution)/shard_map/all_gather | solution.py:344
  55.3 4.0 %collective-permute-start.2 = (bf16[4,64,384]{2,1,0:T(8,128)(2,1)S(1)}, bf16[4,64,384]{2,1,0:T(8,128)(2,1)S(1)}, u32[]{:S(2)}, u32[]{:S(2)}) collective-permute-start(bf16[4,64,384]{2,1,0:T(8,128)(2,1)S(1)} %dynamic-slice_bitcast_fusion), channel_id=1, source_target_pairs={{0,64},{8,456},{16,80},{24,472},{32,96},{40,488},{48,112},{56,504}... | collective-permute-start | bytes 589832 | tf_op jit(solution)/shard_map/ppermute | solution.py:329
  59.3 0.0 copy-start
  59.3 1.7 %copy-done = bf16[3328,384]{1,0:T(8,128)(2,1)S(1)} copy-done((bf16[3328,384]{1,0:T(8,128)(2,1)S(1)}, bf16[3328,384]{1,0:T(8,128)(2,1)}, u32[]{:S(2)}) %copy-start) | copy-done | bytes 2555928
  61.0 2.3 %shard_map.81.refs_4_ = bf16[256,1536]{1,0:T(8,128)(2,1)S(1)} custom-call(s32[2]{0:T(128)S(1)} %pad_add_fusion.place_ref, bf16[256,384]{1,0:T(8,128)(2,1)S(1)} %get-tuple-element.19.refs_0_, bf16[2,4,64,384]{3,2,1,0:T(8,128)(2,1)S(1)} %bitcast.22, bf16[3328,384]{1,0:T(8,128)(2,1)S(1)} %copy-done, bf16[3328,384]{1,0:T(8,128)(2,1)S(1)} %copy-done), custom_call_target="tpu_custom_call" | custom-call | flops 603979776 | bytes 5000000 | tf_op jit(solution)/shard_map/pallas_call | solution.py:265
  63.3 0.0 collective-permute-done.2
  63.3 0.0 collective-permute-done.1.refs_0_.refs_2_.refs_3_
  63.4 0.0 copy-start.4
  63.4 0.0 copy-start.5
  63.4 2.4 %shard_map.82 = bf16[256,1536]{1,0:T(8,128)(2,1)S(1)} custom-call(s32[2]{0:T(128)S(1)} %pad_add_fusion.place_ref, bf16[3328,384]{1,0:T(8,128)(2,1)S(1)} %collective-permute-done.1.refs_0_.refs_2_.refs_3_, bf16[256,384]{1,0:T(8,128)(2,1)S(1)} %bitcast.25, bf16[3328,384]{1,0:T(8,128)(2,1)S(1)} %collective-permute-done.1.refs_0_.refs_2_.refs_3_, ...), custom_call_target="tpu_custom_call" | custom-call | flops 603979776 | bytes 5000000 | tf_op jit(solution)/shard_map/pallas_call | solution.py:265
  65.8 36.7 %all_to_all.15.arrived_ref = bf16[32,8,1536]{2,1,0:T(8,128)(2,1)S(1)} all-to-all(bf16[32,8,1536]{2,1,0:T(8,128)(2,1)S(1)} %bitcast.18), channel_id=1, replica_groups={{0,1,2,3,4,5,6,7,128,129,130,131,132,133,134,135,256,257,258,259,260,26..., dimensions={0} | all-to-all | bytes 1572864 | tf_op jit(solution)/shard_map/all_to_all | solution.py:358
  102.6 0.0 copy-done.4
  102.6 0.0 copy-done.5
  102.6 2.0 %shard_map.83 = f32[4,8,384]{2,1,0:T(8,128)} custom-call(bf16[32,8,1536]{2,1,0:T(8,128)(2,1)S(1)} %all_to_all.15.arrived_ref, bf16[4,8,384]{2,1,0:T(8,128)(2,1)S(1)} %bitcast.26, bf16[4,384,384]{2,1,0:T(8,128)(2,1)S(1)} %copy-done.4), custom_call_target="tpu_custom_call" | custom-call | flops 9437184 | bytes 3000000 | tf_op jit(solution)/shard_map/pallas_call | solution.py:289
  (1 shorter events, 0.0 us)
Async XLA Ops:
  0.6 35.4 %copy-start.1 = (bf16[1,2,1,384,512]{4,3,2,1,0:T(8,128)(2,1)S(1)}, bf16[1,2,1,384,512]{4,3,2,1,0:T(8,128)(2,1)}, u32[]{:S(2)}) copy-start(bf16[1,2,1,384,512]{4,3,2,1,0:T(8,128)(2,1)} %param.6) | copy-start | bytes 2359300
  5.5 57.9 %collective-permute-start.1 = (bf16[3328,384]{1,0:T(8,128)(2,1)}, bf16[3328,384]{1,0:T(8,128)(2,1)S(1)}, u32[]{:S(2)}, u32[]{:S(2)}) collective-permute-start(bf16[3328,384]{1,0:T(8,128)(2,1)} %get-tuple-element.17.refs_2_.refs_3_), channel_id=1, source_target_pairs={{0,64},{8,456},{16,80},{24,472},{32,96},{40,488},{48,112},{56,504}... | collective-permute-start | bytes 7667720 | tf_op jit(solution)/shard_map/ppermute | solution.py:329
  9.8 18.1 %all-to-all-start = ((bf16[8,64,384]{2,1,0:T(8,128)(2,1)}), bf16[8,64,384]{2,1,0:T(8,128)(2,1)}, u32[]{:S(2)}, u32[]{:S(2)}) async-start(bf16[8,64,384]{2,1,0:T(8,128)(2,1)} %get-tuple-element.11), calls=%async_computation | async-start | bytes 786432 | tf_op jit(solution)/shard_map/all_to_all | solution.py:316
  28.9 9.8 %collective-permute-start = (bf16[64,384]{1,0:T(8,128)(2,1)S(1)}, bf16[64,384]{1,0:T(8,128)(2,1)S(1)}, u32[]{:S(2)}, u32[]{:S(2)}) collective-permute-start(bf16[64,384]{1,0:T(8,128)(2,1)S(1)} %shard_map.78), channel_id=1, source_target_pairs={{0,7},{1,15},{2,23},{3,31},{4,39},{5,47},{6,55},{7,63},{8,0},{9,8}... | collective-permute-start | bytes 147464 | tf_op jit(solution)/shard_map/ppermute | solution.py:339
  36.0 1.1 %copy-start.2 = (bf16[1,2,1,384,384]{4,3,2,1,0:T(8,128)(2,1)S(1)}, bf16[1,2,1,384,384]{4,3,2,1,0:T(8,128)(2,1)}, u32[]{:S(2)}) copy-start(bf16[1,2,1,384,384]{4,3,2,1,0:T(8,128)(2,1)} %param.7) | copy-start | bytes 1769476
  37.1 1.0 copy-start.3
  39.7 11.9 %all-to-all-start.1 = ((bf16[4,64,384]{2,1,0:T(8,128)(2,1)}), bf16[4,64,384]{2,1,0:T(8,128)(2,1)S(1)}, u32[]{:S(2)}, u32[]{:S(2)}) async-start(bf16[4,64,384]{2,1,0:T(8,128)(2,1)} %get-tuple-element.18), calls=%async_computation.1 | async-start | bytes 393216 | tf_op jit(solution)/shard_map/all_to_all | solution.py:343
  55.3 8.1 %collective-permute-start.2 = (bf16[4,64,384]{2,1,0:T(8,128)(2,1)S(1)}, bf16[4,64,384]{2,1,0:T(8,128)(2,1)S(1)}, u32[]{:S(2)}, u32[]{:S(2)}) collective-permute-start(bf16[4,64,384]{2,1,0:T(8,128)(2,1)S(1)} %dynamic-slice_bitcast_fusion), channel_id=1, source_target_pairs={{0,64},{8,456},{16,80},{24,472},{32,96},{40,488},{48,112},{56,504}... | collective-permute-start | bytes 589832 | tf_op jit(solution)/shard_map/ppermute | solution.py:329
  59.3 1.7 %copy-start = (bf16[3328,384]{1,0:T(8,128)(2,1)S(1)}, bf16[3328,384]{1,0:T(8,128)(2,1)}, u32[]{:S(2)}) copy-start(bf16[3328,384]{1,0:T(8,128)(2,1)} %get-tuple-element.17.refs_2_.refs_3_) | copy-start | bytes 7667716
  63.4 39.2 %copy-start.4 = (bf16[4,384,384]{2,1,0:T(8,128)(2,1)S(1)}, bf16[4,384,384]{2,1,0:T(8,128)(2,1)}, u32[]{:S(2)}) copy-start(bf16[4,384,384]{2,1,0:T(8,128)(2,1)} %inv_ref.1) | copy-start | bytes 3538948
  63.4 39.2 %copy-start.5 = (bf16[4,384,8]{1,2,0:T(8,128)(2,1)S(1)}, bf16[4,384,8]{1,2,0:T(8,128)(2,1)}, u32[]{:S(2)}) copy-start(bf16[4,384,8]{1,2,0:T(8,128)(2,1)} %param.10) | copy-start | bytes 73732

commit v9 on v8

--- a/solution.py
+++ b/solution.py
@@ -33,12 +33,22 @@
     steps = 2
     held, half = rows // steps, rows // 2
     slots = levels * per_row
+    lanes = max(share, 128)
+    per_lanes = lanes // share
 
     def body(
-        targets_ref, rhs_ref, inv_ref, blocks_ref, answer_ref, part_ref, give_ref,
-        rhs_in, inv_in, blocks_in, zeros, half_out, in_sems, blocks_sems, out_sems,
+        targets_ref, rhs_ref, inv_ref, blocks_ref, part_ref, kept_ref, ready_ref, give_ref,
+        rhs_in, inv_in, next_in, blocks_in, zeros, half_out, in_sems, blocks_sems, out_sems,
     ):
-        kept = lax.axis_index("layer") % 2
+        kept, row = lax.axis_index("layer") % 2, lax.axis_index("row")
+        next_copy = pltpu.make_async_copy(
+            rhs_ref.at[1, :, pl.ds(pl.multiple_of(row // per_lanes * lanes, lanes), lanes)],
+            next_in,
+            in_sems.at[steps + 1],
+        )
+        next_inverse = pltpu.make_async_copy(
+            inv_ref.at[1], ready_ref.at[pl.ds(2 * share, width)], in_sems.at[steps + 2]
+        )
         inv_copy = pltpu.make_async_copy(inv_ref.at[0], inv_in, in_sems.at[steps])
         rhs_copies = [
             pltpu.make_async_copy(
@@ -72,7 +82,7 @@
                 def _(index=index):
                     pltpu.make_async_copy(zeros, give(index), out_sems.at[index]).start()
 
-        for copy in (inv_copy, *rhs_copies, *blocks_copies):
+        for copy in (inv_copy, *rhs_copies, *blocks_copies, next_copy, next_inverse):
             copy.start()
         zeros[...] = jnp.zeros_like(zeros)
         inv_copy.wait()
@@ -85,17 +95,19 @@
             answers.append(answer)
             pieces = [answer[member * share : (member + 1) * share] for member in range(held)]
             for member in range(held):
-                answer_ref[member % 2, step * (held // 2) + member // 2] = pieces[member]
-            for member in range(0, held, 2):
                 start = (step * (held // 2) + member // 2) * share
 
-                @pl.when(kept == 1)
+                @pl.when(kept == member % 2)
+                def _(start=start, piece=pieces[member]):
+                    kept_ref[start : start + share] = piece
+
+                @pl.when(kept != member % 2)
                 def _(start=start, piece=pieces[member]):
                     half_out[start : start + share] = piece
 
-                @pl.when(kept == 0)
-                def _(start=start, piece=pieces[member + 1]):
-                    half_out[start : start + share] = piece
+                @pl.when(row == step * held + member)
+                def _(piece=pieces[member]):
+                    ready_ref[share : 2 * share] = piece
 
         half_copy = pltpu.make_async_copy(
             half_out, give_ref.at[pl.ds(slots * width, half * share)], out_sems.at[slots]
@@ -115,6 +127,15 @@
         def _():
             part_ref[...] = jnp.zeros_like(part_ref)
 
+        next_copy.wait()
+        turned = next_in[...].astype(F32).T
+        picked = turned[:share]
+        for other in range(1, per_lanes):
+            picked = jnp.where(
+                row % per_lanes == other, turned[other * share : (other + 1) * share], picked
+            )
+        ready_ref[:share] = picked.astype(BF16)
+        next_inverse.wait()
         for index in range(slots):
             pltpu.make_async_copy(zeros, give(index), out_sems.at[index]).wait()
         half_copy.wait()
@@ -123,19 +144,21 @@
     return pl.pallas_call(
         body,
         out_shape=(
-            jax.ShapeDtypeStruct((2, half, share, width), BF16),
             jax.ShapeDtypeStruct((rows, share, width), BF16),
+            jax.ShapeDtypeStruct((half * share, width), BF16),
+            jax.ShapeDtypeStruct((2 * share + width, width), BF16),
             jax.ShapeDtypeStruct((slots * width + half * share, width), BF16),
         ),
         in_specs=[pl.BlockSpec(memory_space=pltpu.SMEM), any_spec, any_spec, any_spec],
-        out_specs=(vmem, vmem, any_spec),
+        out_specs=(vmem, vmem, vmem, any_spec),
         scratch_shapes=[
             pltpu.VMEM((steps, width, loads // steps), BF16),
             pltpu.VMEM((width, width), BF16),
+            pltpu.VMEM((width, lanes), BF16),
             pltpu.VMEM(blocks.shape, BF16),
             pltpu.VMEM((width, width), BF16),
             pltpu.VMEM((half * share, width), BF16),
-            pltpu.SemaphoreType.DMA((steps + 1,)),
+            pltpu.SemaphoreType.DMA((steps + 3,)),
             pltpu.SemaphoreType.DMA((levels,)),
             pltpu.SemaphoreType.DMA((slots + 1,)),
         ],
@@ -146,58 +169,6 @@
     )(targets, rhs_low, inv_low, blocks)
 
 
-def prepared(place, rhs_low, inv_low, answer0, level):
-    _, held, share, width = answer0.shape
-    lanes = max(share, 128)
-    per_lanes = lanes // share
-
-    def body(
-        place_ref, rhs_ref, inv_ref, answer0_ref, kept_ref, out_ref, inverse_ref, first_ref, half_ref
-    ):
-        turned = rhs_ref[0].astype(F32).T
-        picked = turned[:share]
-        for other in range(1, per_lanes):
-            picked = jnp.where(
-                place_ref[0] % per_lanes == other,
-                turned[other * share : (other + 1) * share],
-                picked,
-            )
-        out_ref[...] = picked.astype(BF16)
-        inverse_ref[...] = inv_ref[0]
-        first_ref[...] = answer0_ref[0, 0]
-        half_ref[...] = kept_ref[0].reshape(held * share, width)
-
-    return pl.pallas_call(
-        body,
-        out_shape=(
-            jax.ShapeDtypeStruct((share, width), BF16),
-            jax.ShapeDtypeStruct((width, width), BF16),
-            jax.ShapeDtypeStruct((share, width), BF16),
-            jax.ShapeDtypeStruct((held * share, width), BF16),
-        ),
-        grid_spec=pltpu.PrefetchScalarGridSpec(
-            num_scalar_prefetch=1,
-            grid=(1,),
-            in_specs=[
-                pl.BlockSpec((1, width, lanes), lambda i, p: (level, 0, p[0] // per_lanes)),
-                pl.BlockSpec((1, width, width), lambda i, p: (level, 0, 0)),
-                pl.BlockSpec((1, 1, share, width), lambda i, p: (p[0] % 2, p[0] // 2, 0, 0)),
-                pl.BlockSpec((1, held, share, width), lambda i, p: (p[1], 0, 0, 0)),
-            ],
-            out_specs=(
-                pl.BlockSpec((share, width), lambda i, p: (0, 0)),
-                pl.BlockSpec((width, width), lambda i, p: (0, 0)),
-                pl.BlockSpec((share, width), lambda i, p: (0, 0)),
-                pl.BlockSpec((held * share, width), lambda i, p: (0, 0)),
-            ),
-        ),
-        compiler_params=pltpu.CompilerParams(vmem_limit_bytes=SMALL),
-        cost_estimate=pl.CostEstimate(
-            flops=width * width * 1000, bytes_accessed=2_000_000, transcendentals=0
-        ),
-    )(place, rhs_low, inv_low, answer0, answer0)
-
-
 def summed_up(shares):
     def body(shares_ref, out_ref):
         out_ref[...] = jnp.sum(shares_ref[...].astype(F32), axis=0).astype(BF16)
@@ -210,15 +181,15 @@
     )(shares)
 
 
-def second_level(part, right_side, inverse, first, copies):
+def second_level(part, ready, copies):
     share, width = part.shape
 
-    def body(part_ref, rhs_ref, inv_ref, first_ref, answer_ref, both_ref):
-        residual = (rhs_ref[...].astype(F32) - part_ref[...].astype(F32)).astype(BF16)
-        answer = dot_nt(residual, inv_ref[...]).astype(BF16)
+    def body(part_ref, ready_ref, answer_ref, both_ref):
+        residual = (ready_ref[:share].astype(F32) - part_ref[...].astype(F32)).astype(BF16)
+        answer = dot_nt(residual, ready_ref[2 * share :]).astype(BF16)
         for copy in range(copies):
             answer_ref[copy] = answer
-        both_ref[0] = first_ref[...]
+        both_ref[0] = ready_ref[share : 2 * share]
         both_ref[1] = answer
 
     return pl.pallas_call(
@@ -231,7 +202,7 @@
         cost_estimate=pl.CostEstimate(
             flops=2 * width * width * share, bytes_accessed=600_000, transcendentals=0
         ),
-    )(part, right_side, inverse, first)
+    )(part, ready)
 
 
 def ancestor_parts(place, terms, count, loads, before=None):
@@ -311,8 +282,7 @@
     layers = lax.axis_size("layer")
     place = jnp.stack([lax.axis_index("row"), lax.axis_index("layer") & 1]).astype(jnp.int32)
 
-    answer0, part, give = first_level(targets, rhs_low, inv_low, blocks, rows)
-    *ready, kept0 = prepared(place, rhs_low, inv_low, answer0, 1)
+    part, kept0, ready, give = first_level(targets, rhs_low, inv_low, blocks, rows)
     shares = lax.all_to_all(part, "col", 0, 0, tiled=True)
 
     def neighbour(layer, row):
@@ -337,7 +307,7 @@
         for col in range(cols)
     ]
     summed = lax.ppermute(summed, ("row", "col"), turn)
-    pieces, both = second_level(summed, *ready, rows // 2)
+    pieces, both = second_level(summed, ready, rows // 2)
     lines = [list(range(core, rows, 2)) for core in range(2)]
     chips = [[row, row + 1] for row in range(0, rows, 2)]
     pieces = lax.all_to_all(pieces, "row", 0, 0, axis_index_groups=lines, tiled=True)

time: 105 us -> 105 us (level)
  blocking collectives: 40.4 us -> 58.9 us
  waiting for transfers between devices: 16.9 us -> 8.31 us
  starting transfers between devices: 28.4 us -> 21.3 us
  Pallas kernels: 14.2 us -> 12.6 us
  local copies, waits for them, and re-layouts: 3.81 us -> 2.75 us
    all_to_all x0 -> x1, blocking collectives: none -> 18 us  [on_device(): shares = lax.all_to_all(part, 'col', 0, 0, tiled=True)]
    all_to_all x1 -> x0, waiting for transfers between devices: 10.5 us -> none  [on_device(): shares = lax.all_to_all(part, 'col', 0, 0, tiled=True)]
    all_to_all x1 -> x0, starting transfers between devices: 7.56 us -> none  [on_device(): shares = lax.all_to_all(part, 'col', 0, 0, tiled=True)]
    ppermute x1, waiting for transfers between devices: 0.01 us -> 1.73 us  [on_device(): summed = lax.ppermute(summed, ('row', 'col'), turn)]
    all_to_all x1, starting transfers between devices: 5.58 us -> 6.97 us  [on_device(): lax.all_to_all(pieces, 'row', 0, 0, axis_index_groups=lines, tiled=True)]
    unnamed x12 -> x10, local copies, waits for them, and re-layouts: 3.79 us -> 2.73 us
    pallas_call x2 -> x1, Pallas kernels: 5.51 us -> 4.93 us  [first_level(): pl.pallas_call(body, out_shape=(jax.ShapeDtypeStruct((rows, share, width)...]
  transfers between devices with their start and end apart: 5 -> 4, of which waited for: 2 -> 3; matrix products, arithmetic and copies ran while one was open for 0% -> 0% of each run, Pallas kernels for 5% -> 3%
where the time goes in v9:
time: 105 us
  blocking collectives  58.9 us (56%)
  starting transfers between devices  21.3 us (20%)
  Pallas kernels  12.6 us (12%)
  waiting for transfers between devices  8.31 us (8%)
  local copies, waits for them, and re-layouts  2.75 us (3%)
    all_to_all x1, blocking collectives, on_device(): lax.all_to_all(parts.reshape(members, parts.shape[0] // members, -1), ('l...  36.9 us
    all_to_all x1, blocking collectives, on_device(): shares = lax.all_to_all(part, 'col', 0, 0, tiled=True)  18 us
    ppermute x2, starting transfers between devices, swap(): return lax.ppermute(value, ('layer', 'row'), pairs)  7.6 us
    all_to_all x1, starting transfers between devices, on_device(): lax.all_to_all(pieces, 'row', 0, 0, axis_index_groups=lines, tiled=True)  6.97 us
    ppermute x1, starting transfers between devices, on_device(): summed = lax.ppermute(summed, ('row', 'col'), turn)  6.71 us
    all_to_all x1, waiting for transfers between devices, on_device(): lax.all_to_all(pieces, 'row', 0, 0, axis_index_groups=lines, tiled=True)  6.33 us
    pallas_call x1, Pallas kernels, first_level(): pl.pallas_call(body, out_shape=(jax.ShapeDtypeStruct((rows, share, width)...  4.93 us
    pallas_call x2, Pallas kernels, ancestor_parts(): pl.pallas_call(body, out_shape=jax.ShapeDtypeStruct((loads, count * width...  4.73 us
  transfers between devices with their start and end apart: 4, of which 3 were waited for; matrix products, arithmetic and copies ran while one was open for 0% of the time, Pallas kernels for 3%

profile of v9, /device:TPU:8, one launch (start us, length us, event | category | flops | bytes accessed | tf_op | source)
XLA Modules:
  0.0 104.6 jit_solution(14207426309362857594)
XLA Ops:
  0.6 4.9 %shard_map.77 = (bf16[8,64,384]{2,1,0:T(8,128)(2,1)}, bf16[256,384]{1,0:T(8,128)(2,1)}, bf16[512,384]{1,0:T(8,128)(2,1)}, bf16[3328,384]{1,0:T(8,128)(2,1)}) custom-call(s32[2,4]{1,0:T(2,128)} %bitcast.27, bf16[2,384,512]{2,1,0:T(8,128)(2,1)} %bitcast.24, bf16[2,384,384]{2,1,0:T(8,128)(2,1)} %bitcast.25, bf16[2,4,384,384]{3,2,1,0:T(8,128)(2,1)} %bitcast.23), custom_call_target="tpu_custom_call" | custom-call | flops 301989888 | bytes 2200000 | tf_op jit(solution)/shard_map/pallas_call | solution.py:144
  5.6 0.0 copy-start.3
  5.6 4.4 %collective-permute-start.1 = (bf16[3328,384]{1,0:T(8,128)(2,1)}, bf16[3328,384]{1,0:T(8,128)(2,1)S(1)}, u32[]{:S(2)}, u32[]{:S(2)}) collective-permute-start(bf16[3328,384]{1,0:T(8,128)(2,1)} %get-tuple-element.11.refs_2_.refs_3_), channel_id=1, source_target_pairs={{0,64},{8,456},{16,80},{24,472},{32,96},{40,488},{48,112},{56,504}... | collective-permute-start | bytes 7667720 | tf_op jit(solution)/shard_map/ppermute | solution.py:299
  10.0 18.0 %all_to_all.15.shares_ref = bf16[8,64,384]{2,1,0:T(8,128)(2,1)S(1)} all-to-all(bf16[8,64,384]{2,1,0:T(8,128)(2,1)} %get-tuple-element.8), channel_id=1, replica_groups=mesh['layer'=8,'row'=8,'col'=8] {'col'}, dimensions={0} | all-to-all | bytes 786432 | tf_op jit(solution)/shard_map/all_to_all | solution.py:286
  28.0 0.1 shard_map.78
  28.0 6.7 %collective-permute-start = (bf16[64,384]{1,0:T(8,128)(2,1)S(1)}, bf16[64,384]{1,0:T(8,128)(2,1)S(1)}, u32[]{:S(2)}, u32[]{:S(2)}) collective-permute-start(bf16[64,384]{1,0:T(8,128)(2,1)S(1)} %shard_map.78), channel_id=1, source_target_pairs={{0,7},{1,15},{2,23},{3,31},{4,39},{5,47},{6,55},{7,63},{8,0},{9,8}... | collective-permute-start | bytes 147464 | tf_op jit(solution)/shard_map/ppermute | solution.py:309
  34.8 1.7 %collective-permute-done.part_ref = bf16[64,384]{1,0:T(8,128)(2,1)S(1)} collective-permute-done((bf16[64,384]{1,0:T(8,128)(2,1)S(1)}, bf16[64,384]{1,0:T(8,128)(2,1)S(1)}, u32[]{:S(2)}, u32[]{:S(2)}) %collective-permute-start) | collective-permute-done | bytes 49184 | tf_op jit(solution)/shard_map/ppermute | solution.py:309
  36.5 0.0 copy-start.2
  36.5 1.0 copy-done.2
  37.5 0.9 shard_map.79
  38.4 7.0 %all-to-all-start.1 = ((bf16[4,64,384]{2,1,0:T(8,128)(2,1)}), bf16[4,64,384]{2,1,0:T(8,128)(2,1)S(1)}, u32[]{:S(2)}, u32[]{:S(2)}) async-start(bf16[4,64,384]{2,1,0:T(8,128)(2,1)} %get-tuple-element.12), calls=%async_computation.1 | async-start | bytes 393216 | tf_op jit(solution)/shard_map/all_to_all | solution.py:313
  45.4 6.3 %all-to-all-done.1 = bf16[4,64,384]{2,1,0:T(8,128)(2,1)S(1)} async-done(((bf16[4,64,384]{2,1,0:T(8,128)(2,1)}), bf16[4,64,384]{2,1,0:T(8,128)(2,1)S(1)}, u32[]{:S(2)}, u32[]{:S(2)}) %all-to-all-start.1) | async-done | bytes 196640 | tf_op jit(solution)/shard_map/all_to_all | solution.py:313
  51.7 4.0 %all-gather = bf16[8,64,384]{2,1,0:T(8,128)(2,1)S(1)} all-gather(bf16[4,64,384]{2,1,0:T(8,128)(2,1)S(1)} %all-to-all-done.1), channel_id=2, replica_groups={{0,8},{16,24},{32,40},{48,56},{1,9},{17,25},{33,41},{49,57},{2,10},{18,..., dimensions={0}, use_global_device_ids=true | all-gather | bytes 589824 | tf_op jit(solution)/shard_map/all_gather | solution.py:314
  55.7 3.2 %collective-permute-start.2 = (bf16[4,64,384]{2,1,0:T(8,128)(2,1)S(1)}, bf16[4,64,384]{2,1,0:T(8,128)(2,1)S(1)}, u32[]{:S(2)}, u32[]{:S(2)}) collective-permute-start(bf16[4,64,384]{2,1,0:T(8,128)(2,1)S(1)} %dynamic-slice_bitcast_fusion), channel_id=1, source_target_pairs={{0,64},{8,456},{16,80},{24,472},{32,96},{40,488},{48,112},{56,504}... | collective-permute-start | bytes 589832 | tf_op jit(solution)/shard_map/ppermute | solution.py:299
  58.9 0.1 pad_add_fusion.place_ref
  59.0 0.0 copy-done.3
  59.0 0.0 copy-start
  59.0 1.7 %copy-done = bf16[3328,384]{1,0:T(8,128)(2,1)S(1)} copy-done((bf16[3328,384]{1,0:T(8,128)(2,1)S(1)}, bf16[3328,384]{1,0:T(8,128)(2,1)}, u32[]{:S(2)}) %copy-start) | copy-done | bytes 2555928
  60.7 2.3 %shard_map.80.refs_4_ = bf16[256,1536]{1,0:T(8,128)(2,1)S(1)} custom-call(s32[2]{0:T(128)S(1)} %pad_add_fusion.place_ref, bf16[256,384]{1,0:T(8,128)(2,1)S(1)} %copy-done.3, bf16[2,4,64,384]{3,2,1,0:T(8,128)(2,1)S(1)} %bitcast.20, bf16[3328,384]{1,0:T(8,128)(2,1)S(1)} %copy-done, bf16[3328,384]{1,0:T(8,128)(2,1)S(1)} %copy-done), custom_call_target="tpu_custom_call" | custom-call | flops 603979776 | bytes 5000000 | tf_op jit(solution)/shard_map/pallas_call | solution.py:236
  63.0 0.3 collective-permute-done.2
  63.3 0.0 collective-permute-done.1.refs_0_.refs_2_.refs_3_
  63.3 0.0 copy-start.1
  63.3 0.0 copy-start.4
  63.3 2.4 %shard_map.81 = bf16[256,1536]{1,0:T(8,128)(2,1)S(1)} custom-call(s32[2]{0:T(128)S(1)} %pad_add_fusion.place_ref, bf16[3328,384]{1,0:T(8,128)(2,1)S(1)} %collective-permute-done.1.refs_0_.refs_2_.refs_3_, bf16[256,384]{1,0:T(8,128)(2,1)S(1)} %bitcast.21, bf16[3328,384]{1,0:T(8,128)(2,1)S(1)} %collective-permute-done.1.refs_0_.refs_2_.refs_3_, ...), custom_call_target="tpu_custom_call" | custom-call | flops 603979776 | bytes 5000000 | tf_op jit(solution)/shard_map/pallas_call | solution.py:236
  65.7 36.9 %all_to_all.16.arrived_ref = bf16[32,8,1536]{2,1,0:T(8,128)(2,1)S(1)} all-to-all(bf16[32,8,1536]{2,1,0:T(8,128)(2,1)S(1)} %bitcast.18), channel_id=1, replica_groups={{0,1,2,3,4,5,6,7,128,129,130,131,132,133,134,135,256,257,258,259,260,26..., dimensions={0} | all-to-all | bytes 1572864 | tf_op jit(solution)/shard_map/all_to_all | solution.py:328
  102.6 0.0 copy-done.1
  102.6 0.0 copy-done.4
  102.6 1.9 %shard_map.82 = f32[4,8,384]{2,1,0:T(8,128)} custom-call(bf16[32,8,1536]{2,1,0:T(8,128)(2,1)S(1)} %all_to_all.16.arrived_ref, bf16[4,8,384]{2,1,0:T(8,128)(2,1)S(1)} %bitcast.22, bf16[4,384,384]{2,1,0:T(8,128)(2,1)S(1)} %copy-done.1), custom_call_target="tpu_custom_call" | custom-call | flops 9437184 | bytes 3000000 | tf_op jit(solution)/shard_map/pallas_call | solution.py:260
  (1 shorter events, 0.0 us)
Async XLA Ops:
  5.6 53.4 %copy-start.3 = (bf16[256,384]{1,0:T(8,128)(2,1)S(1)}, bf16[256,384]{1,0:T(8,128)(2,1)}, u32[]{:S(2)}) copy-start(bf16[256,384]{1,0:T(8,128)(2,1)} %get-tuple-element.13.refs_0_) | copy-start | bytes 589828
  5.6 57.7 %collective-permute-start.1 = (bf16[3328,384]{1,0:T(8,128)(2,1)}, bf16[3328,384]{1,0:T(8,128)(2,1)S(1)}, u32[]{:S(2)}, u32[]{:S(2)}) collective-permute-start(bf16[3328,384]{1,0:T(8,128)(2,1)} %get-tuple-element.11.refs_2_.refs_3_), channel_id=1, source_target_pairs={{0,64},{8,456},{16,80},{24,472},{32,96},{40,488},{48,112},{56,504}... | collective-permute-start | bytes 7667720 | tf_op jit(solution)/shard_map/ppermute | solution.py:299
  28.0 8.4 %collective-permute-start = (bf16[64,384]{1,0:T(8,128)(2,1)S(1)}, bf16[64,384]{1,0:T(8,128)(2,1)S(1)}, u32[]{:S(2)}, u32[]{:S(2)}) collective-permute-start(bf16[64,384]{1,0:T(8,128)(2,1)S(1)} %shard_map.78), channel_id=1, source_target_pairs={{0,7},{1,15},{2,23},{3,31},{4,39},{5,47},{6,55},{7,63},{8,0},{9,8}... | collective-permute-start | bytes 147464 | tf_op jit(solution)/shard_map/ppermute | solution.py:309
  36.5 1.0 copy-start.2
  38.4 13.3 %all-to-all-start.1 = ((bf16[4,64,384]{2,1,0:T(8,128)(2,1)}), bf16[4,64,384]{2,1,0:T(8,128)(2,1)S(1)}, u32[]{:S(2)}, u32[]{:S(2)}) async-start(bf16[4,64,384]{2,1,0:T(8,128)(2,1)} %get-tuple-element.12), calls=%async_computation.1 | async-start | bytes 393216 | tf_op jit(solution)/shard_map/all_to_all | solution.py:313
  55.7 7.6 %collective-permute-start.2 = (bf16[4,64,384]{2,1,0:T(8,128)(2,1)S(1)}, bf16[4,64,384]{2,1,0:T(8,128)(2,1)S(1)}, u32[]{:S(2)}, u32[]{:S(2)}) collective-permute-start(bf16[4,64,384]{2,1,0:T(8,128)(2,1)S(1)} %dynamic-slice_bitcast_fusion), channel_id=1, source_target_pairs={{0,64},{8,456},{16,80},{24,472},{32,96},{40,488},{48,112},{56,504}... | collective-permute-start | bytes 589832 | tf_op jit(solution)/shard_map/ppermute | solution.py:299
  59.0 1.7 %copy-start = (bf16[3328,384]{1,0:T(8,128)(2,1)S(1)}, bf16[3328,384]{1,0:T(8,128)(2,1)}, u32[]{:S(2)}) copy-start(bf16[3328,384]{1,0:T(8,128)(2,1)} %get-tuple-element.11.refs_2_.refs_3_) | copy-start | bytes 7667716
  63.3 39.3 %copy-start.1 = (bf16[4,384,384]{2,1,0:T(8,128)(2,1)S(1)}, bf16[4,384,384]{2,1,0:T(8,128)(2,1)}, u32[]{:S(2)}) copy-start(bf16[4,384,384]{2,1,0:T(8,128)(2,1)} %inv_ref.1) | copy-start | bytes 3538948
  63.3 39.3 %copy-start.4 = (bf16[4,384,8]{1,2,0:T(8,128)(2,1)S(1)}, bf16[4,384,8]{1,2,0:T(8,128)(2,1)}, u32[]{:S(2)}) copy-start(bf16[4,384,8]{1,2,0:T(8,128)(2,1)} %param.10) | copy-start | bytes 73732

commit v10 on v9

--- a/solution.py
+++ b/solution.py
@@ -37,8 +37,8 @@
     per_lanes = lanes // share
 
     def body(
-        targets_ref, rhs_ref, inv_ref, blocks_ref, part_ref, kept_ref, ready_ref, give_ref,
-        rhs_in, inv_in, next_in, blocks_in, zeros, half_out, in_sems, blocks_sems, out_sems,
+        lists_ref, rhs_ref, inv_ref, blocks_ref, part_ref, kept_ref, ready_ref, give_ref,
+        targets_ref, rhs_in, inv_in, next_in, blocks_in, zeros, half_out, in_sems, blocks_sems, out_sems,
     ):
         kept, row = lax.axis_index("layer") % 2, lax.axis_index("row")
         next_copy = pltpu.make_async_copy(
@@ -82,9 +82,11 @@
                 def _(index=index):
                     pltpu.make_async_copy(zeros, give(index), out_sems.at[index]).start()
 
-        for copy in (inv_copy, *rhs_copies, *blocks_copies, next_copy, next_inverse):
+        lists_copy = pltpu.make_async_copy(lists_ref, targets_ref, in_sems.at[steps + 3])
+        for copy in (inv_copy, *rhs_copies, lists_copy, *blocks_copies, next_copy, next_inverse):
             copy.start()
         zeros[...] = jnp.zeros_like(zeros)
+        lists_copy.wait()
         inv_copy.wait()
         answers = []
         for step in range(steps):
@@ -149,16 +151,17 @@
             jax.ShapeDtypeStruct((2 * share + width, width), BF16),
             jax.ShapeDtypeStruct((slots * width + half * share, width), BF16),
         ),
-        in_specs=[pl.BlockSpec(memory_space=pltpu.SMEM), any_spec, any_spec, any_spec],
+        in_specs=[any_spec] * 4,
         out_specs=(vmem, vmem, vmem, any_spec),
         scratch_shapes=[
+            pltpu.SMEM(targets.shape, targets.dtype),
             pltpu.VMEM((steps, width, loads // steps), BF16),
             pltpu.VMEM((width, width), BF16),
             pltpu.VMEM((width, lanes), BF16),
             pltpu.VMEM(blocks.shape, BF16),
             pltpu.VMEM((width, width), BF16),
             pltpu.VMEM((half * share, width), BF16),
-            pltpu.SemaphoreType.DMA((steps + 3,)),
+            pltpu.SemaphoreType.DMA((steps + 4,)),
             pltpu.SemaphoreType.DMA((levels,)),
             pltpu.SemaphoreType.DMA((slots + 1,)),
         ],
@@ -205,29 +208,27 @@
     )(part, ready)
 
 
-def ancestor_parts(place, terms, count, loads, before=None):
+def ancestor_parts(terms, count, loads, before=None):
     width = terms[0][1].shape[-1]
 
-    def body(place_ref, *refs):
+    def body(*refs):
         answers, blocks, rest = refs[: len(terms)], refs[len(terms) : 2 * len(terms)], refs[2 * len(terms) :]
         total = None
         for answer, block in zip(answers, blocks):
-            product = dot_nt(answer[...].reshape(loads, width), block[...])
+            product = dot_nt(answer[...], block[...])
             total = product if total is None else total + product
         if before is not None:
             total += rest[0][...].astype(F32)
         rest[-1][...] = total.astype(BF16)
 
-    def answer_spec(answer, spot):
-        if spot is None:
-            return pl.BlockSpec((1, *answer.shape[1:]), lambda a, p: (p[1], 0, 0, 0))
-        return pl.BlockSpec((loads, width), lambda a, p: (spot, 0))
+    def answer_spec(spot):
+        return pl.BlockSpec((loads, width), lambda a: (spot, 0))
 
     def block_spec(level):
-        return pl.BlockSpec((width, width), lambda a, p: (level * count + a, 0))
-
-    out_spec = pl.BlockSpec((loads, width), lambda a, p: (0, a))
-    in_specs = [answer_spec(term[2], term[3]) for term in terms]
+        return pl.BlockSpec((width, width), lambda a: (level * count + a, 0))
+
+    out_spec = pl.BlockSpec((loads, width), lambda a: (0, a))
+    in_specs = [answer_spec(term[3]) for term in terms]
     in_specs += [block_spec(term[0]) for term in terms]
     operands = [term[2] for term in terms] + [term[1] for term in terms]
     if before is not None:
@@ -236,16 +237,16 @@
     return pl.pallas_call(
         body,
         out_shape=jax.ShapeDtypeStruct((loads, count * width), BF16),
-        grid_spec=pltpu.PrefetchScalarGridSpec(
-            num_scalar_prefetch=1, grid=(count,), in_specs=in_specs, out_specs=out_spec
-        ),
+        grid=(count,),
+        in_specs=in_specs,
+        out_specs=out_spec,
         compiler_params=pltpu.CompilerParams(vmem_limit_bytes=LARGE),
         cost_estimate=pl.CostEstimate(
             flops=2 * len(terms) * count * width * width * loads,
             bytes_accessed=5_000_000,
             transcendentals=0,
         ),
-    )(place, *operands)
+    )(*operands)
 
 
 def ancestor_solve(arrived, rhs_anc, inv_anc):
@@ -280,7 +281,7 @@
     blocks, targets = blocks[0, 0, 0], targets[0, 0, 0]
     width, loads = rhs_low.shape[1:]
     layers = lax.axis_size("layer")
-    place = jnp.stack([lax.axis_index("row"), lax.axis_index("layer") & 1]).astype(jnp.int32)
+    kept = lax.axis_index("layer") & 1
 
     part, kept0, ready, give = first_level(targets, rhs_low, inv_low, blocks, rows)
     shares = lax.all_to_all(part, "col", 0, 0, tiled=True)
@@ -313,13 +314,20 @@
     pieces = lax.all_to_all(pieces, "row", 0, 0, axis_index_groups=lines, tiled=True)
     answer1 = lax.all_gather(pieces, "row", axis=0, axis_index_groups=chips)
 
-    near_answer1 = swap(lax.dynamic_index_in_dim(answer1, 1 - place[1], 0, keepdims=False))
     wanted, count = loads // 2, inv_anc.shape[0]
-    near_answer1 = near_answer1.reshape(wanted, width)
-    own = [(0, give, kept0, 0), (1, give, answer1, None)]
-    parts = ancestor_parts(place, own, count, wanted)
-    far = [(0, near, near, near.shape[0] // wanted - 1), (1, near, near_answer1, 0)]
-    parts = ancestor_parts(place, far, count, wanted, parts)
+
+    def half_of(parity):
+        half = lax.dynamic_index_in_dim(answer1, parity, 0, keepdims=False)
+        return half.reshape(wanted, width)
+
+    near_answer1 = swap(half_of(1 - kept))
+    early = [
+        (0, give, kept0, 0),
+        (1, give, half_of(kept), 0),
+        (0, near, near, near.shape[0] // wanted - 1),
+    ]
+    parts = ancestor_parts(early, count, wanted)
+    parts = ancestor_parts([(1, near, near_answer1, 0)], count, wanted, parts)
     groups = [
         [layer * cols + col for layer in range(parity, layers, 2) for col in range(cols)]
         for parity in range(2)

time: 105 us -> 103 us (0.981)
  Pallas kernels: 12.6 us -> 10.8 us
    pallas_call x2, Pallas kernels: 4.73 us -> 3.63 us  [ancestor_parts(): pl.pallas_call(body, out_shape=jax.ShapeDtypeStruct((loads, count * width...]
where the time goes in v10:
time: 103 us
  blocking collectives  58.8 us (57%)
  starting transfers between devices  21.3 us (21%)
  Pallas kernels  10.8 us (10%)
  waiting for transfers between devices  8.42 us (8%)
  local copies, waits for them, and re-layouts  2.77 us (3%)
    all_to_all x1, blocking collectives, on_device(): lax.all_to_all(parts.reshape(members, parts.shape[0] // members, -1), ('l...  36.8 us
    all_to_all x1, blocking collectives, on_device(): shares = lax.all_to_all(part, 'col', 0, 0, tiled=True)  18 us
    ppermute x2, starting transfers between devices, swap(): return lax.ppermute(value, ('layer', 'row'), pairs)  7.6 us
    all_to_all x1, starting transfers between devices, on_device(): lax.all_to_all(pieces, 'row', 0, 0, axis_index_groups=lines, tiled=True)  6.98 us
    ppermute x1, starting transfers between devices, on_device(): summed = lax.ppermute(summed, ('row', 'col'), turn)  6.71 us
    all_to_all x1, waiting for transfers between devices, on_device(): lax.all_to_all(pieces, 'row', 0, 0, axis_index_groups=lines, tiled=True)  6.33 us
    pallas_call x1, Pallas kernels, first_level(): pl.pallas_call(body, out_shape=(jax.ShapeDtypeStruct((rows, share, width)...  4.24 us
    all_gather x1, blocking collectives, on_device(): answer1 = lax.all_gather(pieces, 'row', axis=0, axis_index_groups=chips)  3.97 us
  transfers between devices with their start and end apart: 4, of which 3 were waited for; matrix products, arithmetic and copies ran while one was open for 0% of the time, Pallas kernels for 3%

profile of v10, /device:TPU:8, one launch (start us, length us, event | category | flops | bytes accessed | tf_op | source)
XLA Modules:
  0.0 102.8 jit_solution(1337275838192911603)
XLA Ops:
  0.6 4.2 %shard_map.77 = (bf16[8,64,384]{2,1,0:T(8,128)(2,1)}, bf16[256,384]{1,0:T(8,128)(2,1)}, bf16[512,384]{1,0:T(8,128)(2,1)}, bf16[3328,384]{1,0:T(8,128)(2,1)}) custom-call(s32[2,4]{1,0:T(2,128)} %bitcast.24, bf16[2,384,512]{2,1,0:T(8,128)(2,1)} %bitcast.20, bf16[2,384,384]{2,1,0:T(8,128)(2,1)} %bitcast.21, bf16[2,4,384,384]{3,2,1,0:T(8,128)(2,1)} %bitcast.18), custom_call_target="tpu_custom_call" | custom-call | flops 301989888 | bytes 2200000 | tf_op jit(solution)/shard_map/pallas_call | solution.py:146
  4.9 0.0 copy-start.3
  4.9 4.4 %collective-permute-start.2 = (bf16[3328,384]{1,0:T(8,128)(2,1)}, bf16[3328,384]{1,0:T(8,128)(2,1)S(1)}, u32[]{:S(2)}, u32[]{:S(2)}) collective-permute-start(bf16[3328,384]{1,0:T(8,128)(2,1)} %get-tuple-element.12.refs_3_.refs_4_), channel_id=1, source_target_pairs={{0,64},{8,456},{16,80},{24,472},{32,96},{40,488},{48,112},{56,504}... | collective-permute-start | bytes 7667720 | tf_op jit(solution)/shard_map/ppermute | solution.py:300
  9.3 18.0 %all_to_all.15.shares_ref = bf16[8,64,384]{2,1,0:T(8,128)(2,1)S(1)} all-to-all(bf16[8,64,384]{2,1,0:T(8,128)(2,1)} %get-tuple-element.8), channel_id=1, replica_groups=mesh['layer'=8,'row'=8,'col'=8] {'col'}, dimensions={0} | all-to-all | bytes 786432 | tf_op jit(solution)/shard_map/all_to_all | solution.py:287
  27.3 0.1 shard_map.78
  27.4 6.7 %collective-permute-start = (bf16[64,384]{1,0:T(8,128)(2,1)S(1)}, bf16[64,384]{1,0:T(8,128)(2,1)S(1)}, u32[]{:S(2)}, u32[]{:S(2)}) collective-permute-start(bf16[64,384]{1,0:T(8,128)(2,1)S(1)} %shard_map.78), channel_id=1, source_target_pairs={{0,7},{1,15},{2,23},{3,31},{4,39},{5,47},{6,55},{7,63},{8,0},{9,8}... | collective-permute-start | bytes 147464 | tf_op jit(solution)/shard_map/ppermute | solution.py:310
  34.1 1.7 %collective-permute-done.part_ref = bf16[64,384]{1,0:T(8,128)(2,1)S(1)} collective-permute-done((bf16[64,384]{1,0:T(8,128)(2,1)S(1)}, bf16[64,384]{1,0:T(8,128)(2,1)S(1)}, u32[]{:S(2)}, u32[]{:S(2)}) %collective-permute-start) | collective-permute-done | bytes 49184 | tf_op jit(solution)/shard_map/ppermute | solution.py:310
  35.8 0.0 copy-start.2
  35.8 1.0 copy-done.2
  36.8 0.9 shard_map.79
  37.7 7.0 %all-to-all-start.1 = ((bf16[4,64,384]{2,1,0:T(8,128)(2,1)}), bf16[4,64,384]{2,1,0:T(8,128)(2,1)S(1)}, u32[]{:S(2)}, u32[]{:S(2)}) async-start(bf16[4,64,384]{2,1,0:T(8,128)(2,1)} %get-tuple-element.11), calls=%async_computation.1 | async-start | bytes 393216 | tf_op jit(solution)/shard_map/all_to_all | solution.py:314
  44.7 6.3 %all-to-all-done.1 = bf16[4,64,384]{2,1,0:T(8,128)(2,1)S(1)} async-done(((bf16[4,64,384]{2,1,0:T(8,128)(2,1)}), bf16[4,64,384]{2,1,0:T(8,128)(2,1)S(1)}, u32[]{:S(2)}, u32[]{:S(2)}) %all-to-all-start.1) | async-done | bytes 196640 | tf_op jit(solution)/shard_map/all_to_all | solution.py:314
  51.1 4.0 %all-gather = bf16[8,64,384]{2,1,0:T(8,128)(2,1)S(1)} all-gather(bf16[4,64,384]{2,1,0:T(8,128)(2,1)S(1)} %all-to-all-done.1), channel_id=2, replica_groups={{0,8},{16,24},{32,40},{48,56},{1,9},{17,25},{33,41},{49,57},{2,10},{18,..., dimensions={0}, use_global_device_ids=true | all-gather | bytes 589824 | tf_op jit(solution)/shard_map/all_gather | solution.py:315
  55.1 3.2 %collective-permute-start.1 = (bf16[256,384]{1,0:T(8,128)(2,1)S(1)}, bf16[256,384]{1,0:T(8,128)(2,1)S(1)}, u32[]{:S(2)}, u32[]{:S(2)}) collective-permute-start(bf16[256,384]{1,0:T(8,128)(2,1)S(1)} %bitcast.22), channel_id=1, source_target_pairs={{0,64},{8,456},{16,80},{24,472},{32,96},{40,488},{48,112},{56,504}... | collective-permute-start | bytes 589832 | tf_op jit(solution)/shard_map/ppermute | solution.py:300
  58.3 0.0 collective-permute-done.2.refs_2_.refs_5_.refs_1_
  58.3 0.0 copy-done.3
  58.3 0.0 copy-start
  58.3 1.7 %copy-done = bf16[3328,384]{1,0:T(8,128)(2,1)S(1)} copy-done((bf16[3328,384]{1,0:T(8,128)(2,1)S(1)}, bf16[3328,384]{1,0:T(8,128)(2,1)}, u32[]{:S(2)}) %copy-start) | copy-done | bytes 2555928
  60.0 2.2 %shard_map.80.refs_2_ = bf16[256,1536]{1,0:T(8,128)(2,1)S(1)} custom-call(bf16[256,384]{1,0:T(8,128)(2,1)S(1)} %copy-done.3, bf16[256,384]{1,0:T(8,128)(2,1)S(1)} %bitcast.16, bf16[3328,384]{1,0:T(8,128)(2,1)S(1)} %collective-permute-done.2.refs_2_.refs_5_.refs_1_, bf16[3328,384]{1,0:T(8,128)(2,1)S(1)} %copy-done, bf16[3328,384]{1,0:T(8,128)(2,1)S(1)} %copy-done, ...), custom_call_target="tpu_custom_call" | custom-call | flops 905969664 | bytes 5000000 | tf_op jit(solution)/shard_map/pallas_call | solution.py:237
  62.2 0.0 copy-start.1
  62.3 0.0 copy-start.4
  62.3 0.4 collective-permute-done.1.refs_0_
  62.6 1.4 %shard_map.81 = bf16[256,1536]{1,0:T(8,128)(2,1)S(1)} custom-call(bf16[256,384]{1,0:T(8,128)(2,1)S(1)} %collective-permute-done.1.refs_0_, bf16[3328,384]{1,0:T(8,128)(2,1)S(1)} %collective-permute-done.2.refs_2_.refs_5_.refs_1_, bf16[256,1536]{1,0:T(8,128)(2,1)S(1)} %shard_map.80.refs_2_), custom_call_target="tpu_custom_call" | custom-call | flops 301989888 | bytes 5000000 | tf_op jit(solution)/shard_map/pallas_call | solution.py:237
  64.0 36.8 %all_to_all.16.arrived_ref = bf16[32,8,1536]{2,1,0:T(8,128)(2,1)S(1)} all-to-all(bf16[32,8,1536]{2,1,0:T(8,128)(2,1)S(1)} %bitcast.15), channel_id=1, replica_groups={{0,1,2,3,4,5,6,7,128,129,130,131,132,133,134,135,256,257,258,259,260,26..., dimensions={0} | all-to-all | bytes 1572864 | tf_op jit(solution)/shard_map/all_to_all | solution.py:336
  100.9 0.0 copy-done.1
  100.9 0.0 copy-done.4
  100.9 1.9 %shard_map.82 = f32[4,8,384]{2,1,0:T(8,128)} custom-call(bf16[32,8,1536]{2,1,0:T(8,128)(2,1)S(1)} %all_to_all.16.arrived_ref, bf16[4,8,384]{2,1,0:T(8,128)(2,1)S(1)} %bitcast.17, bf16[4,384,384]{2,1,0:T(8,128)(2,1)S(1)} %copy-done.1), custom_call_target="tpu_custom_call" | custom-call | flops 9437184 | bytes 3000000 | tf_op jit(solution)/shard_map/pallas_call | solution.py:261
  (1 shorter events, 0.0 us)
Async XLA Ops:
  4.9 53.4 %copy-start.3 = (bf16[256,384]{1,0:T(8,128)(2,1)S(1)}, bf16[256,384]{1,0:T(8,128)(2,1)}, u32[]{:S(2)}) copy-start(bf16[256,384]{1,0:T(8,128)(2,1)} %get-tuple-element.13.refs_0_) | copy-start | bytes 589828
  4.9 53.4 %collective-permute-start.2 = (bf16[3328,384]{1,0:T(8,128)(2,1)}, bf16[3328,384]{1,0:T(8,128)(2,1)S(1)}, u32[]{:S(2)}, u32[]{:S(2)}) collective-permute-start(bf16[3328,384]{1,0:T(8,128)(2,1)} %get-tuple-element.12.refs_3_.refs_4_), channel_id=1, source_target_pairs={{0,64},{8,456},{16,80},{24,472},{32,96},{40,488},{48,112},{56,504}... | collective-permute-start | bytes 7667720 | tf_op jit(solution)/shard_map/ppermute | solution.py:300
  27.4 8.4 %collective-permute-start = (bf16[64,384]{1,0:T(8,128)(2,1)S(1)}, bf16[64,384]{1,0:T(8,128)(2,1)S(1)}, u32[]{:S(2)}, u32[]{:S(2)}) collective-permute-start(bf16[64,384]{1,0:T(8,128)(2,1)S(1)} %shard_map.78), channel_id=1, source_target_pairs={{0,7},{1,15},{2,23},{3,31},{4,39},{5,47},{6,55},{7,63},{8,0},{9,8}... | collective-permute-start | bytes 147464 | tf_op jit(solution)/shard_map/ppermute | solution.py:310
  35.8 1.0 copy-start.2
  37.7 13.3 %all-to-all-start.1 = ((bf16[4,64,384]{2,1,0:T(8,128)(2,1)}), bf16[4,64,384]{2,1,0:T(8,128)(2,1)S(1)}, u32[]{:S(2)}, u32[]{:S(2)}) async-start(bf16[4,64,384]{2,1,0:T(8,128)(2,1)} %get-tuple-element.11), calls=%async_computation.1 | async-start | bytes 393216 | tf_op jit(solution)/shard_map/all_to_all | solution.py:314
  55.1 7.6 %collective-permute-start.1 = (bf16[256,384]{1,0:T(8,128)(2,1)S(1)}, bf16[256,384]{1,0:T(8,128)(2,1)S(1)}, u32[]{:S(2)}, u32[]{:S(2)}) collective-permute-start(bf16[256,384]{1,0:T(8,128)(2,1)S(1)} %bitcast.22), channel_id=1, source_target_pairs={{0,64},{8,456},{16,80},{24,472},{32,96},{40,488},{48,112},{56,504}... | collective-permute-start | bytes 589832 | tf_op jit(solution)/shard_map/ppermute | solution.py:300
  58.3 1.7 %copy-start = (bf16[3328,384]{1,0:T(8,128)(2,1)S(1)}, bf16[3328,384]{1,0:T(8,128)(2,1)}, u32[]{:S(2)}) copy-start(bf16[3328,384]{1,0:T(8,128)(2,1)} %get-tuple-element.12.refs_3_.refs_4_) | copy-start | bytes 7667716
  62.2 38.6 %copy-start.1 = (bf16[4,384,384]{2,1,0:T(8,128)(2,1)S(1)}, bf16[4,384,384]{2,1,0:T(8,128)(2,1)}, u32[]{:S(2)}) copy-start(bf16[4,384,384]{2,1,0:T(8,128)(2,1)} %inv_ref.1) | copy-start | bytes 3538948
  62.3 38.6 %copy-start.4 = (bf16[4,384,8]{1,2,0:T(8,128)(2,1)S(1)}, bf16[4,384,8]{1,2,0:T(8,128)(2,1)}, u32[]{:S(2)}) copy-start(bf16[4,384,8]{1,2,0:T(8,128)(2,1)} %param.10) | copy-start | bytes 73732

commit v11 on v10

--- a/solution.py
+++ b/solution.py
@@ -210,36 +210,37 @@
 
 def ancestor_parts(terms, count, loads, before=None):
     width = terms[0][1].shape[-1]
+    arrays = []
+    for _, blocks, answer, _ in terms:
+        arrays += [array for array in (blocks, answer) if all(array is not held for held in arrays)]
+    places = [
+        [next(i for i, held in enumerate(arrays) if held is array) for array in term[1:3]]
+        for term in terms
+    ]
 
     def body(*refs):
-        answers, blocks, rest = refs[: len(terms)], refs[len(terms) : 2 * len(terms)], refs[2 * len(terms) :]
-        total = None
-        for answer, block in zip(answers, blocks):
-            product = dot_nt(answer[...], block[...])
-            total = product if total is None else total + product
-        if before is not None:
-            total += rest[0][...].astype(F32)
-        rest[-1][...] = total.astype(BF16)
-
-    def answer_spec(spot):
-        return pl.BlockSpec((loads, width), lambda a: (spot, 0))
-
-    def block_spec(level):
-        return pl.BlockSpec((width, width), lambda a: (level * count + a, 0))
-
-    out_spec = pl.BlockSpec((loads, width), lambda a: (0, a))
-    in_specs = [answer_spec(term[3]) for term in terms]
-    in_specs += [block_spec(term[0]) for term in terms]
-    operands = [term[2] for term in terms] + [term[1] for term in terms]
-    if before is not None:
-        in_specs.append(out_spec)
-        operands.append(before)
+        out_ref = refs[-1]
+        for ancestor in range(count):
+            columns = slice(ancestor * width, (ancestor + 1) * width)
+            total = None
+            for (level, _, _, spot), (blocks, answer) in zip(terms, places):
+                start = (level * count + ancestor) * width
+                product = dot_nt(
+                    refs[answer][spot * loads : (spot + 1) * loads],
+                    refs[blocks][start : start + width],
+                )
+                total = product if total is None else total + product
+            if before is not None:
+                total += refs[len(arrays)][:, columns].astype(F32)
+            out_ref[:, columns] = total.astype(BF16)
+
+    operands = arrays if before is None else [*arrays, before]
+    vmem = pl.BlockSpec(memory_space=pltpu.VMEM)
     return pl.pallas_call(
         body,
         out_shape=jax.ShapeDtypeStruct((loads, count * width), BF16),
-        grid=(count,),
-        in_specs=in_specs,
-        out_specs=out_spec,
+        in_specs=[vmem] * len(operands),
+        out_specs=vmem,
         compiler_params=pltpu.CompilerParams(vmem_limit_bytes=LARGE),
         cost_estimate=pl.CostEstimate(
             flops=2 * len(terms) * count * width * width * loads,
@@ -254,20 +255,18 @@
     count, _, width = rhs_anc.shape
 
     def body(arrived_ref, rhs_ref, inv_ref, out_ref):
-        total = jnp.sum(arrived_ref[...].astype(F32), axis=0)
-        residual = (rhs_ref[0].astype(F32) - total).astype(BF16)
-        out_ref[0] = dot_nt(residual, inv_ref[0])
-
+        for ancestor in range(count):
+            columns = slice(ancestor * width, (ancestor + 1) * width)
+            total = jnp.sum(arrived_ref[:, :, columns].astype(F32), axis=0)
+            residual = (rhs_ref[ancestor].astype(F32) - total).astype(BF16)
+            out_ref[ancestor] = dot_nt(residual, inv_ref[ancestor])
+
+    vmem = pl.BlockSpec(memory_space=pltpu.VMEM)
     return pl.pallas_call(
         body,
         out_shape=jax.ShapeDtypeStruct((count, loads, width), F32),
-        grid=(count,),
-        in_specs=[
-            pl.BlockSpec((sources, loads, width), lambda a: (0, 0, a)),
-            pl.BlockSpec((1, loads, width), lambda a: (a, 0, 0)),
-            pl.BlockSpec((1, width, width), lambda a: (a, 0, 0)),
-        ],
-        out_specs=pl.BlockSpec((1, loads, width), lambda a: (a, 0, 0)),
+        in_specs=[vmem] * 3,
+        out_specs=vmem,
         compiler_params=pltpu.CompilerParams(vmem_limit_bytes=LARGE),
         cost_estimate=pl.CostEstimate(
             flops=2 * count * width * width * loads, bytes_accessed=3_000_000, transcendentals=0

time: 103 us -> 102 us (level)
  Pallas kernels: 10.8 us -> 8.73 us
    pallas_call x2, Pallas kernels: 3.63 us -> 2.4 us  [ancestor_parts(): pl.pallas_call(body, out_shape=jax.ShapeDtypeStruct((loads, count * width...]
where the time goes in v11:
time: 102 us; the launch traced here: 101 us
  blocking collectives  58.9 us (58%)
  starting transfers between devices  21.3 us (21%)
  waiting for transfers between devices  8.96 us (9%)
  Pallas kernels  8.73 us (9%)
  local copies, waits for them, and re-layouts  2.77 us (3%)
    all_to_all x1, blocking collectives, on_device(): lax.all_to_all(parts.reshape(members, parts.shape[0] // members, -1), ('l...  36.9 us
    all_to_all x1, blocking collectives, on_device(): shares = lax.all_to_all(part, 'col', 0, 0, tiled=True)  18 us
    ppermute x2, starting transfers between devices, swap(): return lax.ppermute(value, ('layer', 'row'), pairs)  7.6 us
    all_to_all x1, starting transfers between devices, on_device(): lax.all_to_all(pieces, 'row', 0, 0, axis_index_groups=lines, tiled=True)  6.98 us
    ppermute x1, starting transfers between devices, on_device(): summed = lax.ppermute(summed, ('row', 'col'), turn)  6.71 us
    all_to_all x1, waiting for transfers between devices, on_device(): lax.all_to_all(pieces, 'row', 0, 0, axis_index_groups=lines, tiled=True)  6.33 us
    pallas_call x1, Pallas kernels, first_level(): pl.pallas_call(body, out_shape=(jax.ShapeDtypeStruct((rows, share, width)...  4.24 us
    all_gather x1, blocking collectives, on_device(): answer1 = lax.all_gather(pieces, 'row', axis=0, axis_index_groups=chips)  3.97 us
  transfers between devices with their start and end apart: 4, of which 3 were waited for; matrix products, arithmetic and copies ran while one was open for 0% of the time, Pallas kernels for 3%

profile of v11, /device:TPU:8, one launch (start us, length us, event | category | flops | bytes accessed | tf_op | source)
XLA Modules:
  0.0 101.4 jit_solution(3962751530603671212)
XLA Ops:
  0.6 4.2 %shard_map.77 = (bf16[8,64,384]{2,1,0:T(8,128)(2,1)}, bf16[256,384]{1,0:T(8,128)(2,1)}, bf16[512,384]{1,0:T(8,128)(2,1)}, bf16[3328,384]{1,0:T(8,128)(2,1)}) custom-call(s32[2,4]{1,0:T(2,128)} %bitcast.24, bf16[2,384,512]{2,1,0:T(8,128)(2,1)} %bitcast.20, bf16[2,384,384]{2,1,0:T(8,128)(2,1)} %bitcast.21, bf16[2,4,384,384]{3,2,1,0:T(8,128)(2,1)} %bitcast.18), custom_call_target="tpu_custom_call" | custom-call | flops 301989888 | bytes 2200000 | tf_op jit(solution)/shard_map/pallas_call | solution.py:146
  4.9 0.0 copy-start.3
  4.9 4.4 %collective-permute-start.1 = (bf16[3328,384]{1,0:T(8,128)(2,1)}, bf16[3328,384]{1,0:T(8,128)(2,1)S(1)}, u32[]{:S(2)}, u32[]{:S(2)}) collective-permute-start(bf16[3328,384]{1,0:T(8,128)(2,1)} %get-tuple-element.11.refs_0_), channel_id=1, source_target_pairs={{0,64},{8,456},{16,80},{24,472},{32,96},{40,488},{48,112},{56,504}... | collective-permute-start | bytes 7667720 | tf_op jit(solution)/shard_map/ppermute | solution.py:299
  9.3 18.0 %all_to_all.15.shares_ref = bf16[8,64,384]{2,1,0:T(8,128)(2,1)S(1)} all-to-all(bf16[8,64,384]{2,1,0:T(8,128)(2,1)} %get-tuple-element.8), channel_id=1, replica_groups=mesh['layer'=8,'row'=8,'col'=8] {'col'}, dimensions={0} | all-to-all | bytes 786432 | tf_op jit(solution)/shard_map/all_to_all | solution.py:286
  27.3 0.1 shard_map.78
  27.4 6.7 %collective-permute-start = (bf16[64,384]{1,0:T(8,128)(2,1)S(1)}, bf16[64,384]{1,0:T(8,128)(2,1)S(1)}, u32[]{:S(2)}, u32[]{:S(2)}) collective-permute-start(bf16[64,384]{1,0:T(8,128)(2,1)S(1)} %shard_map.78), channel_id=1, source_target_pairs={{0,7},{1,15},{2,23},{3,31},{4,39},{5,47},{6,55},{7,63},{8,0},{9,8}... | collective-permute-start | bytes 147464 | tf_op jit(solution)/shard_map/ppermute | solution.py:309
  34.1 1.7 %collective-permute-done.part_ref = bf16[64,384]{1,0:T(8,128)(2,1)S(1)} collective-permute-done((bf16[64,384]{1,0:T(8,128)(2,1)S(1)}, bf16[64,384]{1,0:T(8,128)(2,1)S(1)}, u32[]{:S(2)}, u32[]{:S(2)}) %collective-permute-start) | collective-permute-done | bytes 49184 | tf_op jit(solution)/shard_map/ppermute | solution.py:309
  35.8 0.0 copy-start.2
  35.8 1.0 copy-done.2
  36.8 0.9 shard_map.79
  37.7 7.0 %all-to-all-start.1 = ((bf16[4,64,384]{2,1,0:T(8,128)(2,1)}), bf16[4,64,384]{2,1,0:T(8,128)(2,1)S(1)}, u32[]{:S(2)}, u32[]{:S(2)}) async-start(bf16[4,64,384]{2,1,0:T(8,128)(2,1)} %get-tuple-element.12), calls=%async_computation.1 | async-start | bytes 393216 | tf_op jit(solution)/shard_map/all_to_all | solution.py:313
  44.7 6.3 %all-to-all-done.1 = bf16[4,64,384]{2,1,0:T(8,128)(2,1)S(1)} async-done(((bf16[4,64,384]{2,1,0:T(8,128)(2,1)}), bf16[4,64,384]{2,1,0:T(8,128)(2,1)S(1)}, u32[]{:S(2)}, u32[]{:S(2)}) %all-to-all-start.1) | async-done | bytes 196640 | tf_op jit(solution)/shard_map/all_to_all | solution.py:313
  51.1 4.0 %all-gather = bf16[8,64,384]{2,1,0:T(8,128)(2,1)S(1)} all-gather(bf16[4,64,384]{2,1,0:T(8,128)(2,1)S(1)} %all-to-all-done.1), channel_id=2, replica_groups={{0,8},{16,24},{32,40},{48,56},{1,9},{17,25},{33,41},{49,57},{2,10},{18,..., dimensions={0}, use_global_device_ids=true | all-gather | bytes 589824 | tf_op jit(solution)/shard_map/all_gather | solution.py:314
  55.1 3.2 %collective-permute-start.2 = (bf16[256,384]{1,0:T(8,128)(2,1)S(1)}, bf16[256,384]{1,0:T(8,128)(2,1)S(1)}, u32[]{:S(2)}, u32[]{:S(2)}) collective-permute-start(bf16[256,384]{1,0:T(8,128)(2,1)S(1)} %bitcast.22), channel_id=1, source_target_pairs={{0,64},{8,456},{16,80},{24,472},{32,96},{40,488},{48,112},{56,504}... | collective-permute-start | bytes 589832 | tf_op jit(solution)/shard_map/ppermute | solution.py:299
  58.3 0.0 collective-permute-done.1.refs_3_.refs_4_.refs_0_
  58.3 0.0 copy-done.3
  58.3 0.0 copy-start
  58.3 1.7 %copy-done = bf16[3328,384]{1,0:T(8,128)(2,1)S(1)} copy-done((bf16[3328,384]{1,0:T(8,128)(2,1)S(1)}, bf16[3328,384]{1,0:T(8,128)(2,1)}, u32[]{:S(2)}) %copy-start) | copy-done | bytes 2555928
  60.0 1.7 %shard_map.80.refs_2_ = bf16[256,1536]{1,0:T(8,128)(2,1)S(1)} custom-call(bf16[3328,384]{1,0:T(8,128)(2,1)S(1)} %copy-done, bf16[256,384]{1,0:T(8,128)(2,1)S(1)} %copy-done.3, bf16[256,384]{1,0:T(8,128)(2,1)S(1)} %bitcast.16, bf16[3328,384]{1,0:T(8,128)(2,1)S(1)} %collective-permute-done.1.refs_3_.refs_4_.refs_0_, ...), custom_call_target="tpu_custom_call" | custom-call | flops 905969664 | bytes 5000000 | tf_op jit(solution)/shard_map/pallas_call | solution.py:239
  61.7 0.0 copy-start.1
  61.7 0.0 copy-start.4
  61.7 0.9 collective-permute-done.2.refs_1_
  62.6 0.7 shard_map.81
  63.3 36.9 %all_to_all.16.arrived_ref = bf16[32,8,1536]{2,1,0:T(8,128)(2,1)S(1)} all-to-all(bf16[32,8,1536]{2,1,0:T(8,128)(2,1)S(1)} %bitcast.15), channel_id=1, replica_groups={{0,1,2,3,4,5,6,7,128,129,130,131,132,133,134,135,256,257,258,259,260,26..., dimensions={0} | all-to-all | bytes 1572864 | tf_op jit(solution)/shard_map/all_to_all | solution.py:335
  100.3 0.0 copy-done.1
  100.3 0.0 copy-done.4
  100.3 1.1 %shard_map.82 = f32[4,8,384]{2,1,0:T(8,128)} custom-call(bf16[32,8,1536]{2,1,0:T(8,128)(2,1)S(1)} %all_to_all.16.arrived_ref, bf16[4,8,384]{2,1,0:T(8,128)(2,1)S(1)} %bitcast.17, bf16[4,384,384]{2,1,0:T(8,128)(2,1)S(1)} %copy-done.1), custom_call_target="tpu_custom_call" | custom-call | flops 9437184 | bytes 3000000 | tf_op jit(solution)/shard_map/pallas_call | solution.py:265
  (1 shorter events, 0.0 us)
Async XLA Ops:
  4.9 53.4 %copy-start.3 = (bf16[256,384]{1,0:T(8,128)(2,1)S(1)}, bf16[256,384]{1,0:T(8,128)(2,1)}, u32[]{:S(2)}) copy-start(bf16[256,384]{1,0:T(8,128)(2,1)} %get-tuple-element.13.refs_1_) | copy-start | bytes 589828
  4.9 53.4 %collective-permute-start.1 = (bf16[3328,384]{1,0:T(8,128)(2,1)}, bf16[3328,384]{1,0:T(8,128)(2,1)S(1)}, u32[]{:S(2)}, u32[]{:S(2)}) collective-permute-start(bf16[3328,384]{1,0:T(8,128)(2,1)} %get-tuple-element.11.refs_0_), channel_id=1, source_target_pairs={{0,64},{8,456},{16,80},{24,472},{32,96},{40,488},{48,112},{56,504}... | collective-permute-start | bytes 7667720 | tf_op jit(solution)/shard_map/ppermute | solution.py:299
  27.4 8.4 %collective-permute-start = (bf16[64,384]{1,0:T(8,128)(2,1)S(1)}, bf16[64,384]{1,0:T(8,128)(2,1)S(1)}, u32[]{:S(2)}, u32[]{:S(2)}) collective-permute-start(bf16[64,384]{1,0:T(8,128)(2,1)S(1)} %shard_map.78), channel_id=1, source_target_pairs={{0,7},{1,15},{2,23},{3,31},{4,39},{5,47},{6,55},{7,63},{8,0},{9,8}... | collective-permute-start | bytes 147464 | tf_op jit(solution)/shard_map/ppermute | solution.py:309
  35.8 1.0 copy-start.2
  37.7 13.3 %all-to-all-start.1 = ((bf16[4,64,384]{2,1,0:T(8,128)(2,1)}), bf16[4,64,384]{2,1,0:T(8,128)(2,1)S(1)}, u32[]{:S(2)}, u32[]{:S(2)}) async-start(bf16[4,64,384]{2,1,0:T(8,128)(2,1)} %get-tuple-element.12), calls=%async_computation.1 | async-start | bytes 393216 | tf_op jit(solution)/shard_map/all_to_all | solution.py:313
  55.1 7.6 %collective-permute-start.2 = (bf16[256,384]{1,0:T(8,128)(2,1)S(1)}, bf16[256,384]{1,0:T(8,128)(2,1)S(1)}, u32[]{:S(2)}, u32[]{:S(2)}) collective-permute-start(bf16[256,384]{1,0:T(8,128)(2,1)S(1)} %bitcast.22), channel_id=1, source_target_pairs={{0,64},{8,456},{16,80},{24,472},{32,96},{40,488},{48,112},{56,504}... | collective-permute-start | bytes 589832 | tf_op jit(solution)/shard_map/ppermute | solution.py:299
  58.3 1.7 %copy-start = (bf16[3328,384]{1,0:T(8,128)(2,1)S(1)}, bf16[3328,384]{1,0:T(8,128)(2,1)}, u32[]{:S(2)}) copy-start(bf16[3328,384]{1,0:T(8,128)(2,1)} %get-tuple-element.11.refs_0_) | copy-start | bytes 7667716
  61.7 38.5 %copy-start.1 = (bf16[4,384,384]{2,1,0:T(8,128)(2,1)S(1)}, bf16[4,384,384]{2,1,0:T(8,128)(2,1)}, u32[]{:S(2)}) copy-start(bf16[4,384,384]{2,1,0:T(8,128)(2,1)} %inv_ref.1) | copy-start | bytes 3538948
  61.7 38.5 %copy-start.4 = (bf16[4,384,8]{1,2,0:T(8,128)(2,1)S(1)}, bf16[4,384,8]{1,2,0:T(8,128)(2,1)}, u32[]{:S(2)}) copy-start(bf16[4,384,8]{1,2,0:T(8,128)(2,1)} %param.10) | copy-start | bytes 73732

commit v12 on v11

--- a/solution.py
+++ b/solution.py
@@ -172,16 +172,24 @@
     )(targets, rhs_low, inv_low, blocks)
 
 
-def summed_up(shares):
-    def body(shares_ref, out_ref):
+def summed_up(shares, give):
+    def body(shares_ref, give_ref, out_ref, same_ref):
+        del give_ref, same_ref
         out_ref[...] = jnp.sum(shares_ref[...].astype(F32), axis=0).astype(BF16)
 
-    return pl.pallas_call(
-        body,
-        out_shape=jax.ShapeDtypeStruct(shares.shape[1:], BF16),
+    any_spec, vmem = pl.BlockSpec(memory_space=pl.ANY), pl.BlockSpec(memory_space=pltpu.VMEM)
+    return pl.pallas_call(
+        body,
+        out_shape=(
+            jax.ShapeDtypeStruct(shares.shape[1:], BF16),
+            jax.ShapeDtypeStruct(give.shape, BF16),
+        ),
+        in_specs=[vmem, any_spec],
+        out_specs=(vmem, any_spec),
+        input_output_aliases={1: 1},
         compiler_params=pltpu.CompilerParams(vmem_limit_bytes=SMALL),
         cost_estimate=pl.CostEstimate(flops=200_000, bytes_accessed=450_000, transcendentals=0),
-    )(shares)
+    )(shares, give)
 
 
 def second_level(part, ready, copies):
@@ -298,15 +306,14 @@
     def swap(value):
         return lax.ppermute(value, ("layer", "row"), pairs)
 
-    near = swap(give)
-
-    summed = summed_up(shares)
+    summed, give = summed_up(shares, give)
     turn = [
         (row * cols + col, col * cols + (row - 1) % rows)
         for row in range(rows)
         for col in range(cols)
     ]
     summed = lax.ppermute(summed, ("row", "col"), turn)
+    near = swap(give)
     pieces, both = second_level(summed, ready, rows // 2)
     lines = [list(range(core, rows, 2)) for core in range(2)]
     chips = [[row, row + 1] for row in range(0, rows, 2)]

time: 102 us -> 102 us (level)
  local copies, waits for them, and re-layouts: 2.77 us -> 0.06 us
  Pallas kernels: 8.73 us -> 10.5 us
  waiting for transfers between devices: 8.96 us -> 10.4 us
  starting transfers between devices: 21.3 us -> 20.1 us
  blocking collectives: 58.9 us -> 60 us
    all_to_all x1, blocking collectives: 18 us -> 20.9 us  [on_device(): shares = lax.all_to_all(part, 'col', 0, 0, tiled=True)]
    unnamed x10 -> x8, local copies, waits for them, and re-layouts: 2.73 us -> 0.02 us
    pallas_call x2, Pallas kernels: 2.4 us -> 4.12 us  [ancestor_parts(): pl.pallas_call(body, out_shape=jax.ShapeDtypeStruct((loads, count * width...]
    all_to_all x1, starting transfers between devices: 6.98 us -> 8.36 us  [on_device(): lax.all_to_all(pieces, 'row', 0, 0, axis_index_groups=lines, tiled=True)]
    ppermute x1, starting transfers between devices: 6.71 us -> 5.4 us  [on_device(): summed = lax.ppermute(summed, ('row', 'col'), turn)]
    ppermute x2, waiting for transfers between devices: 0.9 us -> 2.18 us  [swap(): return lax.ppermute(value, ('layer', 'row'), pairs)]
    ppermute x2, starting transfers between devices: 7.6 us -> 6.33 us  [swap(): return lax.ppermute(value, ('layer', 'row'), pairs)]
  transfers between devices with their start and end apart: 4 -> 4, of which waited for: 3 -> 4; matrix products, arithmetic and copies ran while one was open for 0% -> 0% of each run, Pallas kernels for 3% -> 4%
where the time goes in v12:
time: 102 us
  blocking collectives  60 us (59%)
  starting transfers between devices  20.1 us (20%)
  Pallas kernels  10.5 us (10%)
  waiting for transfers between devices  10.4 us (10%)
    all_to_all x1, blocking collectives, on_device(): lax.all_to_all(parts.reshape(members, parts.shape[0] // members, -1), ('l...  35.9 us
    all_to_all x1, blocking collectives, on_device(): shares = lax.all_to_all(part, 'col', 0, 0, tiled=True)  20.9 us
    all_to_all x1, starting transfers between devices, on_device(): lax.all_to_all(pieces, 'row', 0, 0, axis_index_groups=lines, tiled=True)  8.36 us
    ppermute x2, starting transfers between devices, swap(): return lax.ppermute(value, ('layer', 'row'), pairs)  6.33 us
    all_to_all x1, waiting for transfers between devices, on_device(): lax.all_to_all(pieces, 'row', 0, 0, axis_index_groups=lines, tiled=True)  6.33 us
    ppermute x1, starting transfers between devices, on_device(): summed = lax.ppermute(summed, ('row', 'col'), turn)  5.4 us
    pallas_call x1, Pallas kernels, first_level(): pl.pallas_call(body, out_shape=(jax.ShapeDtypeStruct((rows, share, width)...  4.24 us
    pallas_call x2, Pallas kernels, ancestor_parts(): pl.pallas_call(body, out_shape=jax.ShapeDtypeStruct((loads, count * width...  4.12 us
  transfers between devices with their start and end apart: 4, of which 4 were waited for; matrix products, arithmetic and copies ran while one was open for 0% of the time, Pallas kernels for 4%

profile of v12, /device:TPU:8, one launch (start us, length us, event | category | flops | bytes accessed | tf_op | source)
XLA Modules:
  0.0 101.7 jit_solution(6607642829195008712)
XLA Ops:
  0.6 4.2 %shard_map.77 = (bf16[8,64,384]{2,1,0:T(8,128)(2,1)}, bf16[256,384]{1,0:T(8,128)(2,1)}, bf16[512,384]{1,0:T(8,128)(2,1)}, bf16[3328,384]{1,0:T(8,128)(2,1)}) custom-call(s32[2,4]{1,0:T(2,128)} %bitcast.24, bf16[2,384,512]{2,1,0:T(8,128)(2,1)} %bitcast.20, bf16[2,384,384]{2,1,0:T(8,128)(2,1)} %bitcast.21, bf16[2,4,384,384]{3,2,1,0:T(8,128)(2,1)} %bitcast.18), custom_call_target="tpu_custom_call" | custom-call | flops 301989888 | bytes 2200000 | tf_op jit(solution)/shard_map/pallas_call | solution.py:146
  4.9 0.0 copy-start.1
  4.9 20.9 %all_to_all.15.shares_ref = bf16[8,64,384]{2,1,0:T(8,128)(2,1)S(1)} all-to-all(bf16[8,64,384]{2,1,0:T(8,128)(2,1)} %get-tuple-element.10), channel_id=1, replica_groups=mesh['layer'=8,'row'=8,'col'=8] {'col'}, dimensions={0} | all-to-all | bytes 786432 | tf_op jit(solution)/shard_map/all_to_all | solution.py:294
  25.8 0.0 copy-start.2
  25.8 0.1 shard_map.78
  25.9 4.4 %collective-permute-start.1 = (bf16[3328,384]{1,0:T(8,128)(2,1)}, bf16[3328,384]{1,0:T(8,128)(2,1)S(1)}, u32[]{:S(2)}, u32[]{:S(2)}) collective-permute-start(bf16[3328,384]{1,0:T(8,128)(2,1)} %get-tuple-element.15.refs_0_), channel_id=1, source_target_pairs={{0,64},{8,456},{16,80},{24,472},{32,96},{40,488},{48,112},{56,504}... | collective-permute-start | bytes 7667720 | tf_op jit(solution)/shard_map/ppermute | solution.py:307
  30.3 5.4 %collective-permute-start = (bf16[64,384]{1,0:T(8,128)(2,1)S(1)}, bf16[64,384]{1,0:T(8,128)(2,1)S(1)}, u32[]{:S(2)}, u32[]{:S(2)}) collective-permute-start(bf16[64,384]{1,0:T(8,128)(2,1)S(1)} %get-tuple-element.12), channel_id=1, source_target_pairs={{0,7},{1,15},{2,23},{3,31},{4,39},{5,47},{6,55},{7,63},{8,0},{9,8}... | collective-permute-start | bytes 147464 | tf_op jit(solution)/shard_map/ppermute | solution.py:315
  35.7 1.9 %collective-permute-done.part_ref = bf16[64,384]{1,0:T(8,128)(2,1)S(1)} collective-permute-done((bf16[64,384]{1,0:T(8,128)(2,1)S(1)}, bf16[64,384]{1,0:T(8,128)(2,1)S(1)}, u32[]{:S(2)}, u32[]{:S(2)}) %collective-permute-start) | collective-permute-done | bytes 49184 | tf_op jit(solution)/shard_map/ppermute | solution.py:315
  37.6 0.0 copy-done.1
  37.6 0.9 shard_map.79
  38.5 8.4 %all-to-all-start.1 = ((bf16[4,64,384]{2,1,0:T(8,128)(2,1)}), bf16[4,64,384]{2,1,0:T(8,128)(2,1)S(1)}, u32[]{:S(2)}, u32[]{:S(2)}) async-start(bf16[4,64,384]{2,1,0:T(8,128)(2,1)} %get-tuple-element.16), calls=%async_computation.1 | async-start | bytes 393216 | tf_op jit(solution)/shard_map/all_to_all | solution.py:320
  46.9 6.3 %all-to-all-done.1 = bf16[4,64,384]{2,1,0:T(8,128)(2,1)S(1)} async-done(((bf16[4,64,384]{2,1,0:T(8,128)(2,1)}), bf16[4,64,384]{2,1,0:T(8,128)(2,1)S(1)}, u32[]{:S(2)}, u32[]{:S(2)}) %all-to-all-start.1) | async-done | bytes 196640 | tf_op jit(solution)/shard_map/all_to_all | solution.py:320
  53.2 3.2 %all-gather = bf16[8,64,384]{2,1,0:T(8,128)(2,1)S(1)} all-gather(bf16[4,64,384]{2,1,0:T(8,128)(2,1)S(1)} %all-to-all-done.1), channel_id=2, replica_groups={{0,8},{16,24},{32,40},{48,56},{1,9},{17,25},{33,41},{49,57},{2,10},{18,..., dimensions={0}, use_global_device_ids=true | all-gather | bytes 589824 | tf_op jit(solution)/shard_map/all_gather | solution.py:321
  56.5 1.9 %collective-permute-start.2 = (bf16[256,384]{1,0:T(8,128)(2,1)S(1)}, bf16[256,384]{1,0:T(8,128)(2,1)S(1)}, u32[]{:S(2)}, u32[]{:S(2)}) collective-permute-start(bf16[256,384]{1,0:T(8,128)(2,1)S(1)} %bitcast.22), channel_id=1, source_target_pairs={{0,64},{8,456},{16,80},{24,472},{32,96},{40,488},{48,112},{56,504}... | collective-permute-start | bytes 589832 | tf_op jit(solution)/shard_map/ppermute | solution.py:307
  58.4 1.0 %collective-permute-done.1.refs_3_.refs_4_.refs_0_ = bf16[3328,384]{1,0:T(8,128)(2,1)S(1)} collective-permute-done((bf16[3328,384]{1,0:T(8,128)(2,1)}, bf16[3328,384]{1,0:T(8,128)(2,1)S(1)}, u32[]{:S(2)}, u32[]{:S(2)}) %collective-permute-start.1) | collective-permute-done | bytes 2555936 | tf_op jit(solution)/shard_map/ppermute | solution.py:307
  59.4 0.0 copy-done.2
  59.4 3.4 %shard_map.80.refs_2_ = bf16[256,1536]{1,0:T(8,128)(2,1)S(1)} custom-call(bf16[3328,384]{1,0:T(8,128)(2,1)} %get-tuple-element.15.refs_0_, bf16[256,384]{1,0:T(8,128)(2,1)S(1)} %copy-done.2, bf16[256,384]{1,0:T(8,128)(2,1)S(1)} %bitcast.16, bf16[3328,384]{1,0:T(8,128)(2,1)S(1)} %collective-permute-done.1.refs_3_.refs_4_.refs_0_, ...), custom_call_target="tpu_custom_call" | custom-call | flops 905969664 | bytes 5000000 | tf_op jit(solution)/shard_map/pallas_call | solution.py:247
  62.8 0.0 copy-start
  62.9 0.0 copy-start.3
  62.9 1.2 %collective-permute-done.2.refs_1_ = bf16[256,384]{1,0:T(8,128)(2,1)S(1)} collective-permute-done((bf16[256,384]{1,0:T(8,128)(2,1)S(1)}, bf16[256,384]{1,0:T(8,128)(2,1)S(1)}, u32[]{:S(2)}, u32[]{:S(2)}) %collective-permute-start.2) | collective-permute-done | bytes 196640 | tf_op jit(solution)/shard_map/ppermute | solution.py:307
  64.0 0.7 shard_map.81
  64.7 35.9 %all_to_all.16.arrived_ref = bf16[32,8,1536]{2,1,0:T(8,128)(2,1)S(1)} all-to-all(bf16[32,8,1536]{2,1,0:T(8,128)(2,1)S(1)} %bitcast.15), channel_id=1, replica_groups={{0,1,2,3,4,5,6,7,128,129,130,131,132,133,134,135,256,257,258,259,260,26..., dimensions={0} | all-to-all | bytes 1572864 | tf_op jit(solution)/shard_map/all_to_all | solution.py:342
  100.6 0.0 copy-done
  100.6 0.0 copy-done.3
  100.6 1.1 %shard_map.82 = f32[4,8,384]{2,1,0:T(8,128)} custom-call(bf16[32,8,1536]{2,1,0:T(8,128)(2,1)S(1)} %all_to_all.16.arrived_ref, bf16[4,8,384]{2,1,0:T(8,128)(2,1)S(1)} %bitcast.17, bf16[4,384,384]{2,1,0:T(8,128)(2,1)S(1)} %copy-done), custom_call_target="tpu_custom_call" | custom-call | flops 9437184 | bytes 3000000 | tf_op jit(solution)/shard_map/pallas_call | solution.py:273
  (1 shorter events, 0.0 us)
Async XLA Ops:
  4.9 32.7 %copy-start.1 = (bf16[512,384]{1,0:T(8,128)(2,1)S(1)}, bf16[512,384]{1,0:T(8,128)(2,1)}, u32[]{:S(2)}) copy-start(bf16[512,384]{1,0:T(8,128)(2,1)} %get-tuple-element.13.ready_ref) | copy-start | bytes 1179652
  25.8 33.6 %copy-start.2 = (bf16[256,384]{1,0:T(8,128)(2,1)S(1)}, bf16[256,384]{1,0:T(8,128)(2,1)}, u32[]{:S(2)}) copy-start(bf16[256,384]{1,0:T(8,128)(2,1)} %get-tuple-element.17.refs_1_) | copy-start | bytes 589828
  25.9 33.5 %collective-permute-start.1 = (bf16[3328,384]{1,0:T(8,128)(2,1)}, bf16[3328,384]{1,0:T(8,128)(2,1)S(1)}, u32[]{:S(2)}, u32[]{:S(2)}) collective-permute-start(bf16[3328,384]{1,0:T(8,128)(2,1)} %get-tuple-element.15.refs_0_), channel_id=1, source_target_pairs={{0,64},{8,456},{16,80},{24,472},{32,96},{40,488},{48,112},{56,504}... | collective-permute-start | bytes 7667720 | tf_op jit(solution)/shard_map/ppermute | solution.py:307
  30.3 7.3 %collective-permute-start = (bf16[64,384]{1,0:T(8,128)(2,1)S(1)}, bf16[64,384]{1,0:T(8,128)(2,1)S(1)}, u32[]{:S(2)}, u32[]{:S(2)}) collective-permute-start(bf16[64,384]{1,0:T(8,128)(2,1)S(1)} %get-tuple-element.12), channel_id=1, source_target_pairs={{0,7},{1,15},{2,23},{3,31},{4,39},{5,47},{6,55},{7,63},{8,0},{9,8}... | collective-permute-start | bytes 147464 | tf_op jit(solution)/shard_map/ppermute | solution.py:315
  38.5 14.7 %all-to-all-start.1 = ((bf16[4,64,384]{2,1,0:T(8,128)(2,1)}), bf16[4,64,384]{2,1,0:T(8,128)(2,1)S(1)}, u32[]{:S(2)}, u32[]{:S(2)}) async-start(bf16[4,64,384]{2,1,0:T(8,128)(2,1)} %get-tuple-element.16), calls=%async_computation.1 | async-start | bytes 393216 | tf_op jit(solution)/shard_map/all_to_all | solution.py:320
  56.5 7.6 %collective-permute-start.2 = (bf16[256,384]{1,0:T(8,128)(2,1)S(1)}, bf16[256,384]{1,0:T(8,128)(2,1)S(1)}, u32[]{:S(2)}, u32[]{:S(2)}) collective-permute-start(bf16[256,384]{1,0:T(8,128)(2,1)S(1)} %bitcast.22), channel_id=1, source_target_pairs={{0,64},{8,456},{16,80},{24,472},{32,96},{40,488},{48,112},{56,504}... | collective-permute-start | bytes 589832 | tf_op jit(solution)/shard_map/ppermute | solution.py:307
  62.8 37.8 %copy-start = (bf16[4,384,384]{2,1,0:T(8,128)(2,1)S(1)}, bf16[4,384,384]{2,1,0:T(8,128)(2,1)}, u32[]{:S(2)}) copy-start(bf16[4,384,384]{2,1,0:T(8,128)(2,1)} %inv_ref.1) | copy-start | bytes 3538948
  62.9 37.8 %copy-start.3 = (bf16[4,384,8]{1,2,0:T(8,128)(2,1)S(1)}, bf16[4,384,8]{1,2,0:T(8,128)(2,1)}, u32[]{:S(2)}) copy-start(bf16[4,384,8]{1,2,0:T(8,128)(2,1)} %param.10) | copy-start | bytes 73732

commit v13 on v12

--- a/solution.py
+++ b/solution.py
@@ -327,13 +327,10 @@
         return half.reshape(wanted, width)
 
     near_answer1 = swap(half_of(1 - kept))
-    early = [
-        (0, give, kept0, 0),
-        (1, give, half_of(kept), 0),
-        (0, near, near, near.shape[0] // wanted - 1),
-    ]
-    parts = ancestor_parts(early, count, wanted)
-    parts = ancestor_parts([(1, near, near_answer1, 0)], count, wanted, parts)
+    own = [(0, give, kept0, 0), (1, give, half_of(kept), 0)]
+    parts = ancestor_parts(own, count, wanted)
+    late = [(0, near, near, near.shape[0] // wanted - 1), (1, near, near_answer1, 0)]
+    parts = ancestor_parts(late, count, wanted, parts)
     groups = [
         [layer * cols + col for layer in range(parity, layers, 2) for col in range(cols)]
         for parity in range(2)

time: 102 us -> 103 us (level)
  transfers between devices with their start and end apart: 4 -> 4, of which waited for: 4 -> 3; matrix products, arithmetic and copies ran while one was open for 0% -> 0% of each run, Pallas kernels for 4% -> 4%
where the time goes in v13:
time: 103 us; the launch traced here: 102 us
  blocking collectives  59.9 us (58%)
  starting transfers between devices  20.1 us (20%)
  waiting for transfers between devices  10.9 us (11%)
  Pallas kernels  10.4 us (10%)
    all_to_all x1, blocking collectives, on_device(): lax.all_to_all(parts.reshape(members, parts.shape[0] // members, -1), ('l...  35.9 us
    all_to_all x1, blocking collectives, on_device(): shares = lax.all_to_all(part, 'col', 0, 0, tiled=True)  20.9 us
    all_to_all x1, starting transfers between devices, on_device(): lax.all_to_all(pieces, 'row', 0, 0, axis_index_groups=lines, tiled=True)  8.36 us
    ppermute x2, starting transfers between devices, swap(): return lax.ppermute(value, ('layer', 'row'), pairs)  6.33 us
    all_to_all x1, waiting for transfers between devices, on_device(): lax.all_to_all(pieces, 'row', 0, 0, axis_index_groups=lines, tiled=True)  6.33 us
    ppermute x1, starting transfers between devices, on_device(): summed = lax.ppermute(summed, ('row', 'col'), turn)  5.4 us
    pallas_call x1, Pallas kernels, first_level(): pl.pallas_call(body, out_shape=(jax.ShapeDtypeStruct((rows, share, width)...  4.24 us
    pallas_call x2, Pallas kernels, ancestor_parts(): pl.pallas_call(body, out_shape=jax.ShapeDtypeStruct((loads, count * width...  4.08 us
  transfers between devices with their start and end apart: 4, of which 3 were waited for; matrix products, arithmetic and copies ran while one was open for 0% of the time, Pallas kernels for 4%

profile of v13, /device:TPU:8, one launch (start us, length us, event | category | flops | bytes accessed | tf_op | source)
XLA Modules:
  0.0 102.2 jit_solution(10208593797764678058)
XLA Ops:
  0.6 4.2 %shard_map.77 = (bf16[8,64,384]{2,1,0:T(8,128)(2,1)}, bf16[256,384]{1,0:T(8,128)(2,1)}, bf16[512,384]{1,0:T(8,128)(2,1)}, bf16[3328,384]{1,0:T(8,128)(2,1)}) custom-call(s32[2,4]{1,0:T(2,128)} %bitcast.24, bf16[2,384,512]{2,1,0:T(8,128)(2,1)} %bitcast.20, bf16[2,384,384]{2,1,0:T(8,128)(2,1)} %bitcast.21, bf16[2,4,384,384]{3,2,1,0:T(8,128)(2,1)} %bitcast.18), custom_call_target="tpu_custom_call" | custom-call | flops 301989888 | bytes 2200000 | tf_op jit(solution)/shard_map/pallas_call | solution.py:146
  4.9 0.0 copy-start.1
  4.9 20.9 %all_to_all.15.shares_ref = bf16[8,64,384]{2,1,0:T(8,128)(2,1)S(1)} all-to-all(bf16[8,64,384]{2,1,0:T(8,128)(2,1)} %get-tuple-element.10), channel_id=1, replica_groups=mesh['layer'=8,'row'=8,'col'=8] {'col'}, dimensions={0} | all-to-all | bytes 786432 | tf_op jit(solution)/shard_map/all_to_all | solution.py:294
  25.8 0.0 copy-start.2
  25.8 0.1 shard_map.78
  25.9 4.4 %collective-permute-start.1 = (bf16[3328,384]{1,0:T(8,128)(2,1)}, bf16[3328,384]{1,0:T(8,128)(2,1)S(1)}, u32[]{:S(2)}, u32[]{:S(2)}) collective-permute-start(bf16[3328,384]{1,0:T(8,128)(2,1)} %get-tuple-element.15.refs_0_), channel_id=1, source_target_pairs={{0,64},{8,456},{16,80},{24,472},{32,96},{40,488},{48,112},{56,504}... | collective-permute-start | bytes 7667720 | tf_op jit(solution)/shard_map/ppermute | solution.py:307
  30.3 5.4 %collective-permute-start = (bf16[64,384]{1,0:T(8,128)(2,1)S(1)}, bf16[64,384]{1,0:T(8,128)(2,1)S(1)}, u32[]{:S(2)}, u32[]{:S(2)}) collective-permute-start(bf16[64,384]{1,0:T(8,128)(2,1)S(1)} %get-tuple-element.12), channel_id=1, source_target_pairs={{0,7},{1,15},{2,23},{3,31},{4,39},{5,47},{6,55},{7,63},{8,0},{9,8}... | collective-permute-start | bytes 147464 | tf_op jit(solution)/shard_map/ppermute | solution.py:315
  35.7 1.9 %collective-permute-done.part_ref = bf16[64,384]{1,0:T(8,128)(2,1)S(1)} collective-permute-done((bf16[64,384]{1,0:T(8,128)(2,1)S(1)}, bf16[64,384]{1,0:T(8,128)(2,1)S(1)}, u32[]{:S(2)}, u32[]{:S(2)}) %collective-permute-start) | collective-permute-done | bytes 49184 | tf_op jit(solution)/shard_map/ppermute | solution.py:315
  37.6 0.0 copy-done.1
  37.6 0.9 shard_map.79
  38.5 8.4 %all-to-all-start.1 = ((bf16[4,64,384]{2,1,0:T(8,128)(2,1)}), bf16[4,64,384]{2,1,0:T(8,128)(2,1)S(1)}, u32[]{:S(2)}, u32[]{:S(2)}) async-start(bf16[4,64,384]{2,1,0:T(8,128)(2,1)} %get-tuple-element.16), calls=%async_computation.1 | async-start | bytes 393216 | tf_op jit(solution)/shard_map/all_to_all | solution.py:320
  46.9 6.3 %all-to-all-done.1 = bf16[4,64,384]{2,1,0:T(8,128)(2,1)S(1)} async-done(((bf16[4,64,384]{2,1,0:T(8,128)(2,1)}), bf16[4,64,384]{2,1,0:T(8,128)(2,1)S(1)}, u32[]{:S(2)}, u32[]{:S(2)}) %all-to-all-start.1) | async-done | bytes 196640 | tf_op jit(solution)/shard_map/all_to_all | solution.py:320
  53.2 3.2 %all-gather = bf16[8,64,384]{2,1,0:T(8,128)(2,1)S(1)} all-gather(bf16[4,64,384]{2,1,0:T(8,128)(2,1)S(1)} %all-to-all-done.1), channel_id=2, replica_groups={{0,8},{16,24},{32,40},{48,56},{1,9},{17,25},{33,41},{49,57},{2,10},{18,..., dimensions={0}, use_global_device_ids=true | all-gather | bytes 589824 | tf_op jit(solution)/shard_map/all_gather | solution.py:321
  56.5 1.9 %collective-permute-start.2 = (bf16[256,384]{1,0:T(8,128)(2,1)S(1)}, bf16[256,384]{1,0:T(8,128)(2,1)S(1)}, u32[]{:S(2)}, u32[]{:S(2)}) collective-permute-start(bf16[256,384]{1,0:T(8,128)(2,1)S(1)} %bitcast.22), channel_id=1, source_target_pairs={{0,64},{8,456},{16,80},{24,472},{32,96},{40,488},{48,112},{56,504}... | collective-permute-start | bytes 589832 | tf_op jit(solution)/shard_map/ppermute | solution.py:307
  58.4 0.0 copy-done.2
  58.4 2.9 %shard_map.80.refs_3_ = bf16[256,1536]{1,0:T(8,128)(2,1)S(1)} custom-call(bf16[3328,384]{1,0:T(8,128)(2,1)} %get-tuple-element.15.refs_0_, bf16[256,384]{1,0:T(8,128)(2,1)S(1)} %copy-done.2, bf16[256,384]{1,0:T(8,128)(2,1)S(1)} %bitcast.16), custom_call_target="tpu_custom_call" | custom-call | flops 603979776 | bytes 5000000 | tf_op jit(solution)/shard_map/pallas_call | solution.py:247
  61.3 0.0 copy-start
  61.3 0.0 copy-start.3
  61.3 2.7 %collective-permute-done.2.refs_2_ = bf16[256,384]{1,0:T(8,128)(2,1)S(1)} collective-permute-done((bf16[256,384]{1,0:T(8,128)(2,1)S(1)}, bf16[256,384]{1,0:T(8,128)(2,1)S(1)}, u32[]{:S(2)}, u32[]{:S(2)}) %collective-permute-start.2) | collective-permute-done | bytes 196640 | tf_op jit(solution)/shard_map/ppermute | solution.py:307
  64.0 0.0 collective-permute-done.1.refs_0_.refs_1_
  64.0 1.2 %shard_map.81 = bf16[256,1536]{1,0:T(8,128)(2,1)S(1)} custom-call(bf16[3328,384]{1,0:T(8,128)(2,1)S(1)} %collective-permute-done.1.refs_0_.refs_1_, bf16[3328,384]{1,0:T(8,128)(2,1)S(1)} %collective-permute-done.1.refs_0_.refs_1_, bf16[256,384]{1,0:T(8,128)(2,1)S(1)} %collective-permute-done.2.refs_2_, bf16[256,1536]{1,0:T(8,128)(2,1)S(1)} %shard_map.80.refs_3_), custom_call_target="tpu_custom_call" | custom-call | flops 603979776 | bytes 5000000 | tf_op jit(solution)/shard_map/pallas_call | solution.py:247
  65.2 35.9 %all_to_all.16.arrived_ref = bf16[32,8,1536]{2,1,0:T(8,128)(2,1)S(1)} all-to-all(bf16[32,8,1536]{2,1,0:T(8,128)(2,1)S(1)} %bitcast.15), channel_id=1, replica_groups={{0,1,2,3,4,5,6,7,128,129,130,131,132,133,134,135,256,257,258,259,260,26..., dimensions={0} | all-to-all | bytes 1572864 | tf_op jit(solution)/shard_map/all_to_all | solution.py:339
  101.1 0.0 copy-done
  101.1 0.0 copy-done.3
  101.1 1.1 %shard_map.82 = f32[4,8,384]{2,1,0:T(8,128)} custom-call(bf16[32,8,1536]{2,1,0:T(8,128)(2,1)S(1)} %all_to_all.16.arrived_ref, bf16[4,8,384]{2,1,0:T(8,128)(2,1)S(1)} %bitcast.17, bf16[4,384,384]{2,1,0:T(8,128)(2,1)S(1)} %copy-done), custom_call_target="tpu_custom_call" | custom-call | flops 9437184 | bytes 3000000 | tf_op jit(solution)/shard_map/pallas_call | solution.py:273
  (1 shorter events, 0.0 us)
Async XLA Ops:
  4.9 32.7 %copy-start.1 = (bf16[512,384]{1,0:T(8,128)(2,1)S(1)}, bf16[512,384]{1,0:T(8,128)(2,1)}, u32[]{:S(2)}) copy-start(bf16[512,384]{1,0:T(8,128)(2,1)} %get-tuple-element.13.ready_ref) | copy-start | bytes 1179652
  25.8 32.6 %copy-start.2 = (bf16[256,384]{1,0:T(8,128)(2,1)S(1)}, bf16[256,384]{1,0:T(8,128)(2,1)}, u32[]{:S(2)}) copy-start(bf16[256,384]{1,0:T(8,128)(2,1)} %get-tuple-element.17.refs_1_) | copy-start | bytes 589828
  25.9 38.2 %collective-permute-start.1 = (bf16[3328,384]{1,0:T(8,128)(2,1)}, bf16[3328,384]{1,0:T(8,128)(2,1)S(1)}, u32[]{:S(2)}, u32[]{:S(2)}) collective-permute-start(bf16[3328,384]{1,0:T(8,128)(2,1)} %get-tuple-element.15.refs_0_), channel_id=1, source_target_pairs={{0,64},{8,456},{16,80},{24,472},{32,96},{40,488},{48,112},{56,504}... | collective-permute-start | bytes 7667720 | tf_op jit(solution)/shard_map/ppermute | solution.py:307
  30.3 7.3 %collective-permute-start = (bf16[64,384]{1,0:T(8,128)(2,1)S(1)}, bf16[64,384]{1,0:T(8,128)(2,1)S(1)}, u32[]{:S(2)}, u32[]{:S(2)}) collective-permute-start(bf16[64,384]{1,0:T(8,128)(2,1)S(1)} %get-tuple-element.12), channel_id=1, source_target_pairs={{0,7},{1,15},{2,23},{3,31},{4,39},{5,47},{6,55},{7,63},{8,0},{9,8}... | collective-permute-start | bytes 147464 | tf_op jit(solution)/shard_map/ppermute | solution.py:315
  38.5 14.7 %all-to-all-start.1 = ((bf16[4,64,384]{2,1,0:T(8,128)(2,1)}), bf16[4,64,384]{2,1,0:T(8,128)(2,1)S(1)}, u32[]{:S(2)}, u32[]{:S(2)}) async-start(bf16[4,64,384]{2,1,0:T(8,128)(2,1)} %get-tuple-element.16), calls=%async_computation.1 | async-start | bytes 393216 | tf_op jit(solution)/shard_map/all_to_all | solution.py:320
  56.5 7.6 %collective-permute-start.2 = (bf16[256,384]{1,0:T(8,128)(2,1)S(1)}, bf16[256,384]{1,0:T(8,128)(2,1)S(1)}, u32[]{:S(2)}, u32[]{:S(2)}) collective-permute-start(bf16[256,384]{1,0:T(8,128)(2,1)S(1)} %bitcast.22), channel_id=1, source_target_pairs={{0,64},{8,456},{16,80},{24,472},{32,96},{40,488},{48,112},{56,504}... | collective-permute-start | bytes 589832 | tf_op jit(solution)/shard_map/ppermute | solution.py:307
  61.3 39.8 %copy-start = (bf16[4,384,384]{2,1,0:T(8,128)(2,1)S(1)}, bf16[4,384,384]{2,1,0:T(8,128)(2,1)}, u32[]{:S(2)}) copy-start(bf16[4,384,384]{2,1,0:T(8,128)(2,1)} %inv_ref.1) | copy-start | bytes 3538948
  61.3 39.8 %copy-start.3 = (bf16[4,384,8]{1,2,0:T(8,128)(2,1)S(1)}, bf16[4,384,8]{1,2,0:T(8,128)(2,1)}, u32[]{:S(2)}) copy-start(bf16[4,384,8]{1,2,0:T(8,128)(2,1)} %param.10) | copy-start | bytes 73732
